TPU v7x, 32 devices: a whole 2x2x4 slice. The times are simulated.
32 devices in a mesh: groups: 2 (over y), mem: 4 (over z), comp: 4 (over x, core).
Axes of the slice: x: 2, y: 2, z: 4, core: 2. Of those that a mesh axis runs over, the one named last changes fastest.
Arguments:
- hidden_in: bfloat16 [64, 8192], P('groups', 'mem'), parts along dimension 0, may hold values from -4 to 4
- lengths: int32 [64], P('groups'), parts along dimension 0, may hold values from 1 to 25344, as said below
- block_table: int32 [64, 128], P('groups'), parts along dimension 0, may hold values from 0 to 159, as said below
- cache_keys: bfloat16 [320, 256, 1024], P(('groups', 'mem'), None, 'comp'), parts along dimension 0, may hold values from -300 to 300
- cache_values: bfloat16 [320, 256, 1024], P(('groups', 'mem'), None, 'comp'), parts along dimension 0, may hold values from -6 to 6
- attn_gain: bfloat16 [8192], P('mem'), may hold values from 0.099609375 to 1.8984375
- w_query: bfloat16 [8192, 8192], P('mem', 'comp'), may hold values from -0.0625 to 0.0625
- w_kv: bfloat16 [8192, 2, 1024], P('mem', None, 'comp'), may hold values from -0.0625 to 0.0625
- w_out: bfloat16 [8192, 8192], P('comp', 'mem'), may hold values from -0.0625 to 0.0625
- ffn_gain: bfloat16 [8192], P('mem'), may hold values from 0.099609375 to 1.8984375
- w_gate_up: bfloat16 [8192, 2, 14336], P('mem', None, 'comp'), may hold values from -0.0625 to 0.0625
- w_down: bfloat16 [14336, 8192], P('comp', 'mem'), may hold values from -0.046875 to 0.046875
Outputs:
- attended: bfloat16 [64, 8192], P('groups', 'comp'), parts along dimension 0
- updated: bfloat16 [64, 8192], P('groups', 'mem'), parts along dimension 0
There are 2 independent parts, one for each index of `groups`. A program takes and returns all parts, laid end to end along the dimension named above; an argument that names none is the same for every part. Nothing has to cross between parts.
Inputs may be any that keep to these rules, and one draw needn't show every extreme that they name: `lengths`: one request has the largest length, the others are ragged and shorter. For each block b of request r that holds a position below lengths[r], block_table[r, b] is its slot; slot s belongs to memory device s // 40. Other entries are 0 or 159 and unused. No two used entries share a slot, the used slots of one memory device are its lowest ones, and in every draw some memory device has all 40 of its slots used. Slots that no entry uses hold arbitrary finite values.
All inputs are finite; a program needn't handle non-finite values.
Results may differ from a plain program's by a relative error of at most 0.01.
The roundings to bfloat16 on the way count: a program that leaves them out, or rounds other values in their place, can miss the bound.
Values may be sent and summed in bfloat16 or wider, within the bound.
No kernel may reach another device: no remote copies, remote signals or barrier semaphores. Data moves between devices by JAX's collectives and lax.ppermute only.
A program may use at most 192 MiB of HBM per device.

v0:
```python
import math

import jax
import jax.numpy as jnp
from jax import lax
from jax.sharding import PartitionSpec as P

D = 8192
HD = 128


NORM_EPS = 1e-05
ROPE_BASE = 500000.0
NEG_FILL = -1e30


def combined_all(value, axis, join):
    pieces = jax.tree.map(lambda part: lax.all_gather(part, axis), value)
    head = jax.tree.map(lambda part: part[0], pieces)
    tail = jax.tree.map(lambda part: part[1:], pieces)
    subtotal, _ = lax.scan(lambda subtotal, section: (join(subtotal, section), None), head, tail)
    return subtotal


def rotate(values, positions):
    half_dim = values.shape[-1] // 2
    freq_steps = jnp.arange(half_dim, dtype=jnp.float32) * (2.0 / values.shape[-1])
    inv_freq = jnp.exp(-freq_steps * math.log(ROPE_BASE))
    angles = positions.astype(jnp.float32)[:, None, None] * inv_freq
    cosine = jnp.cos(angles)
    sine = jnp.sin(angles)
    first_half = values[..., :half_dim]
    second_half = values[..., half_dim:]
    return jnp.concatenate(
        [first_half * cosine - second_half * sine, second_half * cosine + first_half * sine], -1
    )


def slot_stats(queries_slot, key_rows, value_rows, slot_fill, scale_val):
    scores = (
        jnp.einsum("skgd,sbkd->skgb", queries_slot, key_rows, preferred_element_type=jnp.float32)
        * scale_val
    )
    is_valid = (jnp.arange(key_rows.shape[1], dtype=jnp.int32)[None, :] < slot_fill[:, None])[
        :, None, None, :
    ]
    scores = jnp.where(is_valid, scores, NEG_FILL)
    peak_val = jnp.max(scores, -1)
    weights = jnp.where(is_valid, jnp.exp(scores - peak_val[..., None]), 0.0)
    total_w = jnp.sum(weights, -1)
    weighted = jnp.einsum(
        "skgb,sbkd->skgd",
        weights.astype(jnp.bfloat16),
        value_rows,
        preferred_element_type=jnp.float32,
    )
    return (peak_val, total_w, weighted)


def combine(left_part, right_part):
    peak_val = jnp.maximum(left_part[0], right_part[0])
    left_w = jnp.exp(left_part[0] - peak_val)
    right_w = jnp.exp(right_part[0] - peak_val)
    return (
        peak_val,
        left_part[1] * left_w + right_part[1] * right_w,
        left_part[2] * left_w[..., None] + right_part[2] * right_w[..., None],
    )


def finish(peak_val, total_w, weighted, queries, new_keys, new_values, scale_val):
    own_score = (
        jnp.einsum("rkgd,rkd->rkg", queries, new_keys, preferred_element_type=jnp.float32)
        * scale_val
    )
    top_all = jnp.maximum(peak_val, own_score)
    old_part = jnp.exp(peak_val - top_all)
    new_part = jnp.exp(own_score - top_all)
    numer = (
        weighted * old_part[..., None]
        + new_part[..., None] * new_values.astype(jnp.float32)[:, :, None, :]
    )
    denom = total_w * old_part + new_part
    return (numer / denom[..., None]).astype(jnp.bfloat16).reshape(queries.shape[0], -1)


def shards(
    hidden_in,
    lengths,
    block_table,
    cache_keys,
    cache_values,
    attn_gain,
    w_query,
    w_kv,
    w_out,
    ffn_gain,
    w_gate_up,
    w_down,
):
    highest = lax.Precision.HIGHEST
    req_count = hidden_in.shape[0]
    slot_count, blk_len, kv_width = cache_keys.shape
    head_dim = HD
    kv_local = kv_width // head_dim
    group_size = w_query.shape[1] // kv_width
    scale_val = 1.0 / math.sqrt(head_dim)
    resid = hidden_in.astype(jnp.float32)
    normed = (resid * attn_gain.astype(jnp.float32)).astype(jnp.bfloat16)
    query_part = jnp.dot(normed, w_query, preferred_element_type=jnp.float32)
    kv_part = jnp.dot(normed, w_kv.reshape(w_kv.shape[0], -1), preferred_element_type=jnp.float32)
    query_sum, kv_sum, power_sum = lax.psum((query_part, kv_part, jnp.sum(resid * resid, 1)), "mem")
    attn_scale = lax.rsqrt(power_sum / D + NORM_EPS)
    query_rot = rotate((query_sum * attn_scale[:, None]).reshape(req_count, -1, head_dim), lengths)
    queries = query_rot.astype(jnp.bfloat16).reshape(req_count, kv_local, group_size, head_dim)
    kv_scaled = kv_sum * attn_scale[:, None]
    new_keys = rotate(
        kv_scaled[:, :kv_width].reshape(req_count, kv_local, head_dim), lengths
    ).astype(jnp.bfloat16)
    new_values = kv_scaled[:, kv_width:].reshape(req_count, kv_local, head_dim).astype(jnp.bfloat16)
    blk_count = block_table.shape[1]
    mem_pos = lax.axis_index("mem")
    block_first = jnp.arange(blk_count, dtype=jnp.int32) * blk_len
    is_live = block_first[None, :] < lengths[:, None]
    local_slot = block_table - mem_pos * slot_count
    slot_ids = jnp.arange(slot_count, dtype=jnp.int32)
    owners = is_live[:, :, None] & (local_slot[:, :, None] == slot_ids[None, None, :])
    slot_member = jnp.any(owners, 1).T
    block_fill = jnp.clip(lengths[:, None] - block_first[None, :], 0, blk_len)
    slot_fill = jnp.sum(jnp.where(owners, block_fill[:, :, None], 0), (0, 1))
    queries_slot = jnp.dot(
        slot_member.astype(jnp.bfloat16),
        queries.reshape(req_count, -1),
        preferred_element_type=jnp.float32,
    )
    queries_slot = queries_slot.astype(jnp.bfloat16).reshape(
        slot_count, kv_local, group_size, head_dim
    )
    key_rows = cache_keys.reshape(slot_count, blk_len, kv_local, head_dim)
    value_rows = cache_values.reshape(slot_count, blk_len, kv_local, head_dim)
    peak_val, total_w, weighted = slot_stats(
        queries_slot, key_rows, value_rows, slot_fill, scale_val
    )
    member_mask = slot_member[:, :, None, None]
    req_peak = jnp.max(jnp.where(member_mask, peak_val[:, None], NEG_FILL), 0)
    slot_ref = jnp.max(jnp.where(member_mask, req_peak[None], NEG_FILL), 1)
    factor = jnp.exp(peak_val - slot_ref)
    member_wide = slot_member.astype(jnp.float32)
    req_total = jnp.einsum("sr,skg->rkg", member_wide, total_w * factor, precision=highest)
    req_weighted = jnp.einsum(
        "sr,skgd->rkgd", member_wide, weighted * factor[..., None], precision=highest
    )
    all_peak, all_total, all_weighted = combined_all(
        (req_peak, req_total, req_weighted), "mem", combine
    )
    attended = finish(all_peak, all_total, all_weighted, queries, new_keys, new_values, scale_val)
    attn_proj = jnp.dot(attended, w_out, preferred_element_type=jnp.float32)
    attn_sum = lax.psum(attn_proj, "comp")
    middle = (resid + attn_sum).astype(jnp.bfloat16)
    middle_wide = middle.astype(jnp.float32)
    normed_ffn = (middle_wide * ffn_gain.astype(jnp.float32)).astype(jnp.bfloat16)
    gate_up = jnp.einsum("rd,dtf->rtf", normed_ffn, w_gate_up, preferred_element_type=jnp.float32)
    middle_power = jnp.sum(middle_wide * middle_wide, 1)
    gate_up_sum, power_total = lax.psum((gate_up, middle_power), "mem")
    ffn_scale = lax.rsqrt(power_total / D + NORM_EPS)
    activated = (
        jax.nn.silu(gate_up_sum[:, 0] * ffn_scale[:, None])
        * (gate_up_sum[:, 1] * ffn_scale[:, None])
    ).astype(jnp.bfloat16)
    down_part = jnp.dot(activated, w_down, preferred_element_type=jnp.float32)
    down_sum = lax.psum(down_part, "comp")
    updated = (middle_wide + down_sum).astype(jnp.bfloat16)
    return (attended, updated)


def solution(mesh):
    in_specs = (
        P("groups", "mem"),
        P("groups"),
        P("groups", None),
        P(("groups", "mem"), None, "comp"),
        P(("groups", "mem"), None, "comp"),
        P("mem"),
        P("mem", "comp"),
        P("mem", None, "comp"),
        P("comp", "mem"),
        P("mem"),
        P("mem", None, "comp"),
        P("comp", "mem"),
    )
    out_specs = (P("groups", "comp"), P("groups", "mem"))
    return jax.shard_map(shards, mesh=mesh, in_specs=in_specs, out_specs=out_specs, check_vma=False)
```

profile of v0, /device:TPU:0, one launch (start us, length us, event | category | flops | bytes accessed | tf_op | source)
XLA Modules:
  0.0 255.8 jit_solution(6227908742854400100)
XLA Ops:
  7.2 0.7 convert_element_type.66
  7.9 2.0 copy.119
  10.0 5.8 %fusion.54 = f32[32,2048]{1,0:T(8,128)} fusion(bf16[2048,2048]{1,0:T(8,128)(2,1)} %param.20, bf16[32,2048]{1,0:T(8,128)(2,1)} %param.14, f32[2048]{0:T(1024)S(1)} %convert_element_type.66), kind=kOutput, calls=%fused_computation.72 | convolution fusion | flops 268632064 | bytes 8790016 | tf_op jit(solution)/shard_map/dot_general | solution.py:110
  15.7 1.1 fusion.52
  16.9 0.1 fusion.37
  17.1 13.5 %psum.50 = f32[32]{0:T(128)S(1)} all-reduce(f32[32]{0:T(128)S(1)} %fusion.37), channel_id=1, replica_groups=mesh['groups'=2,'mem'=4,'comp'=4] {'mem'}, use_global_device_ids=true, to_apply=%region_4.0 | all-reduce | flops 32 | bytes 256 | tf_op jit(solution)/shard_map/psum | solution.py:112
  30.7 0.6 fusion.23
  31.4 0.3 select_reduce_fusion
  31.7 0.1 multiply_cosine_fusion
  31.9 24.1 %all-reduce.12.cloned.1.call-done = (f32[32,2048]{1,0:T(8,128)}, f32[32,512]{1,0:T(8,128)}) async-done(((f32[32,2048]{1,0:T(8,128)}, f32[32,512]{1,0:T(8,128)}), (f32[32,2048]{1,0:T(8,128)}, f32[32,512]{1,0:T(8,128)})) %all-reduce.12.cloned.1.call-update) | async-done | bytes 327696 | tf_op jit(solution)/shard_map/psum | solution.py:112
  56.0 1.0 multiply_bitcast_fusion
  57.1 0.2 subtract_convert_fusion
  57.3 0.1 pad_maximum_fusion
  57.4 0.2 fusion.21
  57.7 4.1 %fusion.70 = (f32[40,2,8]{2,1,0:T(2,128)S(1)}, f32[40,2,8,256]{3,2,1,0:T(8,128)S(1)}) fusion(bf16[40,2,8,128]{3,2,1,0:T(8,128)(2,1)S(1)} %bitcast.120, pred[40,256]{1,0:T(8,128)(4,1)S(1)} %iota_compare_fusion.1, bf16[40,256,256]{2,1,0:T(8,128)(2,1)} %param.17), kind=kOutput, calls=%fused_computation.103 | convolution fusion | flops 42433920 | bytes 6074880 | tf_op jit(solution)/shard_map/skgd,sbkd->skgb/dot_general | solution.py:41
  61.9 0.2 select_reduce_fusion.2
  62.0 0.1 select_reduce_fusion.1
  62.2 0.1 copy.92
  62.3 3.3 %fusion.18 = f32[40,2,8,128]{3,2,1,0:T(8,128)S(1)} fusion(f32[40,2,8,256]{3,2,1,0:T(8,128)S(1)} %get-tuple-element.111, f32[40,2,8]{2,1,0:T(2,128)S(1)} %get-tuple-element.110, pred[40,256]{1,0:T(8,128)(4,1)S(1)} %iota_compare_fusion.1, f32[40,2,8]{2,1,0:T(2,128)S(1)} %copy.92, bf16[40,256,256]{2,1,0:T(8,128)(2,1)} %param.18), kind=kOutput, calls=%fused_computation.21 | convolution fusion | flops 42516480 | bytes 6241280 | tf_op jit(solution)/shard_map/skgb,sbkd->skgd/dot_general | solution.py:51
  65.6 1.1 fusion.31
  66.8 0.3 fusion.25
  67.2 0.1 convolution_bitcast_fusion
  67.4 0.1 copy.90
  67.5 14.0 %all-gather.1 = f32[128,2,8]{2,1,0:T(2,128)S(1)} all-gather(f32[32,2,8]{2,1,0:T(2,128)S(1)} %copy.90), channel_id=3, replica_groups=mesh['groups'=2,'mem'=4,'comp'=4] {'mem'}, dimensions={0}, use_global_device_ids=true | all-gather | bytes 10240 | tf_op jit(solution)/shard_map/all_gather | solution.py:18
  81.5 14.4 %all-gather = f32[128,2,8]{2,1,0:T(2,128)S(1)} all-gather(f32[32,2,8]{2,1,0:T(2,128)S(1)} %select_reduce_fusion.2), channel_id=2, replica_groups=mesh['groups'=2,'mem'=4,'comp'=4] {'mem'}, dimensions={0}, use_global_device_ids=true | all-gather | bytes 10240 | tf_op jit(solution)/shard_map/all_gather | solution.py:18
  96.1 0.1 subtract_convert_fusion.1
  96.3 0.1 maximum_bitcast_fusion
  96.4 0.3 fusion.51
  96.8 0.1 copy.100
  97.1 1.0 slice.67
  98.1 0.2 copy.98
  98.2 1.2 slice.70
  99.4 1.7 while.14
  99.6 0.1 copy.159
  99.7 0.3 fusion.85
  100.3 0.3 fusion.85
  100.8 0.3 fusion.85
  101.4 0.3 divide_convert_fusion
  101.8 5.7 %fusion.71 = f32[32,2048]{1,0:T(8,128)} fusion(bf16[32,2048]{1,0:T(8,128)(2,1)S(1)} %bitcast.118, bf16[2048,2048]{1,0:T(8,128)(2,1)} %param.22), kind=kOutput, calls=%fused_computation.104 | convolution fusion | flops 268435456 | bytes 8781824 | tf_op jit(solution)/shard_map/dot_general | solution.py:157
  107.5 0.2 all-reduce.8.cloned.1.call-start
  107.7 31.9 %all-reduce.6.cloned.1.call-done = f32[32,2048]{1,0:T(8,128)} async-done(((f32[32,2048]{1,0:T(8,128)}), f32[32,2048]{1,0:T(8,128)}) %all-reduce.6.cloned.1.call-update) | async-done | bytes 262160 | tf_op jit(solution)/shard_map/psum | solution.py:158
  139.6 1.1 fusion.40
  140.7 18.8 %fusion.4 = f32[32,2,3584]{2,0,1:T(8,128)} fusion(bf16[2048,2,3584]{2,1,0:T(2,128)(2,1)} %param.24, bf16[32,2048]{1,0:T(8,128)(2,1)S(1)} %get-tuple-element.100, f32[2048]{0:T(1024)S(1)} %convert_element_type.77), kind=kOutput, calls=%fused_computation.10 | convolution fusion | flops 939720704 | bytes 30416896 | tf_op jit(solution)/shard_map/rd,dtf->rtf/dot_general | solution.py:162
  159.5 11.9 %psum.54 = f32[32]{0:T(128)S(1)} all-reduce(f32[32]{0:T(128)S(1)} %get-tuple-element.99), channel_id=1, replica_groups=mesh['groups'=2,'mem'=4,'comp'=4] {'mem'}, use_global_device_ids=true, to_apply=%region_15.16 | all-reduce | flops 32 | bytes 256 | tf_op jit(solution)/shard_map/psum | solution.py:164
  171.4 36.0 %all-reduce.8.cloned.1.call-done = f32[32,2,3584]{2,0,1:T(8,128)} async-done(((f32[32,2,3584]{2,0,1:T(8,128)}), f32[32,2,3584]{2,0,1:T(8,128)}) %all-reduce.8.cloned.1.call-update) | async-done | bytes 917520 | tf_op jit(solution)/shard_map/psum | solution.py:164
  207.4 8.9 %fusion.42 = f32[32,2048]{1,0:T(8,128)} fusion(bf16[3584,2048]{1,0:T(8,128)(2,1)} %param.25, f32[32,2,3584]{2,0,1:T(8,128)} %all-reduce.8.cloned.1.call-done, f32[32]{0:T(128)S(1)} %add_rsqrt_fusion), kind=kOutput, calls=%fused_computation.60 | convolution fusion | flops 470679552 | bytes 15859840 | tf_op jit(solution)/shard_map/dot_general | solution.py:170
  216.3 31.4 %all-reduce.10.cloned.1.call-done = f32[32,2048]{1,0:T(8,128)} async-done(((f32[32,2048]{1,0:T(8,128)}), f32[32,2048]{1,0:T(8,128)}) %all-reduce.10.cloned.1.call-update) | async-done | bytes 262160 | tf_op jit(solution)/shard_map/psum | solution.py:171
  247.7 1.6 fusion.41
  (65 shorter events, 2.2 us)
Async XLA Ops:
  7.2 48.9 %all-reduce.12.cloned.1.call-start = ((), (), s32[]{:S(2)}) async-start(), calls=%async_computation.4 | async-start | bytes 655360 | tf_op jit(solution)/shard_map/psum | solution.py:112
  9.9 5.8 %copy-start = (bf16[32,2048]{1,0:T(8,128)(2,1)S(1)}, bf16[32,2048]{1,0:T(8,128)(2,1)}, u32[]{:S(2)}) copy-start(bf16[32,2048]{1,0:T(8,128)(2,1)} %param.14) | copy-start | bytes 393220
  10.0 7.1 %copy-start.5 = (s32[32]{0:T(128)S(1)}, s32[32]{0:T(128)}, u32[]{:S(2)}) copy-start(s32[32]{0:T(128)} %param.15) | copy-start | bytes 388
  10.0 20.7 %copy-start.3 = (s32[32,128]{1,0:T(8,128)S(1)}, s32[32,128]{1,0:T(8,128)}, u32[]{:S(2)}) copy-start(s32[32,128]{1,0:T(8,128)} %param.16) | copy-start | bytes 49156
  16.9 80.2 %all-gather.5.cloned.1.call-start = ((), (), s32[]{:S(2)}) async-start(), calls=%async_computation.3 | async-start | bytes 1310720 | tf_op jit(solution)/shard_map/all_gather | solution.py:18
  62.0 34.0 %copy-start.2 = (f32[32,512]{1,0:T(8,128)S(1)}, f32[32,512]{1,0:T(8,128)}, u32[]{:S(2)}) copy-start(f32[32,512]{1,0:T(8,128)} %get-tuple-element.94) | copy-start | bytes 196612
  66.8 72.8 %all-reduce.6.cloned.1.call-start = ((), (), s32[]{:S(2)}) async-start(), calls=%async_computation | async-start | bytes 524288 | tf_op jit(solution)/shard_map/psum | solution.py:158
  101.7 5.7 %copy-start.1 = (bf16[4,8,16,128]{3,1,2,0:T(8,128)(2,1)}, bf16[4,8,16,128]{3,1,2,0:T(8,128)(2,1)S(1)}, u32[]{:S(2)}) copy-start(bf16[4,8,16,128]{3,1,2,0:T(8,128)(2,1)S(1)} %copy.153) | copy-start | bytes 393220
  101.8 6.0 %copy-start.4 = (bf16[2048]{0:T(1024)(128)(2,1)S(1)}, bf16[2048]{0:T(1024)(128)(2,1)}, u32[]{:S(2)}) copy-start(bf16[2048]{0:T(1024)(128)(2,1)} %param.23) | copy-start | bytes 12292
  107.5 99.9 %all-reduce.8.cloned.1.call-start = ((), (), s32[]{:S(2)}) async-start(), calls=%async_computation.1 | async-start | bytes 1835008 | tf_op jit(solution)/shard_map/psum | solution.py:164
  159.5 88.2 %all-reduce.10.cloned.1.call-start = ((), (), s32[]{:S(2)}) async-start(), calls=%async_computation.2 | async-start | bytes 524288 | tf_op jit(solution)/shard_map/psum | solution.py:171
Sparse Core Ops, SparseCore 0:
  17.0 39.0 all-reduce.11
  66.9 30.1 all-gather.4
  107.6 31.9 all-reduce.5
  159.6 47.7 all-reduce.7
  216.4 31.1 all-reduce.9
where the time goes:
time: 256 us
  waiting for transfers between devices  124 us (48%)
  blocking collectives  53.8 us (21%)
  matrix products  49.3 us (19%)
  between operations  14.1 us (6%)
  other arithmetic  8.38 us (3%)
  local copies, waits for them, and re-layouts  6.15 us (2%)
    psum x1, waiting for transfers between devices, shards(): gate_up_sum, power_total = lax.psum((gate_up, middle_power), 'mem')  36 us
    psum x1, waiting for transfers between devices, shards(): attn_sum = lax.psum(attn_proj, 'comp')  31.9 us
    psum x1, waiting for transfers between devices, shards(): down_sum = lax.psum(down_part, 'comp')  31.4 us
    all_gather x2, blocking collectives, combined_all(): pieces = jax.tree.map(lambda part: lax.all_gather(part, axis), value)  28.5 us
    psum x1, waiting for transfers between devices, shards(): lax.psum((query_part, kv_part, jnp.sum(resid * resid, 1)), 'mem')  24.1 us
    dot_general x1, matrix products, shards(): jnp.einsum('rd,dtf->rtf', normed_ffn, w_gate_up, preferred_element_type=j...  18.8 us
    psum x1, blocking collectives, shards(): lax.psum((query_part, kv_part, jnp.sum(resid * resid, 1)), 'mem')  13.5 us
    psum x1, blocking collectives, shards(): gate_up_sum, power_total = lax.psum((gate_up, middle_power), 'mem')  11.9 us
  transfers between devices with their start and end apart: 5, of which 5 were waited for; matrix products, arithmetic and copies ran while one was open for 1% of the time, Pallas kernels for 0%

commit v1 on v0

v1 whole, which is shorter than its diff:
```python
import math

import jax
import jax.numpy as jnp
from jax import lax
from jax.sharding import PartitionSpec as P

D = 8192
HD = 128
NORM_EPS = 1e-05
ROPE_BASE = 500000.0
NEG_FILL = -1e30


def to_bf16(x):
    return x.astype(jnp.bfloat16)


def shifted(x, axis, n, step):
    return lax.ppermute(x, axis, [(i, (i + step) % n) for i in range(n)])


def split_hi_lo(x):
    hi = lax.reduce_precision(x, 8, 7)
    return to_bf16(hi), to_bf16(x - hi)


def scatter_parts(x, axis, n):
    me = lax.axis_index(axis)
    parts = []
    for step in range(1, n):
        send = lax.dynamic_index_in_dim(x, (me + step) % n, 0, False)
        parts.append(shifted(send, axis, n, step))
    return parts


def gather_parts(x, axis, n):
    me = lax.axis_index(axis)
    parts = [shifted(x, axis, n, step) for step in range(n - 1, 0, -1)] + [x]
    both = jnp.concatenate(parts + parts, 0)
    rows = x.shape[0]
    return lax.dynamic_slice_in_dim(both, (n - 1 - me) * rows, n * rows, 0)


def summed(x, axis, n):
    me = lax.axis_index(axis)
    rows = x.shape[0] // n
    x = x.reshape((n, rows) + x.shape[1:])
    own = lax.dynamic_index_in_dim(x, me, 0, False)
    for part in scatter_parts(to_bf16(x), axis, n):
        own = own + part.astype(jnp.float32)
    return own


def rotary(positions, head_dim):
    half_dim = head_dim // 2
    freq_steps = jnp.arange(half_dim, dtype=jnp.float32) * (2.0 / head_dim)
    inv_freq = jnp.exp(-freq_steps * math.log(ROPE_BASE))
    angles = positions.astype(jnp.float32)[:, None, None] * inv_freq
    return jnp.cos(angles), jnp.sin(angles)


def rotate(values, cosine, sine):
    half_dim = values.shape[-1] // 2
    first_half = values[..., :half_dim]
    second_half = values[..., half_dim:]
    return jnp.concatenate(
        [first_half * cosine - second_half * sine, second_half * cosine + first_half * sine], -1
    )


def slot_stats(queries_slot, key_rows, value_rows, slot_fill, scale_val):
    scores = (
        jnp.einsum("skgd,sbkd->skgb", queries_slot, key_rows, preferred_element_type=jnp.float32)
        * scale_val
    )
    is_valid = (jnp.arange(key_rows.shape[1], dtype=jnp.int32)[None, :] < slot_fill[:, None])[
        :, None, None, :
    ]
    scores = jnp.where(is_valid, scores, NEG_FILL)
    peak_val = jnp.max(scores, -1)
    weights = jnp.where(is_valid, jnp.exp(scores - peak_val[..., None]), 0.0)
    total_w = jnp.sum(weights, -1)
    weighted = jnp.einsum(
        "skgb,sbkd->skgd",
        weights.astype(jnp.bfloat16),
        value_rows,
        preferred_element_type=jnp.float32,
    )
    return (peak_val, total_w, weighted)


def make_shards(n_mem, n_comp):
    def shards(
        hidden_in,
        lengths,
        block_table,
        cache_keys,
        cache_values,
        attn_gain,
        w_query,
        w_kv,
        w_out,
        ffn_gain,
        w_gate_up,
        w_down,
    ):
        highest = lax.Precision.HIGHEST
        req_count = hidden_in.shape[0]
        slot_count, blk_len, kv_width = cache_keys.shape
        head_dim = HD
        kv_local = kv_width // head_dim
        q_width = w_query.shape[1]
        group_size = q_width // kv_width
        scale_val = 1.0 / math.sqrt(head_dim)
        mem_pos = lax.axis_index("mem")
        rows = req_count // n_mem
        resid = hidden_in.astype(jnp.float32)
        normed = to_bf16(resid * attn_gain.astype(jnp.float32))
        query_part = jnp.dot(normed, w_query, preferred_element_type=jnp.float32)
        kv_part = jnp.dot(
            normed, w_kv.reshape(w_kv.shape[0], -1), preferred_element_type=jnp.float32
        )
        power = jnp.sum(resid * resid, 1)
        wide = jnp.concatenate(
            [query_part, kv_part, jnp.broadcast_to(power[:, None], (req_count, 128))], 1
        ).reshape(n_mem, rows, -1)
        total = lax.dynamic_index_in_dim(wide, mem_pos, 0, False)
        for part in scatter_parts(wide, "mem", n_mem):
            total = total + part
        body = q_width + 2 * kv_width
        attn_scale = lax.rsqrt(total[:, body] / D + NORM_EPS)
        cosine, sine = rotary(lengths, head_dim)
        cos_own = lax.dynamic_slice_in_dim(cosine, mem_pos * rows, rows, 0)
        sin_own = lax.dynamic_slice_in_dim(sine, mem_pos * rows, rows, 0)
        scaled = total[:, :body] * attn_scale[:, None]
        turned = rotate(
            scaled[:, : q_width + kv_width].reshape(rows, -1, head_dim), cos_own, sin_own
        ).reshape(rows, -1)
        own_qkv = to_bf16(jnp.concatenate([turned, scaled[:, q_width + kv_width :]], 1))
        qkv = gather_parts(own_qkv, "mem", n_mem)
        queries = qkv[:, :q_width].reshape(req_count, kv_local, group_size, head_dim)
        q_own = own_qkv[:, :q_width].reshape(rows, kv_local, group_size, head_dim)
        new_keys = own_qkv[:, q_width : q_width + kv_width].reshape(rows, kv_local, head_dim)
        new_values = own_qkv[:, q_width + kv_width :].reshape(rows, kv_local, head_dim)
        own_score = (
            jnp.einsum("rkgd,rkd->rkg", q_own, new_keys, preferred_element_type=jnp.float32)
            * scale_val
        )

        blk_count = block_table.shape[1]
        block_first = jnp.arange(blk_count, dtype=jnp.int32) * blk_len
        is_live = block_first[None, :] < lengths[:, None]
        local_slot = block_table - mem_pos * slot_count
        slot_ids = jnp.arange(slot_count, dtype=jnp.int32)
        owners = is_live[:, :, None] & (local_slot[:, :, None] == slot_ids[None, None, :])
        slot_member = jnp.any(owners, 1).T
        block_fill = jnp.clip(lengths[:, None] - block_first[None, :], 0, blk_len)
        slot_fill = jnp.sum(jnp.where(owners, block_fill[:, :, None], 0), (0, 1))
        queries_slot = jnp.dot(
            slot_member.astype(jnp.bfloat16),
            queries.reshape(req_count, -1),
            preferred_element_type=jnp.float32,
        )
        queries_slot = queries_slot.astype(jnp.bfloat16).reshape(
            slot_count, kv_local, group_size, head_dim
        )
        key_rows = cache_keys.reshape(slot_count, blk_len, kv_local, head_dim)
        value_rows = cache_values.reshape(slot_count, blk_len, kv_local, head_dim)
        peak_val, total_w, weighted = slot_stats(
            queries_slot, key_rows, value_rows, slot_fill, scale_val
        )
        member_mask = slot_member[:, :, None, None]
        req_peak = jnp.max(jnp.where(member_mask, peak_val[:, None], NEG_FILL), 0)
        peak_hi = lax.reduce_precision(req_peak, 8, 7)
        peak_lo = lax.reduce_precision(req_peak - peak_hi, 8, 7)
        req_peak = peak_hi + peak_lo
        slot_ref = jnp.min(jnp.where(member_mask, req_peak[None], -NEG_FILL), 1)
        factor = jnp.exp(peak_val - slot_ref)
        member_wide = slot_member.astype(jnp.float32)
        req_total = jnp.einsum("sr,skg->rkg", member_wide, total_w * factor, precision=highest)
        req_weighted = jnp.einsum(
            "sr,skgd->rkgd", member_wide, weighted * factor[..., None], precision=highest
        )
        tot_hi = lax.reduce_precision(req_total, 8, 7)
        tot_lo = req_total - tot_hi
        stats = jnp.concatenate(
            [s.reshape(req_count, -1) for s in (peak_hi, peak_lo, tot_hi, tot_lo)], 1
        )
        n_stat = kv_local * group_size
        pad = (-stats.shape[1]) % 128
        stats = jnp.pad(stats, ((0, 0), (0, pad)))
        packed = to_bf16(jnp.concatenate([req_weighted.reshape(req_count, -1), stats], 1))
        packed = packed.reshape(n_mem, rows, -1)
        pieces = [lax.dynamic_index_in_dim(packed, mem_pos, 0, False)]
        pieces += scatter_parts(packed, "mem", n_mem)
        peaks, totals, tops = [], [], []
        for piece in pieces:
            st = piece[:, q_width : q_width + 4 * n_stat].astype(jnp.float32)
            st = st.reshape(rows, 4, kv_local, group_size)
            peaks.append(st[:, 0] + st[:, 1])
            totals.append(st[:, 2] + st[:, 3])
            tops.append(
                piece[:, :q_width]
                .astype(jnp.float32)
                .reshape(rows, kv_local, group_size, head_dim)
            )
        peak = own_score
        for p in peaks:
            peak = jnp.maximum(peak, p)
        own_weight = jnp.exp(own_score - peak)
        denom = own_weight
        numer = own_weight[..., None] * new_values.astype(jnp.float32)[:, :, None, :]
        for p, t, w in zip(peaks, totals, tops):
            f = jnp.exp(p - peak)
            denom = denom + t * f
            numer = numer + w * f[..., None]
        attended_own = to_bf16(numer / denom[..., None]).reshape(rows, -1)
        attended = gather_parts(attended_own, "mem", n_mem)

        comp_pos = lax.axis_index("comp")
        rows_c = req_count // n_comp
        attn_proj = jnp.dot(attended, w_out, preferred_element_type=jnp.float32)
        resid_own = lax.dynamic_slice_in_dim(hidden_in, comp_pos * rows_c, rows_c, 0)
        middle_own = to_bf16(resid_own.astype(jnp.float32) + summed(attn_proj, "comp", n_comp))
        middle = gather_parts(middle_own, "comp", n_comp)
        middle_wide = middle.astype(jnp.float32)
        normed_ffn = to_bf16(middle_wide * ffn_gain.astype(jnp.float32))
        gate_up = jnp.einsum(
            "rd,dtf->rtf", normed_ffn, w_gate_up, preferred_element_type=jnp.float32
        ).reshape(req_count, -1)
        m_hi, m_lo = split_hi_lo(jnp.sum(middle_wide * middle_wide, 1))
        wide = jnp.concatenate(
            [
                to_bf16(gate_up),
                jnp.broadcast_to(m_hi[:, None], (req_count, 128)),
                jnp.broadcast_to(m_lo[:, None], (req_count, 128)),
            ],
            1,
        ).reshape(n_mem, rows, -1)
        total = lax.dynamic_index_in_dim(wide, mem_pos, 0, False).astype(jnp.float32)
        for part in scatter_parts(wide, "mem", n_mem):
            total = total + part.astype(jnp.float32)
        ff = w_gate_up.shape[2]
        ffn_scale = lax.rsqrt((total[:, 2 * ff] + total[:, 2 * ff + 128]) / D + NORM_EPS)
        gate = total[:, :ff] * ffn_scale[:, None]
        up = total[:, ff : 2 * ff] * ffn_scale[:, None]
        activated = gather_parts(to_bf16(jax.nn.silu(gate) * up), "mem", n_mem)
        down_part = jnp.dot(activated, w_down, preferred_element_type=jnp.float32)
        updated_own = to_bf16(middle_own.astype(jnp.float32) + summed(down_part, "comp", n_comp))
        updated = gather_parts(updated_own, "comp", n_comp)
        return (attended, updated)

    return shards


def solution(mesh):
    in_specs = (
        P("groups", "mem"),
        P("groups"),
        P("groups", None),
        P(("groups", "mem"), None, "comp"),
        P(("groups", "mem"), None, "comp"),
        P("mem"),
        P("mem", "comp"),
        P("mem", None, "comp"),
        P("comp", "mem"),
        P("mem"),
        P("mem", None, "comp"),
        P("comp", "mem"),
    )
    out_specs = (P("groups", "comp"), P("groups", "mem"))
    return jax.shard_map(
        make_shards(mesh.shape["mem"], mesh.shape["comp"]),
        mesh=mesh,
        in_specs=in_specs,
        out_specs=out_specs,
        check_vma=False,
    )
```

time: 256 us -> 135 us (0.53)
  waiting for transfers between devices: 124 us -> 39.7 us
  blocking collectives: 53.8 us -> 0 us
  starting transfers between devices: 0.39 us -> 37 us
  between operations: 14.1 us -> 1.3 us
  matrix products: 49.3 us -> 45.2 us
  other arithmetic: 8.38 us -> 5.13 us
    psum x4 -> x0, waiting for transfers between devices: 123 us -> none  [the longest x1 36 us: shards(): gate_up_sum, power_total = lax.psum((gate_up, middle_power), 'mem')]
    ppermute x0 -> x30, waiting for transfers between devices: none -> 39.7 us  [shifted(): return lax.ppermute(x, axis, [(i, (i + step) % n) for i in range(n)])]
    ppermute x0 -> x30, starting transfers between devices: none -> 37 us  [shifted(): return lax.ppermute(x, axis, [(i, (i + step) % n) for i in range(n)])]
    all_gather x2 -> x0, blocking collectives: 28.5 us -> none  [combined_all(): pieces = jax.tree.map(lambda part: lax.all_gather(part, axis), value)]
    psum x2 -> x0, blocking collectives: 25.4 us -> none  [the longest x1 13.5 us: shards(): lax.psum((query_part, kv_part, jnp.sum(resid * resid, 1)), 'mem')]
  transfers between devices with their start and end apart: 5 -> 30, of which waited for: 5 -> 25; matrix products, arithmetic and copies ran while one was open for 1% -> 1% of each run, Pallas kernels for 0% -> 0%
where the time goes in v1:
time: 135 us; the launch traced here: 134 us
  matrix products  45.2 us (33%)
  waiting for transfers between devices  39.7 us (29%)
  starting transfers between devices  37 us (27%)
  local copies, waits for them, and re-layouts  5.98 us (4%)
  other arithmetic  5.13 us (4%)
    ppermute x30, waiting for transfers between devices, shifted(): return lax.ppermute(x, axis, [(i, (i + step) % n) for i in range(n)])  39.7 us
    ppermute x30, starting transfers between devices, shifted(): return lax.ppermute(x, axis, [(i, (i + step) % n) for i in range(n)])  37 us
    dot_general x1, matrix products, shards(): jnp.einsum('rd,dtf->rtf', normed_ffn, w_gate_up, preferred_element_type=j...  17.9 us
    dot_general x1, matrix products, shards(): down_part = jnp.dot(activated, w_down, preferred_element_type=jnp.float32)  7.88 us
    dot_general x1, matrix products, shards(): attn_proj = jnp.dot(attended, w_out, preferred_element_type=jnp.float32)  4.98 us
    dot_general x1, matrix products, shards(): query_part = jnp.dot(normed, w_query, preferred_element_type=jnp.float32)  4.94 us
    dot_general x1, matrix products, slot_stats(): jnp.einsum('skgd,sbkd->skgb', queries_slot, key_rows, preferred_element_t...  4.05 us
    dot_general x1, matrix products, slot_stats(): jnp.einsum('skgb,sbkd->skgd', weights.astype(jnp.bfloat16), value_rows, p...  3.35 us
  transfers between devices with their start and end apart: 30, of which 25 were waited for; matrix products, arithmetic and copies ran while one was open for 1% of the time, Pallas kernels for 0%

profile of v1, /device:TPU:0, one launch (start us, length us, event | category | flops | bytes accessed | tf_op | source)
XLA Modules:
  0.0 134.3 jit_solution(3371468088080689455)
XLA Ops:
  0.7 0.7 convert_element_type.140
  1.4 2.0 %copy.160 = bf16[256,8,2,256]{3,1,2,0:T(8,128)(2,1)S(1)} copy(bf16[256,8,2,256]{3,2,1,0:T(2,128)(2,1)} %bitcast.223) | data formatting | bytes 4194304
  3.4 1.0 fusion.33
  4.5 1.4 %fusion.46 = f32[32,512]{1,0:T(8,128)S(1)} fusion(bf16[2048,512]{1,0:T(8,128)(2,1)S(1)} %bitcast.222, bf16[32,2048]{1,0:T(8,128)(2,1)} %param.12, f32[2048]{0:T(1024)S(1)} %convert_element_type.140), kind=kOutput, calls=%fused_computation.60 | convolution fusion | flops 67305472 | bytes 2301952 | tf_op jit(solution)/shard_map/dot_general | solution.py:121
  5.9 4.9 %fusion.48 = f32[32,2048]{1,0:T(8,128)S(1)} fusion(bf16[2048,2048]{1,0:T(8,128)(2,1)} %param.18, bf16[32,2048]{1,0:T(8,128)(2,1)S(1)} %copy-done, f32[2048]{0:T(1024)S(1)} %convert_element_type.140), kind=kOutput, calls=%fused_computation.61 | convolution fusion | flops 268632064 | bytes 8790016 | tf_op jit(solution)/shard_map/dot_general | solution.py:120
  11.0 3.1 %collective-permute-start = (f32[8,2688]{1,0:T(8,128)S(1)}, f32[8,2688]{1,0:T(8,128)S(1)}, u32[]{:S(2)}, u32[]{:S(2)}) collective-permute-start(f32[8,2688]{1,0:T(8,128)S(1)} %get-tuple-element.13), channel_id=1, source_target_pairs={{0,4},{4,8},{8,12},{12,0},{1,5},{5,9},{9,13},{13,1},{2,6},{6,10},{... | collective-permute-start | bytes 258056 | tf_op jit(solution)/shard_map/ppermute | solution.py:20
  14.0 2.6 %collective-permute-start.1 = (f32[8,2688]{1,0:T(8,128)S(1)}, f32[8,2688]{1,0:T(8,128)S(1)}, u32[]{:S(2)}, u32[]{:S(2)}) collective-permute-start(f32[8,2688]{1,0:T(8,128)S(1)} %get-tuple-element.15), channel_id=1, source_target_pairs={{0,8},{4,12},{8,0},{12,4},{1,9},{5,13},{9,1},{13,5},{2,10},{6,14},... | collective-permute-start | bytes 258056 | tf_op jit(solution)/shard_map/ppermute | solution.py:20
  16.6 1.3 %collective-permute-start.2 = (f32[8,2688]{1,0:T(8,128)S(1)}, f32[8,2688]{1,0:T(8,128)S(1)}, u32[]{:S(2)}, u32[]{:S(2)}) collective-permute-start(f32[8,2688]{1,0:T(8,128)S(1)} %get-tuple-element.14), channel_id=1, source_target_pairs={{0,12},{4,0},{8,4},{12,8},{1,13},{5,1},{9,5},{13,9},{2,14},{6,2},{... | collective-permute-start | bytes 258056 | tf_op jit(solution)/shard_map/ppermute | solution.py:20
  19.3 3.1 %collective-permute-done.1 = f32[8,2688]{1,0:T(8,128)S(1)} collective-permute-done((f32[8,2688]{1,0:T(8,128)S(1)}, f32[8,2688]{1,0:T(8,128)S(1)}, u32[]{:S(2)}, u32[]{:S(2)}) %collective-permute-start.1) | collective-permute-done | bytes 86048 | tf_op jit(solution)/shard_map/ppermute | solution.py:20
  23.0 3.4 %collective-permute-start.3 = (bf16[8,2560]{1,0:T(8,128)(2,1)S(1)}, bf16[8,2560]{1,0:T(8,128)(2,1)S(1)}, u32[]{:S(2)}, u32[]{:S(2)}) collective-permute-start(bf16[8,2560]{1,0:T(8,128)(2,1)S(1)} %pad_maximum_fusion.1), channel_id=1, source_target_pairs={{0,12},{4,0},{8,4},{12,8},{1,13},{5,1},{9,5},{13,9},{2,14},{6,2},{... | collective-permute-start | bytes 122888 | tf_op jit(solution)/shard_map/ppermute | solution.py:20
  27.2 0.9 collective-permute-done.3
  28.1 3.3 %collective-permute-done.4 = bf16[8,2560]{1,0:T(8,128)(2,1)S(1)} collective-permute-done((bf16[8,2560]{1,0:T(8,128)(2,1)S(1)}, bf16[8,2560]{1,0:T(8,128)(2,1)S(1)}, u32[]{:S(2)}, u32[]{:S(2)}) %collective-permute-start.4) | collective-permute-done | bytes 40992 | tf_op jit(solution)/shard_map/ppermute | solution.py:20
  31.4 1.1 collective-permute-done.5
  32.8 4.1 %fusion.105 = (f32[40,2,8]{2,1,0:T(2,128)S(1)}, f32[40,2,8,256]{3,2,1,0:T(8,128)S(1)}) fusion(bf16[40,2,8,128]{3,2,1,0:T(8,128)(2,1)S(1)} %bitcast.224, pred[40,256]{1,0:T(8,128)(4,1)S(1)} %iota_compare_fusion.1, bf16[40,256,256]{2,1,0:T(8,128)(2,1)} %param.15), kind=kOutput, calls=%fused_computation.231 | convolution fusion | flops 42433920 | bytes 6074880 | tf_op jit(solution)/shard_map/skgd,sbkd->skgb/dot_general | solution.py:74
  38.2 3.3 %fusion.20 = f32[2,8,128,40]{2,1,0,3:T(8,128)S(1)} fusion(f32[40,2,8,256]{3,2,1,0:T(8,128)S(1)} %get-tuple-element.45, f32[40,2,8]{2,1,0:T(2,128)S(1)} %get-tuple-element.44, pred[40,256]{1,0:T(8,128)(4,1)S(1)} %iota_compare_fusion.1, f32[2,8,40]{1,0,2:T(2,128)S(1)} %copy.134, bf16[40,256,256]{2,1,0:T(8,128)(2,1)} %param.16), kind=kOutput, calls=%fused_computation.16 | convolution fusion | flops 42516480 | bytes 6241280 | tf_op jit(solution)/shard_map/skgb,sbkd->skgd/dot_general | solution.py:84
  42.1 1.1 collective-permute-start.7
  43.3 2.8 %collective-permute-start.8 = (bf16[8,2176]{1,0:T(8,128)(2,1)S(1)}, bf16[8,2176]{1,0:T(8,128)(2,1)S(1)}, u32[]{:S(2)}, u32[]{:S(2)}) collective-permute-start(bf16[8,2176]{1,0:T(8,128)(2,1)S(1)} %get-tuple-element.19), channel_id=1, source_target_pairs={{0,12},{4,0},{8,4},{12,8},{1,13},{5,1},{9,5},{13,9},{2,14},{6,2},{... | collective-permute-start | bytes 104456 | tf_op jit(solution)/shard_map/ppermute | solution.py:20
  46.1 1.7 %collective-permute-done.6 = bf16[8,2176]{1,0:T(8,128)(2,1)S(1)} collective-permute-done((bf16[8,2176]{1,0:T(8,128)(2,1)S(1)}, bf16[8,2176]{1,0:T(8,128)(2,1)S(1)}, u32[]{:S(2)}, u32[]{:S(2)}) %collective-permute-start.6) | collective-permute-done | bytes 34848 | tf_op jit(solution)/shard_map/ppermute | solution.py:20
  49.7 3.4 %collective-permute-start.9 = (bf16[8,2048]{1,0:T(8,128)(2,1)S(1)}, bf16[8,2048]{1,0:T(8,128)(2,1)S(1)}, u32[]{:S(2)}, u32[]{:S(2)}) collective-permute-start(bf16[8,2048]{1,0:T(8,128)(2,1)S(1)} %divide_convert_fusion), channel_id=1, source_target_pairs={{0,12},{4,0},{8,4},{12,8},{1,13},{5,1},{9,5},{13,9},{2,14},{6,2},{... | collective-permute-start | bytes 98312 | tf_op jit(solution)/shard_map/ppermute | solution.py:20
  53.7 0.9 collective-permute-done.9
  54.6 3.2 %collective-permute-done.10 = bf16[8,2048]{1,0:T(8,128)(2,1)S(1)} collective-permute-done((bf16[8,2048]{1,0:T(8,128)(2,1)S(1)}, bf16[8,2048]{1,0:T(8,128)(2,1)S(1)}, u32[]{:S(2)}, u32[]{:S(2)}) %collective-permute-start.10) | collective-permute-done | bytes 32800 | tf_op jit(solution)/shard_map/ppermute | solution.py:20
  57.8 1.1 collective-permute-done.11
  59.0 5.0 %fusion.106 = (bf16[4,8,2048]{2,1,0:T(8,128)(2,1)S(1)}, f32[4,8,2048]{2,1,0:T(8,128)S(1)}) fusion(bf16[32,2048]{1,0:T(8,128)(2,1)S(1)} %constant_dynamic-slice_fusion, bf16[2048,2048]{1,0:T(8,128)(2,1)} %param.20), kind=kOutput, calls=%fused_computation.232 | convolution fusion | flops 268500992 | bytes 8912896 | tf_op jit(solution)/shard_map/dot_general | solution.py:223
  64.1 1.6 %collective-permute-start.13 = (bf16[8,2048]{1,0:T(8,128)(2,1)S(1)}, bf16[8,2048]{1,0:T(8,128)(2,1)S(1)}, u32[]{:S(2)}, u32[]{:S(2)}) collective-permute-start(bf16[8,2048]{1,0:T(8,128)(2,1)S(1)} %get-tuple-element.25), channel_id=1, source_target_pairs={{0,2},{1,3},{2,0},{3,1},{4,6},{5,7},{6,4},{7,5},{8,10},{9,11},{10,... | collective-permute-start | bytes 98312 | tf_op jit(solution)/shard_map/ppermute | solution.py:20
  65.7 1.4 %collective-permute-start.14 = (bf16[8,2048]{1,0:T(8,128)(2,1)S(1)}, bf16[8,2048]{1,0:T(8,128)(2,1)S(1)}, u32[]{:S(2)}, u32[]{:S(2)}) collective-permute-start(bf16[8,2048]{1,0:T(8,128)(2,1)S(1)} %get-tuple-element.24), channel_id=1, source_target_pairs={{0,3},{1,0},{2,1},{3,2},{4,7},{5,4},{6,5},{7,6},{8,11},{9,8},{10,9... | collective-permute-start | bytes 98312 | tf_op jit(solution)/shard_map/ppermute | solution.py:20
  68.7 1.8 %collective-permute-start.15 = (bf16[8,2048]{1,0:T(8,128)(2,1)S(1)}, bf16[8,2048]{1,0:T(8,128)(2,1)S(1)}, u32[]{:S(2)}, u32[]{:S(2)}) collective-permute-start(bf16[8,2048]{1,0:T(8,128)(2,1)S(1)} %fusion.59), channel_id=1, source_target_pairs={{0,3},{1,0},{2,1},{3,2},{4,7},{5,4},{6,5},{7,6},{8,11},{9,8},{10,9... | collective-permute-start | bytes 98312 | tf_op jit(solution)/shard_map/ppermute | solution.py:20
  71.0 1.1 collective-permute-done.15
  72.1 2.6 %collective-permute-done.16 = bf16[8,2048]{1,0:T(8,128)(2,1)S(1)} collective-permute-done((bf16[8,2048]{1,0:T(8,128)(2,1)S(1)}, bf16[8,2048]{1,0:T(8,128)(2,1)S(1)}, u32[]{:S(2)}, u32[]{:S(2)}) %collective-permute-start.16) | collective-permute-done | bytes 32800 | tf_op jit(solution)/shard_map/ppermute | solution.py:20
  74.9 17.9 %fusion.8 = bf16[32,2,3584]{2,0,1:T(8,128)(2,1)S(1)} fusion(bf16[2048,2,3584]{2,1,0:T(2,128)(2,1)} %param.22, f32[2048]{0:T(1024)S(1)} %convert_element_type.160, bf16[64,2048]{1,0:T(8,128)(2,1)S(1)} %constant_dynamic-update-slice_fusion.16, s32[]{:T(128)S(6)} %select_n.143), kind=kOutput, calls=%fused_computation.8 | convolution fusion | flops 939950080 | bytes 29958148 | tf_op jit(solution)/shard_map/rd,dtf->rtf/dot_general | solution.py:229
  94.0 1.0 collective-permute-start.19
  95.0 2.8 %collective-permute-start.20 = (bf16[8,7424]{1,0:T(8,128)(2,1)S(1)}, bf16[8,7424]{1,0:T(8,128)(2,1)S(1)}, u32[]{:S(2)}, u32[]{:S(2)}) collective-permute-start(bf16[8,7424]{1,0:T(8,128)(2,1)S(1)} %get-tuple-element.11), channel_id=1, source_target_pairs={{0,12},{4,0},{8,4},{12,8},{1,13},{5,1},{9,5},{13,9},{2,14},{6,2},{... | collective-permute-start | bytes 356360 | tf_op jit(solution)/shard_map/ppermute | solution.py:20
  97.9 4.1 %collective-permute-done.18 = bf16[8,7424]{1,0:T(8,128)(2,1)S(1)} collective-permute-done((bf16[8,7424]{1,0:T(8,128)(2,1)S(1)}, bf16[8,7424]{1,0:T(8,128)(2,1)S(1)}, u32[]{:S(2)}, u32[]{:S(2)}) %collective-permute-start.18) | collective-permute-done | bytes 118816 | tf_op jit(solution)/shard_map/ppermute | solution.py:20
  102.0 3.1 %collective-permute-done.19 = bf16[8,7424]{1,0:T(8,128)(2,1)S(1)} collective-permute-done((bf16[8,7424]{1,0:T(8,128)(2,1)S(1)}, bf16[8,7424]{1,0:T(8,128)(2,1)S(1)}, u32[]{:S(2)}, u32[]{:S(2)}) %collective-permute-start.19) | collective-permute-done | bytes 118816 | tf_op jit(solution)/shard_map/ppermute | solution.py:20
  105.5 2.7 %collective-permute-start.21 = (bf16[8,3584]{1,0:T(8,128)(2,1)S(1)}, bf16[8,3584]{1,0:T(8,128)(2,1)S(1)}, u32[]{:S(2)}, u32[]{:S(2)}) collective-permute-start(bf16[8,3584]{1,0:T(8,128)(2,1)S(1)} %fusion.45), channel_id=1, source_target_pairs={{0,12},{4,0},{8,4},{12,8},{1,13},{5,1},{9,5},{13,9},{2,14},{6,2},{... | collective-permute-start | bytes 172040 | tf_op jit(solution)/shard_map/ppermute | solution.py:20
  108.1 1.0 collective-permute-start.22
  109.1 0.9 collective-permute-done.21
  110.0 3.8 %collective-permute-done.22 = bf16[8,3584]{1,0:T(8,128)(2,1)S(1)} collective-permute-done((bf16[8,3584]{1,0:T(8,128)(2,1)S(1)}, bf16[8,3584]{1,0:T(8,128)(2,1)S(1)}, u32[]{:S(2)}, u32[]{:S(2)}) %collective-permute-start.22) | collective-permute-done | bytes 57376 | tf_op jit(solution)/shard_map/ppermute | solution.py:20
  113.8 1.3 collective-permute-done.23
  115.3 7.9 %fusion.107 = (bf16[4,8,2048]{2,1,0:T(8,128)(2,1)S(1)}, f32[4,8,2048]{2,1,0:T(8,128)S(1)}) fusion(bf16[3584,2048]{1,0:T(8,128)(2,1)} %param.23, bf16[64,3584]{1,0:T(8,128)(2,1)S(1)} %constant_dynamic-update-slice_fusion.24, s32[]{:T(128)S(6)} %select_n.130), kind=kOutput, calls=%fused_computation.233 | convolution fusion | flops 469827584 | bytes 15302660 | tf_op jit(solution)/shard_map/dot_general | solution.py:249
  123.3 0.7 collective-permute-start.25
  124.0 1.4 %collective-permute-start.26 = (bf16[8,2048]{1,0:T(8,128)(2,1)S(1)}, bf16[8,2048]{1,0:T(8,128)(2,1)S(1)}, u32[]{:S(2)}, u32[]{:S(2)}) collective-permute-start(bf16[8,2048]{1,0:T(8,128)(2,1)S(1)} %get-tuple-element.21), channel_id=1, source_target_pairs={{0,3},{1,0},{2,1},{3,2},{4,7},{5,4},{6,5},{7,6},{8,11},{9,8},{10,9... | collective-permute-start | bytes 98312 | tf_op jit(solution)/shard_map/ppermute | solution.py:20
  125.4 1.2 collective-permute-done.24
  126.6 0.7 collective-permute-done.25
  127.4 1.4 %collective-permute-start.27 = (bf16[8,2048]{1,0:T(8,128)(2,1)S(1)}, bf16[8,2048]{1,0:T(8,128)(2,1)S(1)}, u32[]{:S(2)}, u32[]{:S(2)}) collective-permute-start(bf16[8,2048]{1,0:T(8,128)(2,1)S(1)} %fusion.55), channel_id=1, source_target_pairs={{0,3},{1,0},{2,1},{3,2},{4,7},{5,4},{6,5},{7,6},{8,11},{9,8},{10,9... | collective-permute-start | bytes 98312 | tf_op jit(solution)/shard_map/ppermute | solution.py:20
  128.8 1.4 %collective-permute-start.28 = (bf16[8,2048]{1,0:T(8,128)(2,1)S(1)}, bf16[8,2048]{1,0:T(8,128)(2,1)S(1)}, u32[]{:S(2)}, u32[]{:S(2)}) collective-permute-start(bf16[8,2048]{1,0:T(8,128)(2,1)S(1)} %fusion.55), channel_id=1, source_target_pairs={{0,2},{1,3},{2,0},{3,1},{4,6},{5,7},{6,4},{7,5},{8,10},{9,11},{10,... | collective-permute-start | bytes 98312 | tf_op jit(solution)/shard_map/ppermute | solution.py:20
  130.4 2.3 %collective-permute-done.28 = bf16[8,2048]{1,0:T(8,128)(2,1)S(1)} collective-permute-done((bf16[8,2048]{1,0:T(8,128)(2,1)S(1)}, bf16[8,2048]{1,0:T(8,128)(2,1)S(1)}, u32[]{:S(2)}, u32[]{:S(2)}) %collective-permute-start.28) | collective-permute-done | bytes 32800 | tf_op jit(solution)/shard_map/ppermute | solution.py:20
  132.7 0.8 collective-permute-done.29
  133.6 0.7 constant_dynamic-slice_fusion.1
  (160 shorter events, 12.1 us)
Async XLA Ops:
  0.6 5.2 %copy-start = (bf16[32,2048]{1,0:T(8,128)(2,1)S(1)}, bf16[32,2048]{1,0:T(8,128)(2,1)}, u32[]{:S(2)}) copy-start(bf16[32,2048]{1,0:T(8,128)(2,1)} %param.12) | copy-start | bytes 393220
  5.8 12.1 %copy-start.4 = (s32[32]{0:T(128)S(1)}, s32[32]{0:T(128)}, u32[]{:S(2)}) copy-start(s32[32]{0:T(128)} %param.13) | copy-start | bytes 388
  5.9 12.3 %copy-start.2 = (s32[32,128]{1,0:T(8,128)S(1)}, s32[32,128]{1,0:T(8,128)}, u32[]{:S(2)}) copy-start(s32[32,128]{1,0:T(8,128)} %param.14) | copy-start | bytes 49156
  11.0 8.3 %collective-permute-start = (f32[8,2688]{1,0:T(8,128)S(1)}, f32[8,2688]{1,0:T(8,128)S(1)}, u32[]{:S(2)}, u32[]{:S(2)}) collective-permute-start(f32[8,2688]{1,0:T(8,128)S(1)} %get-tuple-element.13), channel_id=1, source_target_pairs={{0,4},{4,8},{8,12},{12,0},{1,5},{5,9},{9,13},{13,1},{2,6},{6,10},{... | collective-permute-start | bytes 258056 | tf_op jit(solution)/shard_map/ppermute | solution.py:20
  14.0 8.4 %collective-permute-start.1 = (f32[8,2688]{1,0:T(8,128)S(1)}, f32[8,2688]{1,0:T(8,128)S(1)}, u32[]{:S(2)}, u32[]{:S(2)}) collective-permute-start(f32[8,2688]{1,0:T(8,128)S(1)} %get-tuple-element.15), channel_id=1, source_target_pairs={{0,8},{4,12},{8,0},{12,4},{1,9},{5,13},{9,1},{13,5},{2,10},{6,14},... | collective-permute-start | bytes 258056 | tf_op jit(solution)/shard_map/ppermute | solution.py:20
  16.6 6.0 %collective-permute-start.2 = (f32[8,2688]{1,0:T(8,128)S(1)}, f32[8,2688]{1,0:T(8,128)S(1)}, u32[]{:S(2)}, u32[]{:S(2)}) collective-permute-start(f32[8,2688]{1,0:T(8,128)S(1)} %get-tuple-element.14), channel_id=1, source_target_pairs={{0,12},{4,0},{8,4},{12,8},{1,13},{5,1},{9,5},{13,9},{2,14},{6,2},{... | collective-permute-start | bytes 258056 | tf_op jit(solution)/shard_map/ppermute | solution.py:20
  23.0 5.1 %collective-permute-start.3 = (bf16[8,2560]{1,0:T(8,128)(2,1)S(1)}, bf16[8,2560]{1,0:T(8,128)(2,1)S(1)}, u32[]{:S(2)}, u32[]{:S(2)}) collective-permute-start(bf16[8,2560]{1,0:T(8,128)(2,1)S(1)} %pad_maximum_fusion.1), channel_id=1, source_target_pairs={{0,12},{4,0},{8,4},{12,8},{1,13},{5,1},{9,5},{13,9},{2,14},{6,2},{... | collective-permute-start | bytes 122888 | tf_op jit(solution)/shard_map/ppermute | solution.py:20
  26.4 4.9 %collective-permute-start.4 = (bf16[8,2560]{1,0:T(8,128)(2,1)S(1)}, bf16[8,2560]{1,0:T(8,128)(2,1)S(1)}, u32[]{:S(2)}, u32[]{:S(2)}) collective-permute-start(bf16[8,2560]{1,0:T(8,128)(2,1)S(1)} %pad_maximum_fusion.1), channel_id=1, source_target_pairs={{0,8},{4,12},{8,0},{12,4},{1,9},{5,13},{9,1},{13,5},{2,10},{6,14},... | collective-permute-start | bytes 122888 | tf_op jit(solution)/shard_map/ppermute | solution.py:20
  26.7 5.8 %collective-permute-start.5 = (bf16[8,2560]{1,0:T(8,128)(2,1)S(1)}, bf16[8,2560]{1,0:T(8,128)(2,1)S(1)}, u32[]{:S(2)}, u32[]{:S(2)}) collective-permute-start(bf16[8,2560]{1,0:T(8,128)(2,1)S(1)} %pad_maximum_fusion.1), channel_id=1, source_target_pairs={{0,4},{4,8},{8,12},{12,0},{1,5},{5,9},{9,13},{13,1},{2,6},{6,10},{... | collective-permute-start | bytes 122888 | tf_op jit(solution)/shard_map/ppermute | solution.py:20
  41.9 5.8 %collective-permute-start.6 = (bf16[8,2176]{1,0:T(8,128)(2,1)S(1)}, bf16[8,2176]{1,0:T(8,128)(2,1)S(1)}, u32[]{:S(2)}, u32[]{:S(2)}) collective-permute-start(bf16[8,2176]{1,0:T(8,128)(2,1)S(1)} %get-tuple-element.17), channel_id=1, source_target_pairs={{0,4},{4,8},{8,12},{12,0},{1,5},{5,9},{9,13},{13,1},{2,6},{6,10},{... | collective-permute-start | bytes 104456 | tf_op jit(solution)/shard_map/ppermute | solution.py:20
  42.1 5.6 %collective-permute-start.7 = (bf16[8,2176]{1,0:T(8,128)(2,1)S(1)}, bf16[8,2176]{1,0:T(8,128)(2,1)S(1)}, u32[]{:S(2)}, u32[]{:S(2)}) collective-permute-start(bf16[8,2176]{1,0:T(8,128)(2,1)S(1)} %get-tuple-element.18), channel_id=1, source_target_pairs={{0,8},{4,12},{8,0},{12,4},{1,9},{5,13},{9,1},{13,5},{2,10},{6,14},... | collective-permute-start | bytes 104456 | tf_op jit(solution)/shard_map/ppermute | solution.py:20
  43.3 5.2 %collective-permute-start.8 = (bf16[8,2176]{1,0:T(8,128)(2,1)S(1)}, bf16[8,2176]{1,0:T(8,128)(2,1)S(1)}, u32[]{:S(2)}, u32[]{:S(2)}) collective-permute-start(bf16[8,2176]{1,0:T(8,128)(2,1)S(1)} %get-tuple-element.19), channel_id=1, source_target_pairs={{0,12},{4,0},{8,4},{12,8},{1,13},{5,1},{9,5},{13,9},{2,14},{6,2},{... | collective-permute-start | bytes 104456 | tf_op jit(solution)/shard_map/ppermute | solution.py:20
  49.7 5.0 %collective-permute-start.9 = (bf16[8,2048]{1,0:T(8,128)(2,1)S(1)}, bf16[8,2048]{1,0:T(8,128)(2,1)S(1)}, u32[]{:S(2)}, u32[]{:S(2)}) collective-permute-start(bf16[8,2048]{1,0:T(8,128)(2,1)S(1)} %divide_convert_fusion), channel_id=1, source_target_pairs={{0,12},{4,0},{8,4},{12,8},{1,13},{5,1},{9,5},{13,9},{2,14},{6,2},{... | collective-permute-start | bytes 98312 | tf_op jit(solution)/shard_map/ppermute | solution.py:20
  53.0 4.8 %collective-permute-start.10 = (bf16[8,2048]{1,0:T(8,128)(2,1)S(1)}, bf16[8,2048]{1,0:T(8,128)(2,1)S(1)}, u32[]{:S(2)}, u32[]{:S(2)}) collective-permute-start(bf16[8,2048]{1,0:T(8,128)(2,1)S(1)} %divide_convert_fusion), channel_id=1, source_target_pairs={{0,8},{4,12},{8,0},{12,4},{1,9},{5,13},{9,1},{13,5},{2,10},{6,14},... | collective-permute-start | bytes 98312 | tf_op jit(solution)/shard_map/ppermute | solution.py:20
  53.2 5.7 %collective-permute-start.11 = (bf16[8,2048]{1,0:T(8,128)(2,1)S(1)}, bf16[8,2048]{1,0:T(8,128)(2,1)S(1)}, u32[]{:S(2)}, u32[]{:S(2)}) collective-permute-start(bf16[8,2048]{1,0:T(8,128)(2,1)S(1)} %divide_convert_fusion), channel_id=1, source_target_pairs={{0,4},{4,8},{8,12},{12,0},{1,5},{5,9},{9,13},{13,1},{2,6},{6,10},{... | collective-permute-start | bytes 98312 | tf_op jit(solution)/shard_map/ppermute | solution.py:20
  59.0 5.0 %copy-start.1 = (bf16[32,2048]{1,0:T(8,128)(2,1)}, bf16[32,2048]{1,0:T(8,128)(2,1)S(1)}, u32[]{:S(2)}) copy-start(bf16[32,2048]{1,0:T(8,128)(2,1)S(1)} %constant_dynamic-slice_fusion) | copy-start | bytes 393220
  59.0 11.5 %copy-start.3 = (bf16[2048]{0:T(1024)(128)(2,1)S(1)}, bf16[2048]{0:T(1024)(128)(2,1)}, u32[]{:S(2)}) copy-start(bf16[2048]{0:T(1024)(128)(2,1)} %param.21) | copy-start | bytes 12292
  64.0 3.4 %collective-permute-start.12 = (bf16[8,2048]{1,0:T(8,128)(2,1)S(1)}, bf16[8,2048]{1,0:T(8,128)(2,1)S(1)}, u32[]{:S(2)}, u32[]{:S(2)}) collective-permute-start(bf16[8,2048]{1,0:T(8,128)(2,1)S(1)} %get-tuple-element.23), channel_id=1, source_target_pairs={{0,1},{1,2},{2,3},{3,0},{4,5},{5,6},{6,7},{7,4},{8,9},{9,10},{10,1... | collective-permute-start | bytes 98312 | tf_op jit(solution)/shard_map/ppermute | solution.py:20
  64.1 4.0 %collective-permute-start.13 = (bf16[8,2048]{1,0:T(8,128)(2,1)S(1)}, bf16[8,2048]{1,0:T(8,128)(2,1)S(1)}, u32[]{:S(2)}, u32[]{:S(2)}) collective-permute-start(bf16[8,2048]{1,0:T(8,128)(2,1)S(1)} %get-tuple-element.25), channel_id=1, source_target_pairs={{0,2},{1,3},{2,0},{3,1},{4,6},{5,7},{6,4},{7,5},{8,10},{9,11},{10,... | collective-permute-start | bytes 98312 | tf_op jit(solution)/shard_map/ppermute | solution.py:20
  65.7 3.0 %collective-permute-start.14 = (bf16[8,2048]{1,0:T(8,128)(2,1)S(1)}, bf16[8,2048]{1,0:T(8,128)(2,1)S(1)}, u32[]{:S(2)}, u32[]{:S(2)}) collective-permute-start(bf16[8,2048]{1,0:T(8,128)(2,1)S(1)} %get-tuple-element.24), channel_id=1, source_target_pairs={{0,3},{1,0},{2,1},{3,2},{4,7},{5,4},{6,5},{7,6},{8,11},{9,8},{10,9... | collective-permute-start | bytes 98312 | tf_op jit(solution)/shard_map/ppermute | solution.py:20
  68.7 3.4 %collective-permute-start.15 = (bf16[8,2048]{1,0:T(8,128)(2,1)S(1)}, bf16[8,2048]{1,0:T(8,128)(2,1)S(1)}, u32[]{:S(2)}, u32[]{:S(2)}) collective-permute-start(bf16[8,2048]{1,0:T(8,128)(2,1)S(1)} %fusion.59), channel_id=1, source_target_pairs={{0,3},{1,0},{2,1},{3,2},{4,7},{5,4},{6,5},{7,6},{8,11},{9,8},{10,9... | collective-permute-start | bytes 98312 | tf_op jit(solution)/shard_map/ppermute | solution.py:20
  70.5 4.2 %collective-permute-start.16 = (bf16[8,2048]{1,0:T(8,128)(2,1)S(1)}, bf16[8,2048]{1,0:T(8,128)(2,1)S(1)}, u32[]{:S(2)}, u32[]{:S(2)}) collective-permute-start(bf16[8,2048]{1,0:T(8,128)(2,1)S(1)} %fusion.59), channel_id=1, source_target_pairs={{0,2},{1,3},{2,0},{3,1},{4,6},{5,7},{6,4},{7,5},{8,10},{9,11},{10,... | collective-permute-start | bytes 98312 | tf_op jit(solution)/shard_map/ppermute | solution.py:20
  71.0 3.7 %collective-permute-start.17 = (bf16[8,2048]{1,0:T(8,128)(2,1)S(1)}, bf16[8,2048]{1,0:T(8,128)(2,1)S(1)}, u32[]{:S(2)}, u32[]{:S(2)}) collective-permute-start(bf16[8,2048]{1,0:T(8,128)(2,1)S(1)} %fusion.59), channel_id=1, source_target_pairs={{0,1},{1,2},{2,3},{3,0},{4,5},{5,6},{6,7},{7,4},{8,9},{9,10},{10,1... | collective-permute-start | bytes 98312 | tf_op jit(solution)/shard_map/ppermute | solution.py:20
  93.9 8.1 %collective-permute-start.18 = (bf16[8,7424]{1,0:T(8,128)(2,1)S(1)}, bf16[8,7424]{1,0:T(8,128)(2,1)S(1)}, u32[]{:S(2)}, u32[]{:S(2)}) collective-permute-start(bf16[8,7424]{1,0:T(8,128)(2,1)S(1)} %get-tuple-element.10), channel_id=1, source_target_pairs={{0,4},{4,8},{8,12},{12,0},{1,5},{5,9},{9,13},{13,1},{2,6},{6,10},{... | collective-permute-start | bytes 356360 | tf_op jit(solution)/shard_map/ppermute | solution.py:20
  94.0 11.1 %collective-permute-start.19 = (bf16[8,7424]{1,0:T(8,128)(2,1)S(1)}, bf16[8,7424]{1,0:T(8,128)(2,1)S(1)}, u32[]{:S(2)}, u32[]{:S(2)}) collective-permute-start(bf16[8,7424]{1,0:T(8,128)(2,1)S(1)} %get-tuple-element.12), channel_id=1, source_target_pairs={{0,8},{4,12},{8,0},{12,4},{1,9},{5,13},{9,1},{13,5},{2,10},{6,14},... | collective-permute-start | bytes 356360 | tf_op jit(solution)/shard_map/ppermute | solution.py:20
  95.0 10.1 %collective-permute-start.20 = (bf16[8,7424]{1,0:T(8,128)(2,1)S(1)}, bf16[8,7424]{1,0:T(8,128)(2,1)S(1)}, u32[]{:S(2)}, u32[]{:S(2)}) collective-permute-start(bf16[8,7424]{1,0:T(8,128)(2,1)S(1)} %get-tuple-element.11), channel_id=1, source_target_pairs={{0,12},{4,0},{8,4},{12,8},{1,13},{5,1},{9,5},{13,9},{2,14},{6,2},{... | collective-permute-start | bytes 356360 | tf_op jit(solution)/shard_map/ppermute | solution.py:20
  105.5 4.5 %collective-permute-start.21 = (bf16[8,3584]{1,0:T(8,128)(2,1)S(1)}, bf16[8,3584]{1,0:T(8,128)(2,1)S(1)}, u32[]{:S(2)}, u32[]{:S(2)}) collective-permute-start(bf16[8,3584]{1,0:T(8,128)(2,1)S(1)} %fusion.45), channel_id=1, source_target_pairs={{0,12},{4,0},{8,4},{12,8},{1,13},{5,1},{9,5},{13,9},{2,14},{6,2},{... | collective-permute-start | bytes 172040 | tf_op jit(solution)/shard_map/ppermute | solution.py:20
  108.1 5.7 %collective-permute-start.22 = (bf16[8,3584]{1,0:T(8,128)(2,1)S(1)}, bf16[8,3584]{1,0:T(8,128)(2,1)S(1)}, u32[]{:S(2)}, u32[]{:S(2)}) collective-permute-start(bf16[8,3584]{1,0:T(8,128)(2,1)S(1)} %fusion.45), channel_id=1, source_target_pairs={{0,8},{4,12},{8,0},{12,4},{1,9},{5,13},{9,1},{13,5},{2,10},{6,14},... | collective-permute-start | bytes 172040 | tf_op jit(solution)/shard_map/ppermute | solution.py:20
  109.1 6.0 %collective-permute-start.23 = (bf16[8,3584]{1,0:T(8,128)(2,1)S(1)}, bf16[8,3584]{1,0:T(8,128)(2,1)S(1)}, u32[]{:S(2)}, u32[]{:S(2)}) collective-permute-start(bf16[8,3584]{1,0:T(8,128)(2,1)S(1)} %fusion.45), channel_id=1, source_target_pairs={{0,4},{4,8},{8,12},{12,0},{1,5},{5,9},{9,13},{13,1},{2,6},{6,10},{... | collective-permute-start | bytes 172040 | tf_op jit(solution)/shard_map/ppermute | solution.py:20
  123.3 3.4 %collective-permute-start.24 = (bf16[8,2048]{1,0:T(8,128)(2,1)S(1)}, bf16[8,2048]{1,0:T(8,128)(2,1)S(1)}, u32[]{:S(2)}, u32[]{:S(2)}) collective-permute-start(bf16[8,2048]{1,0:T(8,128)(2,1)S(1)} %get-tuple-element.20), channel_id=1, source_target_pairs={{0,1},{1,2},{2,3},{3,0},{4,5},{5,6},{6,7},{7,4},{8,9},{9,10},{10,1... | collective-permute-start | bytes 98312 | tf_op jit(solution)/shard_map/ppermute | solution.py:20
  123.3 4.0 %collective-permute-start.25 = (bf16[8,2048]{1,0:T(8,128)(2,1)S(1)}, bf16[8,2048]{1,0:T(8,128)(2,1)S(1)}, u32[]{:S(2)}, u32[]{:S(2)}) collective-permute-start(bf16[8,2048]{1,0:T(8,128)(2,1)S(1)} %get-tuple-element.22), channel_id=1, source_target_pairs={{0,2},{1,3},{2,0},{3,1},{4,6},{5,7},{6,4},{7,5},{8,10},{9,11},{10,... | collective-permute-start | bytes 98312 | tf_op jit(solution)/shard_map/ppermute | solution.py:20
  124.0 3.3 %collective-permute-start.26 = (bf16[8,2048]{1,0:T(8,128)(2,1)S(1)}, bf16[8,2048]{1,0:T(8,128)(2,1)S(1)}, u32[]{:S(2)}, u32[]{:S(2)}) collective-permute-start(bf16[8,2048]{1,0:T(8,128)(2,1)S(1)} %get-tuple-element.21), channel_id=1, source_target_pairs={{0,3},{1,0},{2,1},{3,2},{4,7},{5,4},{6,5},{7,6},{8,11},{9,8},{10,9... | collective-permute-start | bytes 98312 | tf_op jit(solution)/shard_map/ppermute | solution.py:20
  127.4 3.0 %collective-permute-start.27 = (bf16[8,2048]{1,0:T(8,128)(2,1)S(1)}, bf16[8,2048]{1,0:T(8,128)(2,1)S(1)}, u32[]{:S(2)}, u32[]{:S(2)}) collective-permute-start(bf16[8,2048]{1,0:T(8,128)(2,1)S(1)} %fusion.55), channel_id=1, source_target_pairs={{0,3},{1,0},{2,1},{3,2},{4,7},{5,4},{6,5},{7,6},{8,11},{9,8},{10,9... | collective-permute-start | bytes 98312 | tf_op jit(solution)/shard_map/ppermute | solution.py:20
  128.8 3.9 %collective-permute-start.28 = (bf16[8,2048]{1,0:T(8,128)(2,1)S(1)}, bf16[8,2048]{1,0:T(8,128)(2,1)S(1)}, u32[]{:S(2)}, u32[]{:S(2)}) collective-permute-start(bf16[8,2048]{1,0:T(8,128)(2,1)S(1)} %fusion.55), channel_id=1, source_target_pairs={{0,2},{1,3},{2,0},{3,1},{4,6},{5,7},{6,4},{7,5},{8,10},{9,11},{10,... | collective-permute-start | bytes 98312 | tf_op jit(solution)/shard_map/ppermute | solution.py:20
  130.2 3.3 %collective-permute-start.29 = (bf16[8,2048]{1,0:T(8,128)(2,1)S(1)}, bf16[8,2048]{1,0:T(8,128)(2,1)S(1)}, u32[]{:S(2)}, u32[]{:S(2)}) collective-permute-start(bf16[8,2048]{1,0:T(8,128)(2,1)S(1)} %fusion.55), channel_id=1, source_target_pairs={{0,1},{1,2},{2,3},{3,0},{4,5},{5,6},{6,7},{7,4},{8,9},{9,10},{10,1... | collective-permute-start | bytes 98312 | tf_op jit(solution)/shard_map/ppermute | solution.py:20

commit v2 on v1

--- a/solution.py
+++ b/solution.py
@@ -3,6 +3,8 @@
 import jax
 import jax.numpy as jnp
 from jax import lax
+from jax.experimental import pallas as pl
+from jax.experimental.pallas import tpu as pltpu
 from jax.sharding import PartitionSpec as P
 
 D = 8192
@@ -50,6 +52,249 @@
     for part in scatter_parts(to_bf16(x), axis, n):
         own = own + part.astype(jnp.float32)
     return own
+
+
+VMEM = pltpu.VMEM
+LIMIT = 12 << 20
+SMALL = 2 << 20
+GATE_LIMIT = 24 << 20
+HIDE = (0.0, 0.0, 0.0, 0.0, 0.0, 0.0)
+CUT = (6, 5)
+
+
+def whole(count):
+    return [pl.BlockSpec(memory_space=VMEM)] * count
+
+
+def cost(hidden_us=0.0, weight=None, rows=32):
+    size = 0 if weight is None else weight.size
+    return pl.CostEstimate(
+        flops=2 * rows * size,
+        bytes_accessed=int(2 * size + hidden_us * 3e6),
+        transcendentals=0,
+    )
+
+
+def place(parts, held, n_mem):
+    me = lax.axis_index("mem")
+    rows = parts[0].shape[0]
+    for step, part in enumerate(parts):
+        at = pl.multiple_of(lax.rem(me - step + n_mem, n_mem) * rows, rows)
+        held[pl.ds(at, rows), :] = part[...].astype(jnp.float32)
+
+
+def fetch(weight, start, count, after):
+    pieces = 4
+    step = count // pieces
+
+    def kernel(after_ref, w_ref, out, sems):
+        copies = [
+            pltpu.make_async_copy(
+                w_ref.at[pl.ds(start + i * step, step)], out.at[pl.ds(i * step, step)], sems.at[i]
+            )
+            for i in range(pieces)
+        ]
+        for copy in copies:
+            copy.start()
+        for copy in copies:
+            copy.wait()
+
+    return pl.pallas_call(
+        kernel,
+        in_specs=[pl.BlockSpec(memory_space=pl.ANY)] * 2,
+        out_specs=pl.BlockSpec(memory_space=VMEM),
+        out_shape=jax.ShapeDtypeStruct((count,) + weight.shape[1:], weight.dtype),
+        scratch_shapes=[pltpu.SemaphoreType.DMA((pieces,))],
+        compiler_params=pltpu.CompilerParams(vmem_limit_bytes=26 << 20),
+        cost_estimate=pl.CostEstimate(
+            flops=700 * count * math.prod(weight.shape[1:]),
+            bytes_accessed=0,
+            transcendentals=0,
+        ),
+    )(after, weight)
+
+
+def tiled_dot(x, w_ref, out_ref, tile):
+    @pl.loop(0, w_ref.shape[-1] // tile)
+    def _(i):
+        cols = pl.ds(pl.multiple_of(i * tile, tile), tile)
+        out_ref[:, cols] = jnp.dot(
+            x, w_ref[:, cols], preferred_element_type=jnp.float32
+        ).astype(out_ref.dtype)
+
+
+def gathered_dot(parts, weight, n_mem, keep, hidden_us):
+    rows = parts[0].shape[0] * n_mem
+    depth, width = weight.shape
+    tile = 512 if width % 512 == 0 else 128
+
+    def kernel(*refs):
+        part_refs, w_ref = refs[:n_mem], refs[n_mem]
+        outs, held = refs[n_mem + 1 : -1], refs[-1]
+        place(part_refs, held, n_mem)
+        x = to_bf16(held[...])
+        if keep:
+            outs[1][...] = x
+        tiled_dot(x, w_ref, outs[0], tile)
+
+    shapes = [jax.ShapeDtypeStruct((rows, width), jnp.bfloat16)]
+    if keep:
+        shapes.append(jax.ShapeDtypeStruct((rows, depth), jnp.bfloat16))
+    return pl.pallas_call(
+        kernel,
+        in_specs=whole(n_mem + 1),
+        out_specs=whole(len(shapes)),
+        out_shape=shapes,
+        scratch_shapes=[VMEM((rows, depth), jnp.float32)],
+        compiler_params=pltpu.CompilerParams(vmem_limit_bytes=LIMIT),
+        cost_estimate=cost(hidden_us, weight),
+    )(*parts, weight)
+
+
+def gate_up_parts(hidden, near, far, gain, held, weight, n_mem, hidden_us):
+    req, depth = hidden.shape
+    ff = weight.shape[2]
+    rows = req // n_mem
+    tile = 512 if ff % 512 == 0 else 128
+
+    n_held = len(held)
+    first = sum(h.shape[0] for h in held)
+    rest = depth - first
+    chunk = 128
+
+    def kernel(hid_ref, near_ref, far_ref, gain_ref, *refs):
+        held_refs, w_ref, mid_ref = refs[:n_held], refs[n_held], refs[n_held + 1]
+        outs, (spread, acc, power, tail, sems) = (
+            refs[n_held + 2 : n_held + 2 + n_mem],
+            refs[n_held + 2 + n_mem :],
+        )
+        copies = [
+            pltpu.make_async_copy(
+                w_ref.at[pl.ds(first + i * chunk, chunk)],
+                tail.at[pl.ds(i * chunk, chunk)],
+                sems.at[i],
+            )
+            for i in range(rest // chunk)
+        ]
+        for copy in copies:
+            copy.start()
+        total = near_ref[...].astype(jnp.float32) + far_ref[...].astype(jnp.float32)
+        middle = to_bf16(hid_ref[...].astype(jnp.float32) + total)
+        mid_ref[...] = middle
+        wide = middle.astype(jnp.float32)
+        power[...] = jnp.broadcast_to(jnp.sum(wide * wide, 1, keepdims=True), power.shape)
+        normed = to_bf16(wide * gain_ref[...].astype(jnp.float32))
+        row = lax.broadcasted_iota(jnp.int32, (128, 256), 0)
+        col = lax.broadcasted_iota(jnp.int32, (128, 256), 1)
+        even = jnp.where(col == 2 * row, 1.0, 0.0).astype(jnp.bfloat16)
+        odd = jnp.where(col == 2 * row + 1, 1.0, 0.0).astype(jnp.bfloat16)
+        for b in range(depth // 128):
+            block = normed[:, b * 128 : (b + 1) * 128]
+            for half, pick in enumerate((even, odd)):
+                spread[half * req : (half + 1) * req, b * 256 : (b + 1) * 256] = to_bf16(
+                    jnp.dot(block, pick, preferred_element_type=jnp.float32)
+                )
+
+        def add_rows(block, at, count, fresh):
+            @pl.loop(0, ff // tile)
+            def _(i):
+                cols = pl.ds(pl.multiple_of(i * tile, tile), tile)
+                term = jnp.dot(
+                    spread[:, 2 * at : 2 * (at + count)],
+                    block[:, :, cols].reshape(2 * count, tile),
+                    preferred_element_type=jnp.float32,
+                )
+                acc[:, cols] = term if fresh else acc[:, cols] + term
+
+        at = 0
+        for ref in held_refs:
+            add_rows(ref, at, ref.shape[0], at == 0)
+            at += ref.shape[0]
+        for copy in copies:
+            copy.wait()
+        if rest:
+            add_rows(tail, first, rest, first == 0)
+
+        me = lax.axis_index("mem")
+        for step in range(n_mem):
+            at = pl.multiple_of(lax.rem(me + step, n_mem) * rows, rows)
+            out = outs[step]
+            gate = acc[pl.ds(at, rows), :]
+            up = acc[pl.ds(at + req, rows), :]
+            out[:, :ff] = to_bf16(jnp.concatenate([gate, up], 0))
+            pw = power[pl.ds(at, rows), :]
+            hi = to_bf16(pw).astype(jnp.float32)
+            out[:, ff:] = to_bf16(jnp.concatenate([hi, pw - hi], 0))
+
+    return pl.pallas_call(
+        kernel,
+        in_specs=whole(4 + n_held) + [pl.BlockSpec(memory_space=pl.ANY)],
+        out_specs=whole(n_mem + 1),
+        out_shape=[jax.ShapeDtypeStruct((req, depth), jnp.bfloat16)]
+        + [jax.ShapeDtypeStruct((2 * rows, ff + 128), jnp.bfloat16)] * n_mem,
+        scratch_shapes=[
+            VMEM((2 * req, 2 * depth), jnp.bfloat16),
+            VMEM((2 * req, ff), jnp.float32),
+            VMEM((req, 128), jnp.float32),
+            VMEM((max(rest, chunk), 2, ff), jnp.bfloat16),
+            pltpu.SemaphoreType.DMA((max(rest // chunk, 1),)),
+        ],
+        compiler_params=pltpu.CompilerParams(vmem_limit_bytes=GATE_LIMIT),
+        cost_estimate=cost(hidden_us, weight, 64),
+    )(hidden, near, far, gain.reshape(1, -1), *held, weight)
+
+
+def activate(parts, hidden_us):
+    rows = parts[0].shape[0] // 2
+    ff = parts[0].shape[1] - 128
+
+    def kernel(*refs):
+        out = refs[-1]
+        total = refs[0][...].astype(jnp.float32)
+        for ref in refs[1:-1]:
+            total = total + ref[...].astype(jnp.float32)
+        power = total[:rows, ff : ff + 1] + total[rows:, ff : ff + 1]
+        scale = lax.rsqrt(power / D + NORM_EPS)
+        gate = total[:rows, :ff] * scale
+        up = total[rows:, :ff] * scale
+        out[...] = to_bf16(gate / (1.0 + jnp.exp(-gate)) * up)
+
+    return pl.pallas_call(
+        kernel,
+        in_specs=whole(len(parts)),
+        out_specs=pl.BlockSpec(memory_space=VMEM),
+        out_shape=jax.ShapeDtypeStruct((rows, ff), jnp.bfloat16),
+        compiler_params=pltpu.CompilerParams(vmem_limit_bytes=LIMIT),
+        cost_estimate=cost(hidden_us),
+    )(*parts)
+
+
+def around(x, axis, n):
+    return [x] + [shifted(x, axis, n, step) for step in range(1, n)]
+
+
+def added(left, right, hidden_us):
+    def kernel(l_ref, r_ref, out):
+        out[...] = to_bf16(l_ref[...].astype(jnp.float32) + r_ref[...].astype(jnp.float32))
+
+    return pl.pallas_call(
+        kernel,
+        in_specs=whole(2),
+        out_specs=pl.BlockSpec(memory_space=VMEM),
+        out_shape=jax.ShapeDtypeStruct(left.shape, left.dtype),
+        compiler_params=pltpu.CompilerParams(vmem_limit_bytes=LIMIT),
+        cost_estimate=cost(hidden_us),
+    )(left, right)
+
+
+def pairwise(x, n, hidden_us):
+    near, step = x, 1
+    while True:
+        far = lax.ppermute(near, "comp", [(i, i ^ step) for i in range(n)])
+        step *= 2
+        if step >= n:
+            return near, far
+        near = added(near, far, hidden_us)
 
 
 def rotary(positions, head_dim):
@@ -216,39 +461,64 @@
             denom = denom + t * f
             numer = numer + w * f[..., None]
         attended_own = to_bf16(numer / denom[..., None]).reshape(rows, -1)
-        attended = gather_parts(attended_own, "mem", n_mem)
-
-        comp_pos = lax.axis_index("comp")
-        rows_c = req_count // n_comp
-        attn_proj = jnp.dot(attended, w_out, preferred_element_type=jnp.float32)
-        resid_own = lax.dynamic_slice_in_dim(hidden_in, comp_pos * rows_c, rows_c, 0)
-        middle_own = to_bf16(resid_own.astype(jnp.float32) + summed(attn_proj, "comp", n_comp))
-        middle = gather_parts(middle_own, "comp", n_comp)
-        middle_wide = middle.astype(jnp.float32)
-        normed_ffn = to_bf16(middle_wide * ffn_gain.astype(jnp.float32))
-        gate_up = jnp.einsum(
-            "rd,dtf->rtf", normed_ffn, w_gate_up, preferred_element_type=jnp.float32
-        ).reshape(req_count, -1)
-        m_hi, m_lo = split_hi_lo(jnp.sum(middle_wide * middle_wide, 1))
-        wide = jnp.concatenate(
-            [
-                to_bf16(gate_up),
-                jnp.broadcast_to(m_hi[:, None], (req_count, 128)),
-                jnp.broadcast_to(m_lo[:, None], (req_count, 128)),
-            ],
-            1,
-        ).reshape(n_mem, rows, -1)
-        total = lax.dynamic_index_in_dim(wide, mem_pos, 0, False).astype(jnp.float32)
-        for part in scatter_parts(wide, "mem", n_mem):
-            total = total + part.astype(jnp.float32)
-        ff = w_gate_up.shape[2]
-        ffn_scale = lax.rsqrt((total[:, 2 * ff] + total[:, 2 * ff + 128]) / D + NORM_EPS)
-        gate = total[:, :ff] * ffn_scale[:, None]
-        up = total[:, ff : 2 * ff] * ffn_scale[:, None]
-        activated = gather_parts(to_bf16(jax.nn.silu(gate) * up), "mem", n_mem)
-        down_part = jnp.dot(activated, w_down, preferred_element_type=jnp.float32)
-        updated_own = to_bf16(middle_own.astype(jnp.float32) + summed(down_part, "comp", n_comp))
-        updated = gather_parts(updated_own, "comp", n_comp)
+        if rows % 8:
+            attended = gather_parts(attended_own, "mem", n_mem)
+
+            comp_pos = lax.axis_index("comp")
+            rows_c = req_count // n_comp
+            attn_proj = jnp.dot(attended, w_out, preferred_element_type=jnp.float32)
+            resid_own = lax.dynamic_slice_in_dim(hidden_in, comp_pos * rows_c, rows_c, 0)
+            middle_own = to_bf16(resid_own.astype(jnp.float32) + summed(attn_proj, "comp", n_comp))
+            middle = gather_parts(middle_own, "comp", n_comp)
+            middle_wide = middle.astype(jnp.float32)
+            normed_ffn = to_bf16(middle_wide * ffn_gain.astype(jnp.float32))
+            gate_up = jnp.einsum(
+                "rd,dtf->rtf", normed_ffn, w_gate_up, preferred_element_type=jnp.float32
+            ).reshape(req_count, -1)
+            m_hi, m_lo = split_hi_lo(jnp.sum(middle_wide * middle_wide, 1))
+            wide = jnp.concatenate(
+                [
+                    to_bf16(gate_up),
+                    jnp.broadcast_to(m_hi[:, None], (req_count, 128)),
+                    jnp.broadcast_to(m_lo[:, None], (req_count, 128)),
+                ],
+                1,
+            ).reshape(n_mem, rows, -1)
+            total = lax.dynamic_index_in_dim(wide, mem_pos, 0, False).astype(jnp.float32)
+            for part in scatter_parts(wide, "mem", n_mem):
+                total = total + part.astype(jnp.float32)
+            ff = w_gate_up.shape[2]
+            ffn_scale = lax.rsqrt((total[:, 2 * ff] + total[:, 2 * ff + 128]) / D + NORM_EPS)
+            gate = total[:, :ff] * ffn_scale[:, None]
+            up = total[:, ff : 2 * ff] * ffn_scale[:, None]
+            activated = gather_parts(to_bf16(jax.nn.silu(gate) * up), "mem", n_mem)
+            down_part = jnp.dot(activated, w_down, preferred_element_type=jnp.float32)
+            updated_own = to_bf16(middle_own.astype(jnp.float32) + summed(down_part, "comp", n_comp))
+            updated = gather_parts(updated_own, "comp", n_comp)
+            return (attended, updated)
+
+        depth = w_gate_up.shape[0]
+        cut_a, cut_b = depth * CUT[0] // 16, depth * CUT[1] // 16
+        out_held = fetch(w_out, 0, w_out.shape[0], own_qkv)
+        gate_a = fetch(w_gate_up, 0, cut_a, attended_own)
+        proj, attended = gathered_dot(
+            around(attended_own, "mem", n_mem), out_held, n_mem, True, HIDE[2]
+        )
+        near, far = pairwise(proj, n_comp, HIDE[3])
+        gate_b = fetch(w_gate_up, cut_a, cut_b, near)
+        middle, *terms = gate_up_parts(
+            hidden_in, near, far, ffn_gain, (gate_a, gate_b), w_gate_up, n_mem, HIDE[3]
+        )
+        down_held = fetch(w_down, 0, w_down.shape[0], terms[0])
+        terms = terms[:1] + [shifted(t, "mem", n_mem, s) for s, t in enumerate(terms) if s]
+        activated = activate(terms, HIDE[4])
+        (down,) = gathered_dot(
+            around(activated, "mem", n_mem), down_held, n_mem, False, HIDE[5]
+        )
+        near, far = pairwise(down, n_comp, 0.0)
+        updated = to_bf16(
+            middle.astype(jnp.float32) + (near.astype(jnp.float32) + far.astype(jnp.float32))
+        )
         return (attended, updated)
 
     return shards

time: 135 us -> 112 us (0.83)
  matrix products: 45.2 us -> 13.7 us
  Pallas kernels: 0 us -> 28 us
  waiting for transfers between devices: 39.7 us -> 26.7 us
  starting transfers between devices: 37 us -> 29.5 us
  local copies, waits for them, and re-layouts: 5.98 us -> 7.47 us
    dot_general x3 -> x0, matrix products: 30.7 us -> none  [the longest x1 17.9 us: shards(): jnp.einsum('rd,dtf->rtf', normed_ffn, w_gate_up, preferred_element_type=j...]
    pallas_call x0 -> x10, Pallas kernels: none -> 28 us  [the longest x4 13.8 us: fetch(): pl.pallas_call(kernel, in_specs=[pl.BlockSpec(memory_space=pl.ANY)] * 2,...]
    ppermute x30 -> x18, waiting for transfers between devices: 39.7 us -> 20.6 us  [shifted(): return lax.ppermute(x, axis, [(i, (i + step) % n) for i in range(n)])]
    ppermute x30 -> x18, starting transfers between devices: 37 us -> 26.4 us  [shifted(): return lax.ppermute(x, axis, [(i, (i + step) % n) for i in range(n)])]
    ppermute x0 -> x4, waiting for transfers between devices: none -> 6.09 us  [pairwise(): far = lax.ppermute(near, 'comp', [(i, i ^ step) for i in range(n)])]
    unnamed x46 -> x19, local copies, waits for them, and re-layouts: 2.32 us -> 5.58 us
    ppermute x0 -> x4, starting transfers between devices: none -> 3.13 us  [pairwise(): far = lax.ppermute(near, 'comp', [(i, i ^ step) for i in range(n)])]
  transfers between devices with their start and end apart: 30 -> 22, of which waited for: 25 -> 14; matrix products, arithmetic and copies ran while one was open for 1% -> 2% of each run, Pallas kernels for 0% -> 12%
where the time goes in v2:
time: 112 us
  starting transfers between devices  29.5 us (26%)
  Pallas kernels  28 us (25%)
  waiting for transfers between devices  26.7 us (24%)
  matrix products  13.7 us (12%)
  local copies, waits for them, and re-layouts  7.47 us (7%)
  other arithmetic  5.03 us (4%)
  between operations  1.16 us (1%)
    ppermute x18, starting transfers between devices, shifted(): return lax.ppermute(x, axis, [(i, (i + step) % n) for i in range(n)])  26.4 us
    ppermute x18, waiting for transfers between devices, shifted(): return lax.ppermute(x, axis, [(i, (i + step) % n) for i in range(n)])  20.6 us
    pallas_call x4, Pallas kernels, fetch(): pl.pallas_call(kernel, in_specs=[pl.BlockSpec(memory_space=pl.ANY)] * 2,...  13.8 us
    pallas_call x1, Pallas kernels, gate_up_parts(): pl.pallas_call(kernel, in_specs=whole(4 + n_held) + [pl.BlockSpec(memory_...  8.82 us
    ppermute x4, waiting for transfers between devices, pairwise(): far = lax.ppermute(near, 'comp', [(i, i ^ step) for i in range(n)])  6.09 us
    unnamed x19, local copies, waits for them, and re-layouts  5.58 us
    pallas_call x2, Pallas kernels, gathered_dot(): pl.pallas_call(kernel, in_specs=whole(n_mem + 1), out_specs=whole(len(sha...  5.14 us
    dot_general x1, matrix products, shards(): query_part = jnp.dot(normed, w_query, preferred_element_type=jnp.float32)  5.06 us
  transfers between devices with their start and end apart: 22, of which 14 were waited for; matrix products, arithmetic and copies ran while one was open for 2% of the time, Pallas kernels for 12%

profile of v2, /device:TPU:0, one launch (start us, length us, event | category | flops | bytes accessed | tf_op | source)
XLA Modules:
  0.0 111.6 jit_solution(2634740814284347478)
XLA Ops:
  0.7 1.0 fusion.28
  1.7 0.7 convert_element_type.68
  2.4 2.0 %copy.186 = bf16[256,8,2,256]{3,1,2,0:T(8,128)(2,1)S(1)} copy(bf16[256,8,2,256]{3,2,1,0:T(2,128)(2,1)} %bitcast.178) | data formatting | bytes 4194304
  4.5 5.1 %fusion.32 = f32[32,2048]{1,0:T(8,128)S(1)} fusion(bf16[2048,2048]{1,0:T(8,128)(2,1)} %param.18, bf16[32,2048]{1,0:T(8,128)(2,1)} %hid_ref.1, f32[2048]{0:T(1024)S(1)} %convert_element_type.68), kind=kOutput, calls=%fused_computation.38 | convolution fusion | flops 268632064 | bytes 8790016 | tf_op jit(solution)/shard_map/dot_general | solution.py:365
  9.6 0.5 fusion.30
  10.2 3.1 %collective-permute-start = (f32[8,2688]{1,0:T(8,128)S(1)}, f32[8,2688]{1,0:T(8,128)S(1)}, u32[]{:S(2)}, u32[]{:S(2)}) collective-permute-start(f32[8,2688]{1,0:T(8,128)S(1)} %get-tuple-element.24), channel_id=1, source_target_pairs={{0,4},{4,8},{8,12},{12,0},{1,5},{5,9},{9,13},{13,1},{2,6},{6,10},{... | collective-permute-start | bytes 258056 | tf_op jit(solution)/shard_map/ppermute | solution.py:22
  13.3 2.1 %collective-permute-start.2 = (f32[8,2688]{1,0:T(8,128)S(1)}, f32[8,2688]{1,0:T(8,128)S(1)}, u32[]{:S(2)}, u32[]{:S(2)}) collective-permute-start(f32[8,2688]{1,0:T(8,128)S(1)} %get-tuple-element.25), channel_id=1, source_target_pairs={{0,12},{4,0},{8,4},{12,8},{1,13},{5,1},{9,5},{13,9},{2,14},{6,2},{... | collective-permute-start | bytes 258056 | tf_op jit(solution)/shard_map/ppermute | solution.py:22
  15.3 0.9 collective-permute-start.1
  16.5 0.6 fusion.20
  17.6 0.6 collective-permute-done
  18.2 0.8 collective-permute-done.2
  19.1 4.2 %collective-permute-done.1 = f32[8,2688]{1,0:T(8,128)S(1)} collective-permute-done((f32[8,2688]{1,0:T(8,128)S(1)}, f32[8,2688]{1,0:T(8,128)S(1)}, u32[]{:S(2)}, u32[]{:S(2)}) %collective-permute-start.1) | collective-permute-done | bytes 86048 | tf_op jit(solution)/shard_map/ppermute | solution.py:22
  23.9 2.4 %collective-permute-start.4 = (bf16[8,2560]{1,0:T(8,128)(2,1)S(1)}, bf16[8,2560]{1,0:T(8,128)(2,1)S(1)}, u32[]{:S(2)}, u32[]{:S(2)}) collective-permute-start(bf16[8,2560]{1,0:T(8,128)(2,1)S(1)} %pad_maximum_fusion.after_ref), channel_id=1, source_target_pairs={{0,8},{4,12},{8,0},{12,4},{1,9},{5,13},{9,1},{13,5},{2,10},{6,14},... | collective-permute-start | bytes 122888 | tf_op jit(solution)/shard_map/ppermute | solution.py:22
  26.3 1.4 %collective-permute-start.3 = (bf16[8,2560]{1,0:T(8,128)(2,1)S(1)}, bf16[8,2560]{1,0:T(8,128)(2,1)S(1)}, u32[]{:S(2)}, u32[]{:S(2)}) collective-permute-start(bf16[8,2560]{1,0:T(8,128)(2,1)S(1)} %pad_maximum_fusion.after_ref), channel_id=1, source_target_pairs={{0,12},{4,0},{8,4},{12,8},{1,13},{5,1},{9,5},{13,9},{2,14},{6,2},{... | collective-permute-start | bytes 122888 | tf_op jit(solution)/shard_map/ppermute | solution.py:22
  27.8 2.5 %collective-permute-done.3 = bf16[8,2560]{1,0:T(8,128)(2,1)S(1)} collective-permute-done((bf16[8,2560]{1,0:T(8,128)(2,1)S(1)}, bf16[8,2560]{1,0:T(8,128)(2,1)S(1)}, u32[]{:S(2)}, u32[]{:S(2)}) %collective-permute-start.3) | collective-permute-done | bytes 40992 | tf_op jit(solution)/shard_map/ppermute | solution.py:22
  30.7 4.1 %fusion.82 = (f32[40,2,8]{2,1,0:T(2,128)S(1)}, f32[40,2,8,256]{3,2,1,0:T(8,128)S(1)}) fusion(bf16[40,2,8,128]{3,2,1,0:T(8,128)(2,1)S(1)} %bitcast.179, pred[40,256]{1,0:T(8,128)(4,1)S(1)} %iota_compare_fusion.1, bf16[40,256,256]{2,1,0:T(8,128)(2,1)} %param.15), kind=kOutput, calls=%fused_computation.152 | convolution fusion | flops 42433920 | bytes 6074880 | tf_op jit(solution)/shard_map/skgd,sbkd->skgb/dot_general | solution.py:319
  36.1 3.4 %fusion.15 = f32[2,8,128,40]{2,1,0,3:T(8,128)S(1)} fusion(f32[40,2,8,256]{3,2,1,0:T(8,128)S(1)} %get-tuple-element.56, f32[40,2,8]{2,1,0:T(2,128)S(1)} %get-tuple-element.55, pred[40,256]{1,0:T(8,128)(4,1)S(1)} %iota_compare_fusion.1, f32[2,8,40]{1,0,2:T(2,128)S(1)} %copy.138, bf16[40,256,256]{2,1,0:T(8,128)(2,1)} %param.16), kind=kOutput, calls=%fused_computation.11 | convolution fusion | flops 42516480 | bytes 6241280 | tf_op jit(solution)/shard_map/skgb,sbkd->skgd/dot_general | solution.py:329
  39.9 2.0 %collective-permute-start.6 = (bf16[8,2176]{1,0:T(8,128)(2,1)S(1)}, bf16[8,2176]{1,0:T(8,128)(2,1)S(1)}, u32[]{:S(2)}, u32[]{:S(2)}) collective-permute-start(bf16[8,2176]{1,0:T(8,128)(2,1)S(1)} %get-tuple-element.28), channel_id=1, source_target_pairs={{0,4},{4,8},{8,12},{12,0},{1,5},{5,9},{9,13},{13,1},{2,6},{6,10},{... | collective-permute-start | bytes 104456 | tf_op jit(solution)/shard_map/ppermute | solution.py:22
  41.9 1.9 %collective-permute-start.7 = (bf16[8,2176]{1,0:T(8,128)(2,1)S(1)}, bf16[8,2176]{1,0:T(8,128)(2,1)S(1)}, u32[]{:S(2)}, u32[]{:S(2)}) collective-permute-start(bf16[8,2176]{1,0:T(8,128)(2,1)S(1)} %get-tuple-element.29), channel_id=1, source_target_pairs={{0,8},{4,12},{8,0},{12,4},{1,9},{5,13},{9,1},{13,5},{2,10},{6,14},... | collective-permute-start | bytes 104456 | tf_op jit(solution)/shard_map/ppermute | solution.py:22
  43.8 0.6 collective-permute-start.8
  44.4 1.6 %collective-permute-done.6 = bf16[8,2176]{1,0:T(8,128)(2,1)S(1)} collective-permute-done((bf16[8,2176]{1,0:T(8,128)(2,1)S(1)}, bf16[8,2176]{1,0:T(8,128)(2,1)S(1)}, u32[]{:S(2)}, u32[]{:S(2)}) %collective-permute-start.6) | collective-permute-done | bytes 34848 | tf_op jit(solution)/shard_map/ppermute | solution.py:22
  46.0 0.8 collective-permute-done.7
  47.1 0.7 collective-permute-done.8
  49.0 2.4 %collective-permute-start.11 = (bf16[8,2048]{1,0:T(8,128)(2,1)S(1)}, bf16[8,2048]{1,0:T(8,128)(2,1)S(1)}, u32[]{:S(2)}, u32[]{:S(2)}) collective-permute-start(bf16[8,2048]{1,0:T(8,128)(2,1)S(1)} %divide_convert_fusion.refs_0_.after_ref), channel_id=1, source_target_pairs={{0,12},{4,0},{8,4},{12,8},{1,13},{5,1},{9,5},{13,9},{2,14},{6,2},{... | collective-permute-start | bytes 98312 | tf_op jit(solution)/shard_map/ppermute | solution.py:22
  51.4 0.8 collective-permute-start.9
  52.2 3.4 %copy-done = bf16[2048,2048]{1,0:T(8,128)(2,1)S(1)} copy-done((bf16[2048,2048]{1,0:T(8,128)(2,1)S(1)}, bf16[2048,2048]{1,0:T(8,128)(2,1)}, u32[]{:S(2)}) %copy-start) | copy-done | bytes 8388632
  55.5 0.6 shard_map.131.refs_4_
  56.2 0.9 collective-permute-done.9.refs_1_
  57.1 2.1 %shard_map.132 = (bf16[32,2048]{1,0:T(8,128)(2,1)S(1)}, bf16[32,2048]{1,0:T(8,128)(2,1)}) custom-call(bf16[8,2048]{1,0:T(8,128)(2,1)S(1)} %divide_convert_fusion.refs_0_.after_ref, bf16[8,2048]{1,0:T(8,128)(2,1)S(1)} %collective-permute-done.9.refs_1_, bf16[8,2048]{1,0:T(8,128)(2,1)S(1)} %collective-permute-done.10.refs_2_, ...), custom_call_target="tpu_custom_call" | custom-call | flops 268435456 | bytes 8388608 | tf_op jit(solution)/shard_map/pallas_call | solution.py:143
  59.2 4.2 %shard_map.134.refs_0_ = bf16[768,2,3584]{2,1,0:T(2,128)(2,1)S(1)} custom-call(bf16[8,2048]{1,0:T(8,128)(2,1)S(1)} %divide_convert_fusion.refs_0_.after_ref, bf16[2048,2,3584]{2,1,0:T(2,128)(2,1)} %refs_2_.1), custom_call_target="tpu_custom_call" | custom-call | flops 3853516800 | tf_op jit(solution)/shard_map/pallas_call | solution.py:102
  63.5 1.6 %collective-permute-start.13 = (bf16[32,2048]{1,0:T(8,128)(2,1)S(1)}, bf16[32,2048]{1,0:T(8,128)(2,1)S(1)}, u32[]{:S(2)}, u32[]{:S(2)}) collective-permute-start(bf16[32,2048]{1,0:T(8,128)(2,1)S(1)} %shard_map.133.after_ref.near_ref), channel_id=1, source_target_pairs={{0,2},{1,3},{2,0},{3,1},{4,6},{5,7},{6,4},{7,5},{8,10},{9,11},{10,... | collective-permute-start | bytes 393224 | tf_op jit(solution)/shard_map/ppermute | solution.py:293
  65.1 3.7 %shard_map.135.refs_1_ = bf16[640,2,3584]{2,1,0:T(2,128)(2,1)S(1)} custom-call(bf16[32,2048]{1,0:T(8,128)(2,1)S(1)} %shard_map.133.after_ref.near_ref, bf16[2048,2,3584]{2,1,0:T(2,128)(2,1)} %refs_2_.1), custom_call_target="tpu_custom_call" | custom-call | flops 3211264000 | tf_op jit(solution)/shard_map/pallas_call | solution.py:102
  68.8 0.7 collective-permute-done.13.far_ref
  69.5 8.8 %shard_map.136 = (bf16[32,2048]{1,0:T(8,128)(2,1)S(1)}, bf16[16,3712]{1,0:T(8,128)(2,1)S(1)}, bf16[16,3712]{1,0:T(8,128)(2,1)S(1)}, bf16[16,3712]{1,0:T(8,128)(2,1)S(1)}, bf16[16,3712]{1,0:T(8,128)(2,1)S(1)}) custom-call(bf16[32,2048]{1,0:T(8,128)(2,1)S(1)} %copy-done.1, bf16[32,2048]{1,0:T(8,128)(2,1)S(1)} %shard_map.133.after_ref.near_ref, ...), custom_call_target="tpu_custom_call" | custom-call | flops 1879048192 | bytes 29360128 | tf_op jit(solution)/shard_map/pallas_call | solution.py:229
  78.3 1.8 %collective-permute-start.14 = (bf16[16,3712]{1,0:T(8,128)(2,1)S(1)}, bf16[16,3712]{1,0:T(8,128)(2,1)S(1)}, u32[]{:S(2)}, u32[]{:S(2)}) collective-permute-start(bf16[16,3712]{1,0:T(8,128)(2,1)S(1)} %get-tuple-element.13), channel_id=1, source_target_pairs={{0,4},{4,8},{8,12},{12,0},{1,5},{5,9},{9,13},{13,1},{2,6},{6,10},{... | collective-permute-start | bytes 356360 | tf_op jit(solution)/shard_map/ppermute | solution.py:22
  80.2 0.9 collective-permute-start.15
  81.1 1.5 %collective-permute-start.16 = (bf16[16,3712]{1,0:T(8,128)(2,1)S(1)}, bf16[16,3712]{1,0:T(8,128)(2,1)S(1)}, u32[]{:S(2)}, u32[]{:S(2)}) collective-permute-start(bf16[16,3712]{1,0:T(8,128)(2,1)S(1)} %get-tuple-element.15), channel_id=1, source_target_pairs={{0,12},{4,0},{8,4},{12,8},{1,13},{5,1},{9,5},{13,9},{2,14},{6,2},{... | collective-permute-start | bytes 356360 | tf_op jit(solution)/shard_map/ppermute | solution.py:22
  82.6 3.8 %collective-permute-done.14.refs_1_ = bf16[16,3712]{1,0:T(8,128)(2,1)S(1)} collective-permute-done((bf16[16,3712]{1,0:T(8,128)(2,1)S(1)}, bf16[16,3712]{1,0:T(8,128)(2,1)S(1)}, u32[]{:S(2)}, u32[]{:S(2)}) %collective-permute-start.14) | collective-permute-done | bytes 118816 | tf_op jit(solution)/shard_map/ppermute | solution.py:22
  86.4 3.8 %collective-permute-done.15.refs_2_ = bf16[16,3712]{1,0:T(8,128)(2,1)S(1)} collective-permute-done((bf16[16,3712]{1,0:T(8,128)(2,1)S(1)}, bf16[16,3712]{1,0:T(8,128)(2,1)S(1)}, u32[]{:S(2)}, u32[]{:S(2)}) %collective-permute-start.15) | collective-permute-done | bytes 118816 | tf_op jit(solution)/shard_map/ppermute | solution.py:22
  90.4 3.1 %collective-permute-start.19 = (bf16[8,3584]{1,0:T(8,128)(2,1)S(1)}, bf16[8,3584]{1,0:T(8,128)(2,1)S(1)}, u32[]{:S(2)}, u32[]{:S(2)}) collective-permute-start(bf16[8,3584]{1,0:T(8,128)(2,1)S(1)} %shard_map.137.refs_0_), channel_id=1, source_target_pairs={{0,12},{4,0},{8,4},{12,8},{1,13},{5,1},{9,5},{13,9},{2,14},{6,2},{... | collective-permute-start | bytes 172040 | tf_op jit(solution)/shard_map/ppermute | solution.py:22
  93.5 1.4 %collective-permute-start.18 = (bf16[8,3584]{1,0:T(8,128)(2,1)S(1)}, bf16[8,3584]{1,0:T(8,128)(2,1)S(1)}, u32[]{:S(2)}, u32[]{:S(2)}) collective-permute-start(bf16[8,3584]{1,0:T(8,128)(2,1)S(1)} %shard_map.137.refs_0_), channel_id=1, source_target_pairs={{0,8},{4,12},{8,0},{12,4},{1,9},{5,13},{9,1},{13,5},{2,10},{6,14},... | collective-permute-start | bytes 172040 | tf_op jit(solution)/shard_map/ppermute | solution.py:22
  94.9 5.3 %shard_map.138.refs_4_ = bf16[3584,2048]{1,0:T(8,128)(2,1)S(1)} custom-call(bf16[16,3712]{1,0:T(8,128)(2,1)S(1)} %get-tuple-element.12.refs_0_.after_ref, bf16[3584,2048]{1,0:T(8,128)(2,1)} %w_ref.7), custom_call_target="tpu_custom_call" | custom-call | flops 5138022400 | tf_op jit(solution)/shard_map/pallas_call | solution.py:102
  100.2 0.7 collective-permute-done.17.refs_1_
  100.9 3.0 %shard_map.139.l_ref = bf16[32,2048]{1,0:T(8,128)(2,1)S(1)} custom-call(bf16[8,3584]{1,0:T(8,128)(2,1)S(1)} %shard_map.137.refs_0_, bf16[8,3584]{1,0:T(8,128)(2,1)S(1)} %collective-permute-done.17.refs_1_, bf16[8,3584]{1,0:T(8,128)(2,1)S(1)} %collective-permute-done.18.refs_2_, bf16[8,3584]{1,0:T(8,128)(2,1)S(1)} %collective-permute-done.19.refs_3_, ...), custom_call_target="tpu_custom_call" | custom-call | flops 469762048 | bytes 14680064 | tf_op jit(solution)/shard_map/pallas_call | solution.py:143
  103.9 1.4 %collective-permute-done.20.r_ref = bf16[32,2048]{1,0:T(8,128)(2,1)S(1)} collective-permute-done((bf16[32,2048]{1,0:T(8,128)(2,1)S(1)}, bf16[32,2048]{1,0:T(8,128)(2,1)S(1)}, u32[]{:S(2)}, u32[]{:S(2)}) %collective-permute-start.20) | collective-permute-done | bytes 131104 | tf_op jit(solution)/shard_map/ppermute | solution.py:293
  105.3 1.6 %collective-permute-start.21 = (bf16[32,2048]{1,0:T(8,128)(2,1)S(1)}, bf16[32,2048]{1,0:T(8,128)(2,1)S(1)}, u32[]{:S(2)}, u32[]{:S(2)}) collective-permute-start(bf16[32,2048]{1,0:T(8,128)(2,1)S(1)} %shard_map.140), channel_id=1, source_target_pairs={{0,2},{1,3},{2,0},{3,1},{4,6},{5,7},{6,4},{7,5},{8,10},{9,11},{10,... | collective-permute-start | bytes 393224 | tf_op jit(solution)/shard_map/ppermute | solution.py:293
  106.8 4.1 %collective-permute-done.21 = bf16[32,2048]{1,0:T(8,128)(2,1)S(1)} collective-permute-done((bf16[32,2048]{1,0:T(8,128)(2,1)S(1)}, bf16[32,2048]{1,0:T(8,128)(2,1)S(1)}, u32[]{:S(2)}, u32[]{:S(2)}) %collective-permute-start.21) | collective-permute-done | bytes 131104 | tf_op jit(solution)/shard_map/ppermute | solution.py:293
  110.9 0.7 add_convert_fusion
  (102 shorter events, 5.1 us)
Async XLA Ops:
  4.4 5.1 %copy-start.1 = (bf16[32,2048]{1,0:T(8,128)(2,1)S(1)}, bf16[32,2048]{1,0:T(8,128)(2,1)}, u32[]{:S(2)}) copy-start(bf16[32,2048]{1,0:T(8,128)(2,1)} %hid_ref.1) | copy-start | bytes 393220
  4.5 11.9 %copy-start.4 = (s32[32]{0:T(128)S(1)}, s32[32]{0:T(128)}, u32[]{:S(2)}) copy-start(s32[32]{0:T(128)} %param.13) | copy-start | bytes 388
  4.5 12.0 %copy-start.3 = (bf16[2048]{0:T(1024)(128)(2,1)S(1)}, bf16[2048]{0:T(1024)(128)(2,1)}, u32[]{:S(2)}) copy-start(bf16[2048]{0:T(1024)(128)(2,1)} %param.21) | copy-start | bytes 12292
  4.5 12.0 %copy-start.2 = (s32[32,128]{1,0:T(8,128)S(1)}, s32[32,128]{1,0:T(8,128)}, u32[]{:S(2)}) copy-start(s32[32,128]{1,0:T(8,128)} %param.14) | copy-start | bytes 49156
  10.2 8.1 %collective-permute-start = (f32[8,2688]{1,0:T(8,128)S(1)}, f32[8,2688]{1,0:T(8,128)S(1)}, u32[]{:S(2)}, u32[]{:S(2)}) collective-permute-start(f32[8,2688]{1,0:T(8,128)S(1)} %get-tuple-element.24), channel_id=1, source_target_pairs={{0,4},{4,8},{8,12},{12,0},{1,5},{5,9},{9,13},{13,1},{2,6},{6,10},{... | collective-permute-start | bytes 258056 | tf_op jit(solution)/shard_map/ppermute | solution.py:22
  13.3 5.8 %collective-permute-start.2 = (f32[8,2688]{1,0:T(8,128)S(1)}, f32[8,2688]{1,0:T(8,128)S(1)}, u32[]{:S(2)}, u32[]{:S(2)}) collective-permute-start(f32[8,2688]{1,0:T(8,128)S(1)} %get-tuple-element.25), channel_id=1, source_target_pairs={{0,12},{4,0},{8,4},{12,8},{1,13},{5,1},{9,5},{13,9},{2,14},{6,2},{... | collective-permute-start | bytes 258056 | tf_op jit(solution)/shard_map/ppermute | solution.py:22
  15.3 8.0 %collective-permute-start.1 = (f32[8,2688]{1,0:T(8,128)S(1)}, f32[8,2688]{1,0:T(8,128)S(1)}, u32[]{:S(2)}, u32[]{:S(2)}) collective-permute-start(f32[8,2688]{1,0:T(8,128)S(1)} %get-tuple-element.26), channel_id=1, source_target_pairs={{0,8},{4,12},{8,0},{12,4},{1,9},{5,13},{9,1},{13,5},{2,10},{6,14},... | collective-permute-start | bytes 258056 | tf_op jit(solution)/shard_map/ppermute | solution.py:22
  23.8 6.5 %collective-permute-start.5 = (bf16[8,2560]{1,0:T(8,128)(2,1)S(1)}, bf16[8,2560]{1,0:T(8,128)(2,1)S(1)}, u32[]{:S(2)}, u32[]{:S(2)}) collective-permute-start(bf16[8,2560]{1,0:T(8,128)(2,1)S(1)} %pad_maximum_fusion.after_ref), channel_id=1, source_target_pairs={{0,4},{4,8},{8,12},{12,0},{1,5},{5,9},{9,13},{13,1},{2,6},{6,10},{... | collective-permute-start | bytes 122888 | tf_op jit(solution)/shard_map/ppermute | solution.py:22
  23.9 6.5 %collective-permute-start.4 = (bf16[8,2560]{1,0:T(8,128)(2,1)S(1)}, bf16[8,2560]{1,0:T(8,128)(2,1)S(1)}, u32[]{:S(2)}, u32[]{:S(2)}) collective-permute-start(bf16[8,2560]{1,0:T(8,128)(2,1)S(1)} %pad_maximum_fusion.after_ref), channel_id=1, source_target_pairs={{0,8},{4,12},{8,0},{12,4},{1,9},{5,13},{9,1},{13,5},{2,10},{6,14},... | collective-permute-start | bytes 122888 | tf_op jit(solution)/shard_map/ppermute | solution.py:22
  26.3 4.1 %collective-permute-start.3 = (bf16[8,2560]{1,0:T(8,128)(2,1)S(1)}, bf16[8,2560]{1,0:T(8,128)(2,1)S(1)}, u32[]{:S(2)}, u32[]{:S(2)}) collective-permute-start(bf16[8,2560]{1,0:T(8,128)(2,1)S(1)} %pad_maximum_fusion.after_ref), channel_id=1, source_target_pairs={{0,12},{4,0},{8,4},{12,8},{1,13},{5,1},{9,5},{13,9},{2,14},{6,2},{... | collective-permute-start | bytes 122888 | tf_op jit(solution)/shard_map/ppermute | solution.py:22
  39.9 6.1 %collective-permute-start.6 = (bf16[8,2176]{1,0:T(8,128)(2,1)S(1)}, bf16[8,2176]{1,0:T(8,128)(2,1)S(1)}, u32[]{:S(2)}, u32[]{:S(2)}) collective-permute-start(bf16[8,2176]{1,0:T(8,128)(2,1)S(1)} %get-tuple-element.28), channel_id=1, source_target_pairs={{0,4},{4,8},{8,12},{12,0},{1,5},{5,9},{9,13},{13,1},{2,6},{6,10},{... | collective-permute-start | bytes 104456 | tf_op jit(solution)/shard_map/ppermute | solution.py:22
  41.9 4.9 %collective-permute-start.7 = (bf16[8,2176]{1,0:T(8,128)(2,1)S(1)}, bf16[8,2176]{1,0:T(8,128)(2,1)S(1)}, u32[]{:S(2)}, u32[]{:S(2)}) collective-permute-start(bf16[8,2176]{1,0:T(8,128)(2,1)S(1)} %get-tuple-element.29), channel_id=1, source_target_pairs={{0,8},{4,12},{8,0},{12,4},{1,9},{5,13},{9,1},{13,5},{2,10},{6,14},... | collective-permute-start | bytes 104456 | tf_op jit(solution)/shard_map/ppermute | solution.py:22
  43.8 3.9 %collective-permute-start.8 = (bf16[8,2176]{1,0:T(8,128)(2,1)S(1)}, bf16[8,2176]{1,0:T(8,128)(2,1)S(1)}, u32[]{:S(2)}, u32[]{:S(2)}) collective-permute-start(bf16[8,2176]{1,0:T(8,128)(2,1)S(1)} %get-tuple-element.30), channel_id=1, source_target_pairs={{0,12},{4,0},{8,4},{12,8},{1,13},{5,1},{9,5},{13,9},{2,14},{6,2},{... | collective-permute-start | bytes 104456 | tf_op jit(solution)/shard_map/ppermute | solution.py:22
  49.0 7.2 %collective-permute-start.11 = (bf16[8,2048]{1,0:T(8,128)(2,1)S(1)}, bf16[8,2048]{1,0:T(8,128)(2,1)S(1)}, u32[]{:S(2)}, u32[]{:S(2)}) collective-permute-start(bf16[8,2048]{1,0:T(8,128)(2,1)S(1)} %divide_convert_fusion.refs_0_.after_ref), channel_id=1, source_target_pairs={{0,12},{4,0},{8,4},{12,8},{1,13},{5,1},{9,5},{13,9},{2,14},{6,2},{... | collective-permute-start | bytes 98312 | tf_op jit(solution)/shard_map/ppermute | solution.py:22
  51.4 4.8 %collective-permute-start.10 = (bf16[8,2048]{1,0:T(8,128)(2,1)S(1)}, bf16[8,2048]{1,0:T(8,128)(2,1)S(1)}, u32[]{:S(2)}, u32[]{:S(2)}) collective-permute-start(bf16[8,2048]{1,0:T(8,128)(2,1)S(1)} %divide_convert_fusion.refs_0_.after_ref), channel_id=1, source_target_pairs={{0,8},{4,12},{8,0},{12,4},{1,9},{5,13},{9,1},{13,5},{2,10},{6,14},... | collective-permute-start | bytes 98312 | tf_op jit(solution)/shard_map/ppermute | solution.py:22
  51.4 5.7 %collective-permute-start.9 = (bf16[8,2048]{1,0:T(8,128)(2,1)S(1)}, bf16[8,2048]{1,0:T(8,128)(2,1)S(1)}, u32[]{:S(2)}, u32[]{:S(2)}) collective-permute-start(bf16[8,2048]{1,0:T(8,128)(2,1)S(1)} %divide_convert_fusion.refs_0_.after_ref), channel_id=1, source_target_pairs={{0,4},{4,8},{8,12},{12,0},{1,5},{5,9},{9,13},{13,1},{2,6},{6,10},{... | collective-permute-start | bytes 98312 | tf_op jit(solution)/shard_map/ppermute | solution.py:22
  52.2 3.4 %copy-start = (bf16[2048,2048]{1,0:T(8,128)(2,1)S(1)}, bf16[2048,2048]{1,0:T(8,128)(2,1)}, u32[]{:S(2)}) copy-start(bf16[2048,2048]{1,0:T(8,128)(2,1)} %w_ref.4) | copy-start | bytes 25165828
  59.2 4.3 %collective-permute-start.12 = (bf16[32,2048]{1,0:T(8,128)(2,1)S(1)}, bf16[32,2048]{1,0:T(8,128)(2,1)S(1)}, u32[]{:S(2)}, u32[]{:S(2)}) collective-permute-start(bf16[32,2048]{1,0:T(8,128)(2,1)S(1)} %get-tuple-element.10.l_ref), channel_id=1, source_target_pairs={{0,1},{1,0},{2,3},{3,2},{4,5},{5,4},{6,7},{7,6},{8,9},{9,8},{10,11... | collective-permute-start | bytes 393224 | tf_op jit(solution)/shard_map/ppermute | solution.py:293
  63.5 6.0 %collective-permute-start.13 = (bf16[32,2048]{1,0:T(8,128)(2,1)S(1)}, bf16[32,2048]{1,0:T(8,128)(2,1)S(1)}, u32[]{:S(2)}, u32[]{:S(2)}) collective-permute-start(bf16[32,2048]{1,0:T(8,128)(2,1)S(1)} %shard_map.133.after_ref.near_ref), channel_id=1, source_target_pairs={{0,2},{1,3},{2,0},{3,1},{4,6},{5,7},{6,4},{7,5},{8,10},{9,11},{10,... | collective-permute-start | bytes 393224 | tf_op jit(solution)/shard_map/ppermute | solution.py:293
  78.3 8.1 %collective-permute-start.14 = (bf16[16,3712]{1,0:T(8,128)(2,1)S(1)}, bf16[16,3712]{1,0:T(8,128)(2,1)S(1)}, u32[]{:S(2)}, u32[]{:S(2)}) collective-permute-start(bf16[16,3712]{1,0:T(8,128)(2,1)S(1)} %get-tuple-element.13), channel_id=1, source_target_pairs={{0,4},{4,8},{8,12},{12,0},{1,5},{5,9},{9,13},{13,1},{2,6},{6,10},{... | collective-permute-start | bytes 356360 | tf_op jit(solution)/shard_map/ppermute | solution.py:22
  80.2 10.0 %collective-permute-start.15 = (bf16[16,3712]{1,0:T(8,128)(2,1)S(1)}, bf16[16,3712]{1,0:T(8,128)(2,1)S(1)}, u32[]{:S(2)}, u32[]{:S(2)}) collective-permute-start(bf16[16,3712]{1,0:T(8,128)(2,1)S(1)} %get-tuple-element.14), channel_id=1, source_target_pairs={{0,8},{4,12},{8,0},{12,4},{1,9},{5,13},{9,1},{13,5},{2,10},{6,14},... | collective-permute-start | bytes 356360 | tf_op jit(solution)/shard_map/ppermute | solution.py:22
  81.1 9.1 %collective-permute-start.16 = (bf16[16,3712]{1,0:T(8,128)(2,1)S(1)}, bf16[16,3712]{1,0:T(8,128)(2,1)S(1)}, u32[]{:S(2)}, u32[]{:S(2)}) collective-permute-start(bf16[16,3712]{1,0:T(8,128)(2,1)S(1)} %get-tuple-element.15), channel_id=1, source_target_pairs={{0,12},{4,0},{8,4},{12,8},{1,13},{5,1},{9,5},{13,9},{2,14},{6,2},{... | collective-permute-start | bytes 356360 | tf_op jit(solution)/shard_map/ppermute | solution.py:22
  90.4 9.8 %collective-permute-start.19 = (bf16[8,3584]{1,0:T(8,128)(2,1)S(1)}, bf16[8,3584]{1,0:T(8,128)(2,1)S(1)}, u32[]{:S(2)}, u32[]{:S(2)}) collective-permute-start(bf16[8,3584]{1,0:T(8,128)(2,1)S(1)} %shard_map.137.refs_0_), channel_id=1, source_target_pairs={{0,12},{4,0},{8,4},{12,8},{1,13},{5,1},{9,5},{13,9},{2,14},{6,2},{... | collective-permute-start | bytes 172040 | tf_op jit(solution)/shard_map/ppermute | solution.py:22
  93.5 6.7 %collective-permute-start.18 = (bf16[8,3584]{1,0:T(8,128)(2,1)S(1)}, bf16[8,3584]{1,0:T(8,128)(2,1)S(1)}, u32[]{:S(2)}, u32[]{:S(2)}) collective-permute-start(bf16[8,3584]{1,0:T(8,128)(2,1)S(1)} %shard_map.137.refs_0_), channel_id=1, source_target_pairs={{0,8},{4,12},{8,0},{12,4},{1,9},{5,13},{9,1},{13,5},{2,10},{6,14},... | collective-permute-start | bytes 172040 | tf_op jit(solution)/shard_map/ppermute | solution.py:22
  94.9 6.0 %collective-permute-start.17 = (bf16[8,3584]{1,0:T(8,128)(2,1)S(1)}, bf16[8,3584]{1,0:T(8,128)(2,1)S(1)}, u32[]{:S(2)}, u32[]{:S(2)}) collective-permute-start(bf16[8,3584]{1,0:T(8,128)(2,1)S(1)} %shard_map.137.refs_0_), channel_id=1, source_target_pairs={{0,4},{4,8},{8,12},{12,0},{1,5},{5,9},{9,13},{13,1},{2,6},{6,10},{... | collective-permute-start | bytes 172040 | tf_op jit(solution)/shard_map/ppermute | solution.py:22
  103.9 1.4 %collective-permute-start.20 = (bf16[32,2048]{1,0:T(8,128)(2,1)S(1)}, bf16[32,2048]{1,0:T(8,128)(2,1)S(1)}, u32[]{:S(2)}, u32[]{:S(2)}) collective-permute-start(bf16[32,2048]{1,0:T(8,128)(2,1)S(1)} %shard_map.139.l_ref), channel_id=1, source_target_pairs={{0,1},{1,0},{2,3},{3,2},{4,5},{5,4},{6,7},{7,6},{8,9},{9,8},{10,11... | collective-permute-start | bytes 393224 | tf_op jit(solution)/shard_map/ppermute | solution.py:293
  105.3 5.6 %collective-permute-start.21 = (bf16[32,2048]{1,0:T(8,128)(2,1)S(1)}, bf16[32,2048]{1,0:T(8,128)(2,1)S(1)}, u32[]{:S(2)}, u32[]{:S(2)}) collective-permute-start(bf16[32,2048]{1,0:T(8,128)(2,1)S(1)} %shard_map.140), channel_id=1, source_target_pairs={{0,2},{1,3},{2,0},{3,1},{4,6},{5,7},{6,4},{7,5},{8,10},{9,11},{10,... | collective-permute-start | bytes 393224 | tf_op jit(solution)/shard_map/ppermute | solution.py:293

commit v3 on v2

--- a/solution.py
+++ b/solution.py
@@ -56,10 +56,11 @@
 
 VMEM = pltpu.VMEM
 LIMIT = 12 << 20
-SMALL = 2 << 20
 GATE_LIMIT = 24 << 20
-HIDE = (0.0, 0.0, 0.0, 0.0, 0.0, 0.0)
+QUERY_LIMIT = 56 << 20
+FETCH_LIMIT = 26 << 20
 CUT = (6, 5)
+OUT_LIMIT = 40 << 20
 
 
 def whole(count):
@@ -83,7 +84,7 @@
         held[pl.ds(at, rows), :] = part[...].astype(jnp.float32)
 
 
-def fetch(weight, start, count, after):
+def fetch(weight, start, count, after, limit=None):
     pieces = 4
     step = count // pieces
 
@@ -105,7 +106,7 @@
         out_specs=pl.BlockSpec(memory_space=VMEM),
         out_shape=jax.ShapeDtypeStruct((count,) + weight.shape[1:], weight.dtype),
         scratch_shapes=[pltpu.SemaphoreType.DMA((pieces,))],
-        compiler_params=pltpu.CompilerParams(vmem_limit_bytes=26 << 20),
+        compiler_params=pltpu.CompilerParams(vmem_limit_bytes=FETCH_LIMIT if limit is None else limit),
         cost_estimate=pl.CostEstimate(
             flops=700 * count * math.prod(weight.shape[1:]),
             bytes_accessed=0,
@@ -123,14 +124,14 @@
         ).astype(out_ref.dtype)
 
 
-def gathered_dot(parts, weight, n_mem, keep, hidden_us):
+def gathered_dot(parts, weight, n_mem, keep, beside=()):
     rows = parts[0].shape[0] * n_mem
     depth, width = weight.shape
     tile = 512 if width % 512 == 0 else 128
 
     def kernel(*refs):
         part_refs, w_ref = refs[:n_mem], refs[n_mem]
-        outs, held = refs[n_mem + 1 : -1], refs[-1]
+        outs, held = refs[n_mem + 1 + len(beside) : -1], refs[-1]
         place(part_refs, held, n_mem)
         x = to_bf16(held[...])
         if keep:
@@ -142,20 +143,139 @@
         shapes.append(jax.ShapeDtypeStruct((rows, depth), jnp.bfloat16))
     return pl.pallas_call(
         kernel,
-        in_specs=whole(n_mem + 1),
+        in_specs=whole(n_mem + 1) + [pl.BlockSpec(memory_space=pl.ANY)] * len(beside),
         out_specs=whole(len(shapes)),
         out_shape=shapes,
         scratch_shapes=[VMEM((rows, depth), jnp.float32)],
         compiler_params=pltpu.CompilerParams(vmem_limit_bytes=LIMIT),
-        cost_estimate=cost(hidden_us, weight),
-    )(*parts, weight)
+        cost_estimate=cost(0.0, weight),
+    )(*parts, weight, *beside)
+
+
+def unfold(x, spread):
+    count = x.shape[0]
+    row = lax.broadcasted_iota(jnp.int32, (128, 256), 0)
+    col = lax.broadcasted_iota(jnp.int32, (128, 256), 1)
+    even = jnp.where(col == 2 * row, 1.0, 0.0).astype(jnp.bfloat16)
+    odd = jnp.where(col == 2 * row + 1, 1.0, 0.0).astype(jnp.bfloat16)
+    for b in range(x.shape[1] // 128):
+        block = x[:, b * 128 : (b + 1) * 128]
+        for half, pick in enumerate((even, odd)):
+            spread[half * count : (half + 1) * count, b * 256 : (b + 1) * 256] = to_bf16(
+                jnp.dot(block, pick, preferred_element_type=jnp.float32)
+            )
+
+
+def query_parts(hidden, gain, w_query, w_kv, n_mem):
+    req, depth = hidden.shape
+    q_width, kv_width = w_query.shape[1], w_kv.shape[2]
+    rows = req // n_mem
+    body = q_width + 2 * kv_width
+    chunks, ahead = 8, 3
+    step = depth // chunks
+
+    def kernel(hid_ref, gain_ref, wq_ref, wkv_ref, *refs):
+        outs = refs[:n_mem]
+        acc, spread, q_buf, kv_buf, q_sems, kv_sems, hid_buf, gain_buf = refs[n_mem:]
+        small = [
+            pltpu.make_async_copy(hid_ref, hid_buf, kv_sems.at[1]),
+            pltpu.make_async_copy(gain_ref, gain_buf, kv_sems.at[2]),
+        ]
+        for copy in small:
+            copy.start()
+        kv_copy = pltpu.make_async_copy(wkv_ref, kv_buf, kv_sems.at[0])
+        kv_copy.start()
+        copies = [
+            pltpu.make_async_copy(
+                wq_ref.at[pl.ds(i * step, step)], q_buf.at[pl.ds(i * step, step)], q_sems.at[i]
+            )
+            for i in range(chunks)
+        ]
+        for copy in copies[:ahead]:
+            copy.start()
+        for copy in small:
+            copy.wait()
+        wide = hid_buf[...].astype(jnp.float32)
+        acc[:, body:] = jnp.broadcast_to(jnp.sum(wide * wide, 1, keepdims=True), (req, 128))
+        normed = to_bf16(wide * gain_buf[...].astype(jnp.float32).reshape(1, depth))
+        unfold(normed, spread)
+        kv_copy.wait()
+        both = jnp.dot(
+            spread[...],
+            kv_buf[...].reshape(2 * depth, kv_width),
+            preferred_element_type=jnp.float32,
+        )
+        acc[:, q_width : q_width + kv_width] = both[:req]
+        acc[:, q_width + kv_width : body] = both[req:]
+        for i, copy in enumerate(copies):
+            copy.wait()
+            if i + ahead < chunks:
+                copies[i + ahead].start()
+            term = jnp.dot(
+                normed[:, i * step : (i + 1) * step],
+                q_buf[i * step : (i + 1) * step, :],
+                preferred_element_type=jnp.float32,
+            )
+            acc[:, :q_width] = term if i == 0 else acc[:, :q_width] + term
+        me = lax.axis_index("mem")
+        for step_to in range(n_mem):
+            at = pl.multiple_of(lax.rem(me + step_to, n_mem) * rows, rows)
+            outs[step_to][...] = acc[pl.ds(at, rows), :]
+
+    return pl.pallas_call(
+        kernel,
+        in_specs=[pl.BlockSpec(memory_space=pltpu.HBM)] * 4,
+        out_specs=whole(n_mem),
+        out_shape=[jax.ShapeDtypeStruct((rows, body + 128), jnp.float32)] * n_mem,
+        scratch_shapes=[
+            VMEM((req, body + 128), jnp.float32),
+            VMEM((2 * req, 2 * depth), jnp.bfloat16),
+            VMEM(w_query.shape, jnp.bfloat16),
+            VMEM(w_kv.shape, jnp.bfloat16),
+            pltpu.SemaphoreType.DMA((chunks,)),
+            pltpu.SemaphoreType.DMA((3,)),
+            VMEM(hidden.shape, jnp.bfloat16),
+            VMEM(gain.shape, jnp.bfloat16),
+        ],
+        compiler_params=pltpu.CompilerParams(vmem_limit_bytes=QUERY_LIMIT),
+        cost_estimate=pl.CostEstimate(
+            flops=2 * req * w_query.size, bytes_accessed=2 * w_query.size, transcendentals=0
+        ),
+    )(hidden, gain, w_query, w_kv)
+
+
+def turned_parts(parts, cosine, sine, q_width, kv_width, beside):
+    rows = parts[0].shape[0]
+    body = q_width + 2 * kv_width
+    n = len(parts)
+
+    def kernel(*refs):
+        cos_ref, sin_ref, out = refs[n], refs[n + 1], refs[-1]
+        total = refs[0][...]
+        for ref in refs[1:n]:
+            total = total + ref[...]
+        scale = lax.rsqrt(total[:, body : body + 1] / D + NORM_EPS)
+        cos, sin = cos_ref[...], sin_ref[...]
+        for at in range(0, q_width + kv_width, HD):
+            head = total[:, at : at + HD] * scale
+            out[:, at : at + HD] = to_bf16(head * cos + pltpu.roll(head, HD // 2, 1) * sin)
+        out[:, q_width + kv_width :] = to_bf16(total[:, q_width + kv_width : body] * scale)
+
+    return pl.pallas_call(
+        kernel,
+        in_specs=whole(n + 2) + [pl.BlockSpec(memory_space=pl.ANY)] * len(beside),
+        out_specs=pl.BlockSpec(memory_space=VMEM),
+        out_shape=jax.ShapeDtypeStruct((rows, body), jnp.bfloat16),
+        compiler_params=pltpu.CompilerParams(vmem_limit_bytes=LIMIT),
+        cost_estimate=cost(0.0),
+    )(*parts, cosine, sine, *beside)
 
 
 def gate_up_parts(hidden, near, far, gain, held, weight, n_mem, hidden_us):
     req, depth = hidden.shape
     ff = weight.shape[2]
     rows = req // n_mem
-    tile = 512 if ff % 512 == 0 else 128
+    tile = ff // 2 if ff % 256 == 0 else 128
 
     n_held = len(held)
     first = sum(h.shape[0] for h in held)
@@ -183,17 +303,8 @@
         mid_ref[...] = middle
         wide = middle.astype(jnp.float32)
         power[...] = jnp.broadcast_to(jnp.sum(wide * wide, 1, keepdims=True), power.shape)
-        normed = to_bf16(wide * gain_ref[...].astype(jnp.float32))
-        row = lax.broadcasted_iota(jnp.int32, (128, 256), 0)
-        col = lax.broadcasted_iota(jnp.int32, (128, 256), 1)
-        even = jnp.where(col == 2 * row, 1.0, 0.0).astype(jnp.bfloat16)
-        odd = jnp.where(col == 2 * row + 1, 1.0, 0.0).astype(jnp.bfloat16)
-        for b in range(depth // 128):
-            block = normed[:, b * 128 : (b + 1) * 128]
-            for half, pick in enumerate((even, odd)):
-                spread[half * req : (half + 1) * req, b * 256 : (b + 1) * 256] = to_bf16(
-                    jnp.dot(block, pick, preferred_element_type=jnp.float32)
-                )
+        normed = to_bf16(wide * gain_ref[...].astype(jnp.float32).reshape(1, depth))
+        unfold(normed, spread)
 
         def add_rows(block, at, count, fresh):
             @pl.loop(0, ff // tile)
@@ -241,17 +352,17 @@
         ],
         compiler_params=pltpu.CompilerParams(vmem_limit_bytes=GATE_LIMIT),
         cost_estimate=cost(hidden_us, weight, 64),
-    )(hidden, near, far, gain.reshape(1, -1), *held, weight)
-
-
-def activate(parts, hidden_us):
+    )(hidden, near, far, gain, *held, weight)
+
+
+def activate(parts, beside):
     rows = parts[0].shape[0] // 2
     ff = parts[0].shape[1] - 128
 
     def kernel(*refs):
         out = refs[-1]
         total = refs[0][...].astype(jnp.float32)
-        for ref in refs[1:-1]:
+        for ref in refs[1 : len(parts)]:
             total = total + ref[...].astype(jnp.float32)
         power = total[:rows, ff : ff + 1] + total[rows:, ff : ff + 1]
         scale = lax.rsqrt(power / D + NORM_EPS)
@@ -261,12 +372,12 @@
 
     return pl.pallas_call(
         kernel,
-        in_specs=whole(len(parts)),
+        in_specs=whole(len(parts)) + [pl.BlockSpec(memory_space=pl.ANY)] * len(beside),
         out_specs=pl.BlockSpec(memory_space=VMEM),
         out_shape=jax.ShapeDtypeStruct((rows, ff), jnp.bfloat16),
         compiler_params=pltpu.CompilerParams(vmem_limit_bytes=LIMIT),
-        cost_estimate=cost(hidden_us),
-    )(*parts)
+        cost_estimate=cost(0.0),
+    )(*parts, *beside)
 
 
 def around(x, axis, n):
@@ -360,29 +471,39 @@
         scale_val = 1.0 / math.sqrt(head_dim)
         mem_pos = lax.axis_index("mem")
         rows = req_count // n_mem
-        resid = hidden_in.astype(jnp.float32)
-        normed = to_bf16(resid * attn_gain.astype(jnp.float32))
-        query_part = jnp.dot(normed, w_query, preferred_element_type=jnp.float32)
-        kv_part = jnp.dot(
-            normed, w_kv.reshape(w_kv.shape[0], -1), preferred_element_type=jnp.float32
-        )
-        power = jnp.sum(resid * resid, 1)
-        wide = jnp.concatenate(
-            [query_part, kv_part, jnp.broadcast_to(power[:, None], (req_count, 128))], 1
-        ).reshape(n_mem, rows, -1)
-        total = lax.dynamic_index_in_dim(wide, mem_pos, 0, False)
-        for part in scatter_parts(wide, "mem", n_mem):
-            total = total + part
-        body = q_width + 2 * kv_width
-        attn_scale = lax.rsqrt(total[:, body] / D + NORM_EPS)
-        cosine, sine = rotary(lengths, head_dim)
-        cos_own = lax.dynamic_slice_in_dim(cosine, mem_pos * rows, rows, 0)
-        sin_own = lax.dynamic_slice_in_dim(sine, mem_pos * rows, rows, 0)
-        scaled = total[:, :body] * attn_scale[:, None]
-        turned = rotate(
-            scaled[:, : q_width + kv_width].reshape(rows, -1, head_dim), cos_own, sin_own
-        ).reshape(rows, -1)
-        own_qkv = to_bf16(jnp.concatenate([turned, scaled[:, q_width + kv_width :]], 1))
+        if rows % 8:
+            resid = hidden_in.astype(jnp.float32)
+            normed = to_bf16(resid * attn_gain.astype(jnp.float32))
+            query_part = jnp.dot(normed, w_query, preferred_element_type=jnp.float32)
+            kv_part = jnp.dot(
+                normed, w_kv.reshape(w_kv.shape[0], -1), preferred_element_type=jnp.float32
+            )
+            power = jnp.sum(resid * resid, 1)
+            wide = jnp.concatenate(
+                [query_part, kv_part, jnp.broadcast_to(power[:, None], (req_count, 128))], 1
+            ).reshape(n_mem, rows, -1)
+            total = lax.dynamic_index_in_dim(wide, mem_pos, 0, False)
+            for part in scatter_parts(wide, "mem", n_mem):
+                total = total + part
+            body = q_width + 2 * kv_width
+            attn_scale = lax.rsqrt(total[:, body] / D + NORM_EPS)
+            cosine, sine = rotary(lengths, head_dim)
+            cos_own = lax.dynamic_slice_in_dim(cosine, mem_pos * rows, rows, 0)
+            sin_own = lax.dynamic_slice_in_dim(sine, mem_pos * rows, rows, 0)
+            scaled = total[:, :body] * attn_scale[:, None]
+            turned = rotate(
+                scaled[:, : q_width + kv_width].reshape(rows, -1, head_dim), cos_own, sin_own
+            ).reshape(rows, -1)
+            own_qkv = to_bf16(jnp.concatenate([turned, scaled[:, q_width + kv_width :]], 1))
+        else:
+            here = lax.dynamic_slice_in_dim(lengths, mem_pos * rows, rows, 0)
+            cosine, sine = rotary(here, head_dim)
+            cosine = jnp.concatenate([cosine, cosine], -1)[:, 0]
+            sine = jnp.concatenate([-sine, sine], -1)[:, 0]
+            terms = list(query_parts(hidden_in, attn_gain, w_query, w_kv, n_mem))
+            out_held = fetch(w_out, 0, w_out.shape[0], terms[0], OUT_LIMIT)
+            terms = terms[:1] + [shifted(t, "mem", n_mem, s) for s, t in enumerate(terms) if s]
+            own_qkv = turned_parts(terms, cosine, sine, q_width, kv_width, (out_held,))
         qkv = gather_parts(own_qkv, "mem", n_mem)
         queries = qkv[:, :q_width].reshape(req_count, kv_local, group_size, head_dim)
         q_own = own_qkv[:, :q_width].reshape(rows, kv_local, group_size, head_dim)
@@ -499,21 +620,20 @@
 
         depth = w_gate_up.shape[0]
         cut_a, cut_b = depth * CUT[0] // 16, depth * CUT[1] // 16
-        out_held = fetch(w_out, 0, w_out.shape[0], own_qkv)
         gate_a = fetch(w_gate_up, 0, cut_a, attended_own)
         proj, attended = gathered_dot(
-            around(attended_own, "mem", n_mem), out_held, n_mem, True, HIDE[2]
-        )
-        near, far = pairwise(proj, n_comp, HIDE[3])
+            around(attended_own, "mem", n_mem), out_held, n_mem, True, (gate_a,)
+        )
+        near, far = pairwise(proj, n_comp, 0.0)
         gate_b = fetch(w_gate_up, cut_a, cut_b, near)
         middle, *terms = gate_up_parts(
-            hidden_in, near, far, ffn_gain, (gate_a, gate_b), w_gate_up, n_mem, HIDE[3]
+            hidden_in, near, far, ffn_gain, (gate_a, gate_b), w_gate_up, n_mem, 0.0
         )
         down_held = fetch(w_down, 0, w_down.shape[0], terms[0])
         terms = terms[:1] + [shifted(t, "mem", n_mem, s) for s, t in enumerate(terms) if s]
-        activated = activate(terms, HIDE[4])
+        activated = activate(terms, (down_held,))
         (down,) = gathered_dot(
-            around(activated, "mem", n_mem), down_held, n_mem, False, HIDE[5]
+            around(activated, "mem", n_mem), down_held, n_mem, False
         )
         near, far = pairwise(down, n_comp, 0.0)
         updated = to_bf16(

time: 112 us -> 102 us (0.911)
  Pallas kernels: 28 us -> 36.8 us
  matrix products: 13.7 us -> 5.72 us
  local copies, waits for them, and re-layouts: 7.47 us -> 2.84 us
  waiting for transfers between devices: 26.7 us -> 22.1 us
  other arithmetic: 5.03 us -> 3.04 us
    pallas_call x3 -> x5, Pallas kernels: 5.26 us -> 12.7 us  [the longest x1 7.27 us: query_parts(): pl.pallas_call(kernel, in_specs=[pl.BlockSpec(memory_space=pltpu.HBM)] *...]
    ppermute x18, waiting for transfers between devices: 20.6 us -> 14.7 us  [shifted(): return lax.ppermute(x, axis, [(i, (i + step) % n) for i in range(n)])]
    dot_general x2 -> x0, matrix products: 5.52 us -> none  [the longest x1 5.06 us: shards(): query_part = jnp.dot(normed, w_query, preferred_element_type=jnp.float32)]
    unnamed x19 -> x29, local copies, waits for them, and re-layouts: 5.58 us -> 1.08 us
    pallas_call x4, Pallas kernels: 13.8 us -> 16.7 us  [fetch(): pl.pallas_call(kernel, in_specs=[pl.BlockSpec(memory_space=pl.ANY)] * 2,...]
    dot_general x1, matrix products: 4.06 us -> 1.58 us  [slot_stats(): jnp.einsum('skgd,sbkd->skgb', queries_slot, key_rows, preferred_element_t...]
    pallas_call x1, Pallas kernels: 8.82 us -> 7.25 us  [gate_up_parts(): pl.pallas_call(kernel, in_specs=whole(4 + n_held) + [pl.BlockSpec(memory_...]
    ppermute x4, waiting for transfers between devices: 6.09 us -> 7.4 us  [pairwise(): far = lax.ppermute(near, 'comp', [(i, i ^ step) for i in range(n)])]
  transfers between devices with their start and end apart: 22 -> 22, of which waited for: 14 -> 13; matrix products, arithmetic and copies ran while one was open for 2% -> 2% of each run, Pallas kernels for 12% -> 16%
where the time goes in v3:
time: 102 us
  Pallas kernels  36.8 us (36%)
  starting transfers between devices  30 us (29%)
  waiting for transfers between devices  22.1 us (22%)
  matrix products  5.72 us (6%)
  other arithmetic  3.04 us (3%)
  local copies, waits for them, and re-layouts  2.84 us (3%)
  between operations  1.12 us (1%)
    ppermute x18, starting transfers between devices, shifted(): return lax.ppermute(x, axis, [(i, (i + step) % n) for i in range(n)])  27.2 us
    pallas_call x4, Pallas kernels, fetch(): pl.pallas_call(kernel, in_specs=[pl.BlockSpec(memory_space=pl.ANY)] * 2,...  16.7 us
    ppermute x18, waiting for transfers between devices, shifted(): return lax.ppermute(x, axis, [(i, (i + step) % n) for i in range(n)])  14.7 us
    ppermute x4, waiting for transfers between devices, pairwise(): far = lax.ppermute(near, 'comp', [(i, i ^ step) for i in range(n)])  7.4 us
    pallas_call x1, Pallas kernels, query_parts(): pl.pallas_call(kernel, in_specs=[pl.BlockSpec(memory_space=pltpu.HBM)] *...  7.27 us
    pallas_call x1, Pallas kernels, gate_up_parts(): pl.pallas_call(kernel, in_specs=whole(4 + n_held) + [pl.BlockSpec(memory_...  7.25 us
    pallas_call x2, Pallas kernels, gathered_dot(): pl.pallas_call(kernel, in_specs=whole(n_mem + 1) + [pl.BlockSpec(memory_s...  5.13 us
    dot_general x1, matrix products, slot_stats(): jnp.einsum('skgb,sbkd->skgd', weights.astype(jnp.bfloat16), value_rows, p...  3.37 us
  transfers between devices with their start and end apart: 22, of which 13 were waited for; matrix products, arithmetic and copies ran while one was open for 2% of the time, Pallas kernels for 16%

profile of v3, /device:TPU:0, one launch (start us, length us, event | category | flops | bytes accessed | tf_op | source)
XLA Modules:
  0.0 101.6 jit_solution(17346180171639753216)
XLA Ops:
  0.7 7.3 %shard_map.131 = (f32[8,2688]{1,0:T(8,128)}, f32[8,2688]{1,0:T(8,128)}, f32[8,2688]{1,0:T(8,128)}, f32[8,2688]{1,0:T(8,128)}) custom-call(bf16[32,2048]{1,0:T(8,128)(2,1)} %hid_ref.3, bf16[2048]{0:T(1024)(128)(2,1)} %gain_ref.2, bf16[2048,2048]{1,0:T(8,128)(2,1)} %wq_ref.1, bf16[2048,2,256]{2,1,0:T(2,128)(2,1)} %wkv_ref.1), custom_call_target="tpu_custom_call" | custom-call | flops 268435456 | bytes 8388608 | tf_op jit(solution)/shard_map/pallas_call | solution.py:225
  7.9 3.1 %collective-permute-start = (f32[8,2688]{1,0:T(8,128)}, f32[8,2688]{1,0:T(8,128)S(1)}, u32[]{:S(2)}, u32[]{:S(2)}) collective-permute-start(f32[8,2688]{1,0:T(8,128)} %get-tuple-element.14), channel_id=1, source_target_pairs={{0,4},{4,8},{8,12},{12,0},{1,5},{5,9},{9,13},{13,1},{2,6},{6,10},{... | collective-permute-start | bytes 258056 | tf_op jit(solution)/shard_map/ppermute | solution.py:22
  11.0 2.6 %collective-permute-start.1 = (f32[8,2688]{1,0:T(8,128)}, f32[8,2688]{1,0:T(8,128)S(1)}, u32[]{:S(2)}, u32[]{:S(2)}) collective-permute-start(f32[8,2688]{1,0:T(8,128)} %get-tuple-element.15), channel_id=1, source_target_pairs={{0,8},{4,12},{8,0},{12,4},{1,9},{5,13},{9,1},{13,5},{2,10},{6,14},... | collective-permute-start | bytes 258056 | tf_op jit(solution)/shard_map/ppermute | solution.py:22
  13.6 1.3 %collective-permute-start.2 = (f32[8,2688]{1,0:T(8,128)}, f32[8,2688]{1,0:T(8,128)S(1)}, u32[]{:S(2)}, u32[]{:S(2)}) collective-permute-start(f32[8,2688]{1,0:T(8,128)} %get-tuple-element.16), channel_id=1, source_target_pairs={{0,12},{4,0},{8,4},{12,8},{1,13},{5,1},{9,5},{13,9},{2,14},{6,2},{... | collective-permute-start | bytes 258056 | tf_op jit(solution)/shard_map/ppermute | solution.py:22
  15.2 0.6 fusion.20
  15.8 0.3 select_reduce_fusion
  16.3 0.9 copy-done.2
  17.2 3.5 %shard_map.132.refs_6_.refs_4_ = bf16[2048,2048]{1,0:T(8,128)(2,1)S(1)} custom-call(f32[8,2688]{1,0:T(8,128)S(1)} %copy-done.2, bf16[2048,2048]{1,0:T(8,128)(2,1)} %w_ref.4), custom_call_target="tpu_custom_call" | custom-call | flops 2936012800 | tf_op jit(solution)/shard_map/pallas_call | solution.py:103
  21.0 1.1 %collective-permute-start.5 = (bf16[8,2560]{1,0:T(8,128)(2,1)S(1)}, bf16[8,2560]{1,0:T(8,128)(2,1)S(1)}, u32[]{:S(2)}, u32[]{:S(2)}) collective-permute-start(bf16[8,2560]{1,0:T(8,128)(2,1)S(1)} %shard_map.133), channel_id=1, source_target_pairs={{0,4},{4,8},{8,12},{12,0},{1,5},{5,9},{9,13},{13,1},{2,6},{6,10},{... | collective-permute-start | bytes 122888 | tf_op jit(solution)/shard_map/ppermute | solution.py:22
  22.1 1.8 %collective-permute-start.4 = (bf16[8,2560]{1,0:T(8,128)(2,1)S(1)}, bf16[8,2560]{1,0:T(8,128)(2,1)S(1)}, u32[]{:S(2)}, u32[]{:S(2)}) collective-permute-start(bf16[8,2560]{1,0:T(8,128)(2,1)S(1)} %shard_map.133), channel_id=1, source_target_pairs={{0,8},{4,12},{8,0},{12,4},{1,9},{5,13},{9,1},{13,5},{2,10},{6,14},... | collective-permute-start | bytes 122888 | tf_op jit(solution)/shard_map/ppermute | solution.py:22
  23.9 1.0 collective-permute-start.3
  25.0 2.9 %collective-permute-done.3 = bf16[8,2560]{1,0:T(8,128)(2,1)S(1)} collective-permute-done((bf16[8,2560]{1,0:T(8,128)(2,1)S(1)}, bf16[8,2560]{1,0:T(8,128)(2,1)S(1)}, u32[]{:S(2)}, u32[]{:S(2)}) %collective-permute-start.3) | collective-permute-done | bytes 40992 | tf_op jit(solution)/shard_map/ppermute | solution.py:22
  28.1 0.2 fusion.18
  28.4 1.6 %fusion.73 = (f32[40,2,8]{2,1,0:T(2,128)S(1)}, f32[40,2,8,256]{3,2,1,0:T(8,128)S(1)}) fusion(bf16[40,2,8,128]{3,2,1,0:T(8,128)(2,1)S(1)} %bitcast.161, pred[40,256]{1,0:T(8,128)(4,1)S(1)} %iota_compare_fusion.1, bf16[40,256,256]{2,1,0:T(8,128)(2,1)S(1)} %bitcast.160), kind=kOutput, calls=%fused_computation.132 | convolution fusion | flops 42433920 | bytes 6074880 | tf_op jit(solution)/shard_map/skgd,sbkd->skgb/dot_general | solution.py:430
  30.7 0.3 fusion.21
  31.3 3.4 %fusion.15 = f32[2,8,128,40]{2,1,0,3:T(8,128)S(1)} fusion(f32[40,2,8,256]{3,2,1,0:T(8,128)S(1)} %get-tuple-element.60, f32[40,2,8]{2,1,0:T(2,128)S(1)} %get-tuple-element.59, pred[40,256]{1,0:T(8,128)(4,1)S(1)} %iota_compare_fusion.1, f32[2,8,40]{1,0,2:T(2,128)S(1)} %copy.138, bf16[40,256,256]{2,1,0:T(8,128)(2,1)} %param.16), kind=kOutput, calls=%fused_computation.11 | convolution fusion | flops 42516480 | bytes 6241280 | tf_op jit(solution)/shard_map/skgb,sbkd->skgd/dot_general | solution.py:440
  34.8 0.3 convolution_convert_fusion.1
  35.2 1.6 %collective-permute-start.6 = (bf16[8,2176]{1,0:T(8,128)(2,1)S(1)}, bf16[8,2176]{1,0:T(8,128)(2,1)S(1)}, u32[]{:S(2)}, u32[]{:S(2)}) collective-permute-start(bf16[8,2176]{1,0:T(8,128)(2,1)S(1)} %get-tuple-element.31), channel_id=1, source_target_pairs={{0,4},{4,8},{8,12},{12,0},{1,5},{5,9},{9,13},{13,1},{2,6},{6,10},{... | collective-permute-start | bytes 104456 | tf_op jit(solution)/shard_map/ppermute | solution.py:22
  36.8 1.9 %collective-permute-start.7 = (bf16[8,2176]{1,0:T(8,128)(2,1)S(1)}, bf16[8,2176]{1,0:T(8,128)(2,1)S(1)}, u32[]{:S(2)}, u32[]{:S(2)}) collective-permute-start(bf16[8,2176]{1,0:T(8,128)(2,1)S(1)} %get-tuple-element.32), channel_id=1, source_target_pairs={{0,8},{4,12},{8,0},{12,4},{1,9},{5,13},{9,1},{13,5},{2,10},{6,14},... | collective-permute-start | bytes 104456 | tf_op jit(solution)/shard_map/ppermute | solution.py:22
  38.6 0.7 collective-permute-start.8
  39.4 1.6 %collective-permute-done.6 = bf16[8,2176]{1,0:T(8,128)(2,1)S(1)} collective-permute-done((bf16[8,2176]{1,0:T(8,128)(2,1)S(1)}, bf16[8,2176]{1,0:T(8,128)(2,1)S(1)}, u32[]{:S(2)}, u32[]{:S(2)}) %collective-permute-start.6) | collective-permute-done | bytes 34848 | tf_op jit(solution)/shard_map/ppermute | solution.py:22
  41.1 0.6 collective-permute-done.7
  41.9 0.7 collective-permute-done.8
  43.8 2.6 %collective-permute-start.11 = (bf16[8,2048]{1,0:T(8,128)(2,1)S(1)}, bf16[8,2048]{1,0:T(8,128)(2,1)S(1)}, u32[]{:S(2)}, u32[]{:S(2)}) collective-permute-start(bf16[8,2048]{1,0:T(8,128)(2,1)S(1)} %divide_convert_fusion.after_ref.refs_0_), channel_id=1, source_target_pairs={{0,12},{4,0},{8,4},{12,8},{1,13},{5,1},{9,5},{13,9},{2,14},{6,2},{... | collective-permute-start | bytes 98312 | tf_op jit(solution)/shard_map/ppermute | solution.py:22
  46.4 0.5 collective-permute-start.9
  47.0 4.2 %shard_map.134.refs_5_.refs_0_ = bf16[768,2,3584]{2,1,0:T(2,128)(2,1)S(1)} custom-call(bf16[8,2048]{1,0:T(8,128)(2,1)S(1)} %divide_convert_fusion.after_ref.refs_0_, bf16[2048,2,3584]{2,1,0:T(2,128)(2,1)} %refs_2_.1), custom_call_target="tpu_custom_call" | custom-call | flops 3853516800 | tf_op jit(solution)/shard_map/pallas_call | solution.py:103
  51.2 0.9 collective-permute-done.9.refs_1_
  52.2 2.1 %shard_map.135 = (bf16[32,2048]{1,0:T(8,128)(2,1)S(1)}, bf16[32,2048]{1,0:T(8,128)(2,1)}) custom-call(bf16[8,2048]{1,0:T(8,128)(2,1)S(1)} %divide_convert_fusion.after_ref.refs_0_, bf16[8,2048]{1,0:T(8,128)(2,1)S(1)} %collective-permute-done.9.refs_1_, bf16[8,2048]{1,0:T(8,128)(2,1)S(1)} %collective-permute-done.10.refs_2_, ...), custom_call_target="tpu_custom_call" | custom-call | flops 268435456 | bytes 8388608 | tf_op jit(solution)/shard_map/pallas_call | solution.py:144
  54.3 1.3 %collective-permute-done.12.r_ref = bf16[32,2048]{1,0:T(8,128)(2,1)S(1)} collective-permute-done((bf16[32,2048]{1,0:T(8,128)(2,1)S(1)}, bf16[32,2048]{1,0:T(8,128)(2,1)S(1)}, u32[]{:S(2)}, u32[]{:S(2)}) %collective-permute-start.12) | collective-permute-done | bytes 131104 | tf_op jit(solution)/shard_map/ppermute | solution.py:404
  55.7 1.5 %collective-permute-start.13 = (bf16[32,2048]{1,0:T(8,128)(2,1)S(1)}, bf16[32,2048]{1,0:T(8,128)(2,1)S(1)}, u32[]{:S(2)}, u32[]{:S(2)}) collective-permute-start(bf16[32,2048]{1,0:T(8,128)(2,1)S(1)} %shard_map.136.after_ref.near_ref), channel_id=1, source_target_pairs={{0,2},{1,3},{2,0},{3,1},{4,6},{5,7},{6,4},{7,5},{8,10},{9,11},{10,... | collective-permute-start | bytes 393224 | tf_op jit(solution)/shard_map/ppermute | solution.py:404
  57.2 3.7 %shard_map.137.refs_1_ = bf16[640,2,3584]{2,1,0:T(2,128)(2,1)S(1)} custom-call(bf16[32,2048]{1,0:T(8,128)(2,1)S(1)} %shard_map.136.after_ref.near_ref, bf16[2048,2,3584]{2,1,0:T(2,128)(2,1)} %refs_2_.1), custom_call_target="tpu_custom_call" | custom-call | flops 3211264000 | tf_op jit(solution)/shard_map/pallas_call | solution.py:103
  60.9 0.4 collective-permute-done.13.far_ref
  61.3 7.2 %shard_map.138 = (bf16[32,2048]{1,0:T(8,128)(2,1)S(1)}, bf16[16,3712]{1,0:T(8,128)(2,1)S(1)}, bf16[16,3712]{1,0:T(8,128)(2,1)S(1)}, bf16[16,3712]{1,0:T(8,128)(2,1)S(1)}, bf16[16,3712]{1,0:T(8,128)(2,1)S(1)}) custom-call(bf16[32,2048]{1,0:T(8,128)(2,1)S(1)} %copy-done.1, bf16[32,2048]{1,0:T(8,128)(2,1)S(1)} %shard_map.136.after_ref.near_ref, ...), custom_call_target="tpu_custom_call" | custom-call | flops 1879048192 | bytes 29360128 | tf_op jit(solution)/shard_map/pallas_call | solution.py:340
  68.6 2.0 %collective-permute-start.14 = (bf16[16,3712]{1,0:T(8,128)(2,1)S(1)}, bf16[16,3712]{1,0:T(8,128)(2,1)S(1)}, u32[]{:S(2)}, u32[]{:S(2)}) collective-permute-start(bf16[16,3712]{1,0:T(8,128)(2,1)S(1)} %get-tuple-element.21), channel_id=1, source_target_pairs={{0,4},{4,8},{8,12},{12,0},{1,5},{5,9},{9,13},{13,1},{2,6},{6,10},{... | collective-permute-start | bytes 356360 | tf_op jit(solution)/shard_map/ppermute | solution.py:22
  70.6 1.0 %collective-permute-start.15 = (bf16[16,3712]{1,0:T(8,128)(2,1)S(1)}, bf16[16,3712]{1,0:T(8,128)(2,1)S(1)}, u32[]{:S(2)}, u32[]{:S(2)}) collective-permute-start(bf16[16,3712]{1,0:T(8,128)(2,1)S(1)} %get-tuple-element.22), channel_id=1, source_target_pairs={{0,8},{4,12},{8,0},{12,4},{1,9},{5,13},{9,1},{13,5},{2,10},{6,14},... | collective-permute-start | bytes 356360 | tf_op jit(solution)/shard_map/ppermute | solution.py:22
  71.6 1.4 %collective-permute-start.16 = (bf16[16,3712]{1,0:T(8,128)(2,1)S(1)}, bf16[16,3712]{1,0:T(8,128)(2,1)S(1)}, u32[]{:S(2)}, u32[]{:S(2)}) collective-permute-start(bf16[16,3712]{1,0:T(8,128)(2,1)S(1)} %get-tuple-element.23), channel_id=1, source_target_pairs={{0,12},{4,0},{8,4},{12,8},{1,13},{5,1},{9,5},{13,9},{2,14},{6,2},{... | collective-permute-start | bytes 356360 | tf_op jit(solution)/shard_map/ppermute | solution.py:22
  73.0 5.3 %shard_map.139.refs_4_ = bf16[3584,2048]{1,0:T(8,128)(2,1)S(1)} custom-call(bf16[16,3712]{1,0:T(8,128)(2,1)S(1)} %get-tuple-element.20.after_ref.refs_0_, bf16[3584,2048]{1,0:T(8,128)(2,1)} %w_ref.7), custom_call_target="tpu_custom_call" | custom-call | flops 5138022400 | tf_op jit(solution)/shard_map/pallas_call | solution.py:103
  78.3 1.9 %collective-permute-done.15.refs_2_ = bf16[16,3712]{1,0:T(8,128)(2,1)S(1)} collective-permute-done((bf16[16,3712]{1,0:T(8,128)(2,1)S(1)}, bf16[16,3712]{1,0:T(8,128)(2,1)S(1)}, u32[]{:S(2)}, u32[]{:S(2)}) %collective-permute-start.15) | collective-permute-done | bytes 118816 | tf_op jit(solution)/shard_map/ppermute | solution.py:22
  80.4 3.4 %collective-permute-start.19 = (bf16[8,3584]{1,0:T(8,128)(2,1)S(1)}, bf16[8,3584]{1,0:T(8,128)(2,1)S(1)}, u32[]{:S(2)}, u32[]{:S(2)}) collective-permute-start(bf16[8,3584]{1,0:T(8,128)(2,1)S(1)} %shard_map.140.refs_0_), channel_id=1, source_target_pairs={{0,12},{4,0},{8,4},{12,8},{1,13},{5,1},{9,5},{13,9},{2,14},{6,2},{... | collective-permute-start | bytes 172040 | tf_op jit(solution)/shard_map/ppermute | solution.py:22
  83.7 1.2 %collective-permute-start.18 = (bf16[8,3584]{1,0:T(8,128)(2,1)S(1)}, bf16[8,3584]{1,0:T(8,128)(2,1)S(1)}, u32[]{:S(2)}, u32[]{:S(2)}) collective-permute-start(bf16[8,3584]{1,0:T(8,128)(2,1)S(1)} %shard_map.140.refs_0_), channel_id=1, source_target_pairs={{0,8},{4,12},{8,0},{12,4},{1,9},{5,13},{9,1},{13,5},{2,10},{6,14},... | collective-permute-start | bytes 172040 | tf_op jit(solution)/shard_map/ppermute | solution.py:22
  84.9 1.2 %collective-permute-done.19.refs_3_ = bf16[8,3584]{1,0:T(8,128)(2,1)S(1)} collective-permute-done((bf16[8,3584]{1,0:T(8,128)(2,1)S(1)}, bf16[8,3584]{1,0:T(8,128)(2,1)S(1)}, u32[]{:S(2)}, u32[]{:S(2)}) %collective-permute-start.19) | collective-permute-done | bytes 57376 | tf_op jit(solution)/shard_map/ppermute | solution.py:22
  86.1 3.8 %collective-permute-done.18.refs_2_ = bf16[8,3584]{1,0:T(8,128)(2,1)S(1)} collective-permute-done((bf16[8,3584]{1,0:T(8,128)(2,1)S(1)}, bf16[8,3584]{1,0:T(8,128)(2,1)S(1)}, u32[]{:S(2)}, u32[]{:S(2)}) %collective-permute-start.18) | collective-permute-done | bytes 57376 | tf_op jit(solution)/shard_map/ppermute | solution.py:22
  89.9 0.9 collective-permute-done.17.refs_1_
  90.9 3.0 %shard_map.141.l_ref = bf16[32,2048]{1,0:T(8,128)(2,1)S(1)} custom-call(bf16[8,3584]{1,0:T(8,128)(2,1)S(1)} %shard_map.140.refs_0_, bf16[8,3584]{1,0:T(8,128)(2,1)S(1)} %collective-permute-done.17.refs_1_, bf16[8,3584]{1,0:T(8,128)(2,1)S(1)} %collective-permute-done.18.refs_2_, bf16[8,3584]{1,0:T(8,128)(2,1)S(1)} %collective-permute-done.19.refs_3_, ...), custom_call_target="tpu_custom_call" | custom-call | flops 469762048 | bytes 14680064 | tf_op jit(solution)/shard_map/pallas_call | solution.py:144
  93.9 1.3 %collective-permute-done.20.r_ref = bf16[32,2048]{1,0:T(8,128)(2,1)S(1)} collective-permute-done((bf16[32,2048]{1,0:T(8,128)(2,1)S(1)}, bf16[32,2048]{1,0:T(8,128)(2,1)S(1)}, u32[]{:S(2)}, u32[]{:S(2)}) %collective-permute-start.20) | collective-permute-done | bytes 131104 | tf_op jit(solution)/shard_map/ppermute | solution.py:404
  95.3 1.3 %collective-permute-start.21 = (bf16[32,2048]{1,0:T(8,128)(2,1)S(1)}, bf16[32,2048]{1,0:T(8,128)(2,1)S(1)}, u32[]{:S(2)}, u32[]{:S(2)}) collective-permute-start(bf16[32,2048]{1,0:T(8,128)(2,1)S(1)} %shard_map.142), channel_id=1, source_target_pairs={{0,2},{1,3},{2,0},{3,1},{4,6},{5,7},{6,4},{7,5},{8,10},{9,11},{10,... | collective-permute-start | bytes 393224 | tf_op jit(solution)/shard_map/ppermute | solution.py:404
  96.6 4.3 %collective-permute-done.21 = bf16[32,2048]{1,0:T(8,128)(2,1)S(1)} collective-permute-done((bf16[32,2048]{1,0:T(8,128)(2,1)S(1)}, bf16[32,2048]{1,0:T(8,128)(2,1)S(1)}, u32[]{:S(2)}, u32[]{:S(2)}) %collective-permute-start.21) | collective-permute-done | bytes 131104 | tf_op jit(solution)/shard_map/ppermute | solution.py:404
  100.9 0.7 add_convert_fusion
  (101 shorter events, 3.9 us)
Async XLA Ops:
  0.6 14.3 %copy-start.5 = (s32[32]{0:T(128)S(1)}, s32[32]{0:T(128)}, u32[]{:S(2)}) copy-start(s32[32]{0:T(128)} %param.13) | copy-start | bytes 388
  0.6 14.6 %copy-start.4 = (s32[32,128]{1,0:T(8,128)S(1)}, s32[32,128]{1,0:T(8,128)}, u32[]{:S(2)}) copy-start(s32[32,128]{1,0:T(8,128)} %param.14) | copy-start | bytes 49156
  7.9 12.9 %collective-permute-start = (f32[8,2688]{1,0:T(8,128)}, f32[8,2688]{1,0:T(8,128)S(1)}, u32[]{:S(2)}, u32[]{:S(2)}) collective-permute-start(f32[8,2688]{1,0:T(8,128)} %get-tuple-element.14), channel_id=1, source_target_pairs={{0,4},{4,8},{8,12},{12,0},{1,5},{5,9},{9,13},{13,1},{2,6},{6,10},{... | collective-permute-start | bytes 258056 | tf_op jit(solution)/shard_map/ppermute | solution.py:22
  11.0 9.8 %collective-permute-start.1 = (f32[8,2688]{1,0:T(8,128)}, f32[8,2688]{1,0:T(8,128)S(1)}, u32[]{:S(2)}, u32[]{:S(2)}) collective-permute-start(f32[8,2688]{1,0:T(8,128)} %get-tuple-element.15), channel_id=1, source_target_pairs={{0,8},{4,12},{8,0},{12,4},{1,9},{5,13},{9,1},{13,5},{2,10},{6,14},... | collective-permute-start | bytes 258056 | tf_op jit(solution)/shard_map/ppermute | solution.py:22
  13.6 7.2 %collective-permute-start.2 = (f32[8,2688]{1,0:T(8,128)}, f32[8,2688]{1,0:T(8,128)S(1)}, u32[]{:S(2)}, u32[]{:S(2)}) collective-permute-start(f32[8,2688]{1,0:T(8,128)} %get-tuple-element.16), channel_id=1, source_target_pairs={{0,12},{4,0},{8,4},{12,8},{1,13},{5,1},{9,5},{13,9},{2,14},{6,2},{... | collective-permute-start | bytes 258056 | tf_op jit(solution)/shard_map/ppermute | solution.py:22
  16.3 0.9 copy-start.2
  20.7 9.2 %copy-start = (bf16[2048,2048]{1,0:T(8,128)(2,1)}, bf16[2048,2048]{1,0:T(8,128)(2,1)S(1)}, u32[]{:S(2)}) copy-start(bf16[2048,2048]{1,0:T(8,128)(2,1)S(1)} %shard_map.132.refs_6_.refs_4_) | copy-start | bytes 25165828
  20.7 7.6 %slice-start.2 = ((s8[5242880]{0:T(1024)(128)(4,1)}), s8[4194304]{0:T(1024)(128)(4,1)S(1)}, s32[]{:S(2)}) async-start(s8[5242880]{0:T(1024)(128)(4,1)} %bitcast.159), calls=%async_computation.2 | async-start | bytes 8388608
  20.8 7.5 %slice-start.3 = ((s8[5242880]{0:T(1024)(128)(4,1)}), s8[1048576]{0:T(1024)(128)(4,1)S(1)}, s32[]{:S(2)}) async-start(s8[5242880]{0:T(1024)(128)(4,1)} %bitcast.159), calls=%async_computation.3 | async-start | bytes 2097152
  21.0 6.9 %collective-permute-start.5 = (bf16[8,2560]{1,0:T(8,128)(2,1)S(1)}, bf16[8,2560]{1,0:T(8,128)(2,1)S(1)}, u32[]{:S(2)}, u32[]{:S(2)}) collective-permute-start(bf16[8,2560]{1,0:T(8,128)(2,1)S(1)} %shard_map.133), channel_id=1, source_target_pairs={{0,4},{4,8},{8,12},{12,0},{1,5},{5,9},{9,13},{13,1},{2,6},{6,10},{... | collective-permute-start | bytes 122888 | tf_op jit(solution)/shard_map/ppermute | solution.py:22
  22.1 5.8 %collective-permute-start.4 = (bf16[8,2560]{1,0:T(8,128)(2,1)S(1)}, bf16[8,2560]{1,0:T(8,128)(2,1)S(1)}, u32[]{:S(2)}, u32[]{:S(2)}) collective-permute-start(bf16[8,2560]{1,0:T(8,128)(2,1)S(1)} %shard_map.133), channel_id=1, source_target_pairs={{0,8},{4,12},{8,0},{12,4},{1,9},{5,13},{9,1},{13,5},{2,10},{6,14},... | collective-permute-start | bytes 122888 | tf_op jit(solution)/shard_map/ppermute | solution.py:22
  23.9 4.0 %collective-permute-start.3 = (bf16[8,2560]{1,0:T(8,128)(2,1)S(1)}, bf16[8,2560]{1,0:T(8,128)(2,1)S(1)}, u32[]{:S(2)}, u32[]{:S(2)}) collective-permute-start(bf16[8,2560]{1,0:T(8,128)(2,1)S(1)} %shard_map.133), channel_id=1, source_target_pairs={{0,12},{4,0},{8,4},{12,8},{1,13},{5,1},{9,5},{13,9},{2,14},{6,2},{... | collective-permute-start | bytes 122888 | tf_op jit(solution)/shard_map/ppermute | solution.py:22
  35.2 5.8 %collective-permute-start.6 = (bf16[8,2176]{1,0:T(8,128)(2,1)S(1)}, bf16[8,2176]{1,0:T(8,128)(2,1)S(1)}, u32[]{:S(2)}, u32[]{:S(2)}) collective-permute-start(bf16[8,2176]{1,0:T(8,128)(2,1)S(1)} %get-tuple-element.31), channel_id=1, source_target_pairs={{0,4},{4,8},{8,12},{12,0},{1,5},{5,9},{9,13},{13,1},{2,6},{6,10},{... | collective-permute-start | bytes 104456 | tf_op jit(solution)/shard_map/ppermute | solution.py:22
  36.8 4.9 %collective-permute-start.7 = (bf16[8,2176]{1,0:T(8,128)(2,1)S(1)}, bf16[8,2176]{1,0:T(8,128)(2,1)S(1)}, u32[]{:S(2)}, u32[]{:S(2)}) collective-permute-start(bf16[8,2176]{1,0:T(8,128)(2,1)S(1)} %get-tuple-element.32), channel_id=1, source_target_pairs={{0,8},{4,12},{8,0},{12,4},{1,9},{5,13},{9,1},{13,5},{2,10},{6,14},... | collective-permute-start | bytes 104456 | tf_op jit(solution)/shard_map/ppermute | solution.py:22
  38.6 3.9 %collective-permute-start.8 = (bf16[8,2176]{1,0:T(8,128)(2,1)S(1)}, bf16[8,2176]{1,0:T(8,128)(2,1)S(1)}, u32[]{:S(2)}, u32[]{:S(2)}) collective-permute-start(bf16[8,2176]{1,0:T(8,128)(2,1)S(1)} %get-tuple-element.33), channel_id=1, source_target_pairs={{0,12},{4,0},{8,4},{12,8},{1,13},{5,1},{9,5},{13,9},{2,14},{6,2},{... | collective-permute-start | bytes 104456 | tf_op jit(solution)/shard_map/ppermute | solution.py:22
  43.7 8.5 %slice-start = ((s8[8388608]{0:T(1024)(128)(4,1)}), s8[4194304]{0:T(1024)(128)(4,1)S(1)}, s32[]{:S(2)}) async-start(s8[8388608]{0:T(1024)(128)(4,1)} %bitcast.157), calls=%async_computation | async-start | bytes 8388608
  43.7 8.4 %slice-start.1 = ((s8[8388608]{0:T(1024)(128)(4,1)}), s8[4194304]{0:T(1024)(128)(4,1)S(1)}, s32[]{:S(2)}) async-start(s8[8388608]{0:T(1024)(128)(4,1)} %bitcast.157), calls=%async_computation.1 | async-start | bytes 8388608
  43.8 7.5 %collective-permute-start.11 = (bf16[8,2048]{1,0:T(8,128)(2,1)S(1)}, bf16[8,2048]{1,0:T(8,128)(2,1)S(1)}, u32[]{:S(2)}, u32[]{:S(2)}) collective-permute-start(bf16[8,2048]{1,0:T(8,128)(2,1)S(1)} %divide_convert_fusion.after_ref.refs_0_), channel_id=1, source_target_pairs={{0,12},{4,0},{8,4},{12,8},{1,13},{5,1},{9,5},{13,9},{2,14},{6,2},{... | collective-permute-start | bytes 98312 | tf_op jit(solution)/shard_map/ppermute | solution.py:22
  46.3 4.9 %collective-permute-start.10 = (bf16[8,2048]{1,0:T(8,128)(2,1)S(1)}, bf16[8,2048]{1,0:T(8,128)(2,1)S(1)}, u32[]{:S(2)}, u32[]{:S(2)}) collective-permute-start(bf16[8,2048]{1,0:T(8,128)(2,1)S(1)} %divide_convert_fusion.after_ref.refs_0_), channel_id=1, source_target_pairs={{0,8},{4,12},{8,0},{12,4},{1,9},{5,13},{9,1},{13,5},{2,10},{6,14},... | collective-permute-start | bytes 98312 | tf_op jit(solution)/shard_map/ppermute | solution.py:22
  46.4 5.7 %collective-permute-start.9 = (bf16[8,2048]{1,0:T(8,128)(2,1)S(1)}, bf16[8,2048]{1,0:T(8,128)(2,1)S(1)}, u32[]{:S(2)}, u32[]{:S(2)}) collective-permute-start(bf16[8,2048]{1,0:T(8,128)(2,1)S(1)} %divide_convert_fusion.after_ref.refs_0_), channel_id=1, source_target_pairs={{0,4},{4,8},{8,12},{12,0},{1,5},{5,9},{9,13},{13,1},{2,6},{6,10},{... | collective-permute-start | bytes 98312 | tf_op jit(solution)/shard_map/ppermute | solution.py:22
  54.3 1.3 %collective-permute-start.12 = (bf16[32,2048]{1,0:T(8,128)(2,1)S(1)}, bf16[32,2048]{1,0:T(8,128)(2,1)S(1)}, u32[]{:S(2)}, u32[]{:S(2)}) collective-permute-start(bf16[32,2048]{1,0:T(8,128)(2,1)S(1)} %get-tuple-element.18.l_ref), channel_id=1, source_target_pairs={{0,1},{1,0},{2,3},{3,2},{4,5},{5,4},{6,7},{7,6},{8,9},{9,8},{10,11... | collective-permute-start | bytes 393224 | tf_op jit(solution)/shard_map/ppermute | solution.py:404
  55.7 5.6 %copy-start.1 = (bf16[32,2048]{1,0:T(8,128)(2,1)S(1)}, bf16[32,2048]{1,0:T(8,128)(2,1)}, u32[]{:S(2)}) copy-start(bf16[32,2048]{1,0:T(8,128)(2,1)} %hid_ref.3) | copy-start | bytes 393220
  55.7 5.6 %copy-start.3 = (bf16[2048]{0:T(1024)(128)(2,1)S(1)}, bf16[2048]{0:T(1024)(128)(2,1)}, u32[]{:S(2)}) copy-start(bf16[2048]{0:T(1024)(128)(2,1)} %gain_ref.3) | copy-start | bytes 12292
  55.7 5.6 %collective-permute-start.13 = (bf16[32,2048]{1,0:T(8,128)(2,1)S(1)}, bf16[32,2048]{1,0:T(8,128)(2,1)S(1)}, u32[]{:S(2)}, u32[]{:S(2)}) collective-permute-start(bf16[32,2048]{1,0:T(8,128)(2,1)S(1)} %shard_map.136.after_ref.near_ref), channel_id=1, source_target_pairs={{0,2},{1,3},{2,0},{3,1},{4,6},{5,7},{6,4},{7,5},{8,10},{9,11},{10,... | collective-permute-start | bytes 393224 | tf_op jit(solution)/shard_map/ppermute | solution.py:404
  68.6 9.7 %collective-permute-start.14 = (bf16[16,3712]{1,0:T(8,128)(2,1)S(1)}, bf16[16,3712]{1,0:T(8,128)(2,1)S(1)}, u32[]{:S(2)}, u32[]{:S(2)}) collective-permute-start(bf16[16,3712]{1,0:T(8,128)(2,1)S(1)} %get-tuple-element.21), channel_id=1, source_target_pairs={{0,4},{4,8},{8,12},{12,0},{1,5},{5,9},{9,13},{13,1},{2,6},{6,10},{... | collective-permute-start | bytes 356360 | tf_op jit(solution)/shard_map/ppermute | solution.py:22
  70.6 9.6 %collective-permute-start.15 = (bf16[16,3712]{1,0:T(8,128)(2,1)S(1)}, bf16[16,3712]{1,0:T(8,128)(2,1)S(1)}, u32[]{:S(2)}, u32[]{:S(2)}) collective-permute-start(bf16[16,3712]{1,0:T(8,128)(2,1)S(1)} %get-tuple-element.22), channel_id=1, source_target_pairs={{0,8},{4,12},{8,0},{12,4},{1,9},{5,13},{9,1},{13,5},{2,10},{6,14},... | collective-permute-start | bytes 356360 | tf_op jit(solution)/shard_map/ppermute | solution.py:22
  71.6 8.6 %collective-permute-start.16 = (bf16[16,3712]{1,0:T(8,128)(2,1)S(1)}, bf16[16,3712]{1,0:T(8,128)(2,1)S(1)}, u32[]{:S(2)}, u32[]{:S(2)}) collective-permute-start(bf16[16,3712]{1,0:T(8,128)(2,1)S(1)} %get-tuple-element.23), channel_id=1, source_target_pairs={{0,12},{4,0},{8,4},{12,8},{1,13},{5,1},{9,5},{13,9},{2,14},{6,2},{... | collective-permute-start | bytes 356360 | tf_op jit(solution)/shard_map/ppermute | solution.py:22
  80.4 5.7 %collective-permute-start.19 = (bf16[8,3584]{1,0:T(8,128)(2,1)S(1)}, bf16[8,3584]{1,0:T(8,128)(2,1)S(1)}, u32[]{:S(2)}, u32[]{:S(2)}) collective-permute-start(bf16[8,3584]{1,0:T(8,128)(2,1)S(1)} %shard_map.140.refs_0_), channel_id=1, source_target_pairs={{0,12},{4,0},{8,4},{12,8},{1,13},{5,1},{9,5},{13,9},{2,14},{6,2},{... | collective-permute-start | bytes 172040 | tf_op jit(solution)/shard_map/ppermute | solution.py:22
  83.7 6.2 %collective-permute-start.18 = (bf16[8,3584]{1,0:T(8,128)(2,1)S(1)}, bf16[8,3584]{1,0:T(8,128)(2,1)S(1)}, u32[]{:S(2)}, u32[]{:S(2)}) collective-permute-start(bf16[8,3584]{1,0:T(8,128)(2,1)S(1)} %shard_map.140.refs_0_), channel_id=1, source_target_pairs={{0,8},{4,12},{8,0},{12,4},{1,9},{5,13},{9,1},{13,5},{2,10},{6,14},... | collective-permute-start | bytes 172040 | tf_op jit(solution)/shard_map/ppermute | solution.py:22
  84.9 6.0 %collective-permute-start.17 = (bf16[8,3584]{1,0:T(8,128)(2,1)S(1)}, bf16[8,3584]{1,0:T(8,128)(2,1)S(1)}, u32[]{:S(2)}, u32[]{:S(2)}) collective-permute-start(bf16[8,3584]{1,0:T(8,128)(2,1)S(1)} %shard_map.140.refs_0_), channel_id=1, source_target_pairs={{0,4},{4,8},{8,12},{12,0},{1,5},{5,9},{9,13},{13,1},{2,6},{6,10},{... | collective-permute-start | bytes 172040 | tf_op jit(solution)/shard_map/ppermute | solution.py:22
  93.9 1.4 %collective-permute-start.20 = (bf16[32,2048]{1,0:T(8,128)(2,1)S(1)}, bf16[32,2048]{1,0:T(8,128)(2,1)S(1)}, u32[]{:S(2)}, u32[]{:S(2)}) collective-permute-start(bf16[32,2048]{1,0:T(8,128)(2,1)S(1)} %shard_map.141.l_ref), channel_id=1, source_target_pairs={{0,1},{1,0},{2,3},{3,2},{4,5},{5,4},{6,7},{7,6},{8,9},{9,8},{10,11... | collective-permute-start | bytes 393224 | tf_op jit(solution)/shard_map/ppermute | solution.py:404
  95.3 5.6 %collective-permute-start.21 = (bf16[32,2048]{1,0:T(8,128)(2,1)S(1)}, bf16[32,2048]{1,0:T(8,128)(2,1)S(1)}, u32[]{:S(2)}, u32[]{:S(2)}) collective-permute-start(bf16[32,2048]{1,0:T(8,128)(2,1)S(1)} %shard_map.142), channel_id=1, source_target_pairs={{0,2},{1,3},{2,0},{3,1},{4,6},{5,7},{6,4},{7,5},{8,10},{9,11},{10,... | collective-permute-start | bytes 393224 | tf_op jit(solution)/shard_map/ppermute | solution.py:404

commit v4 on v3

--- a/solution.py
+++ b/solution.py
@@ -127,7 +127,7 @@
 def gathered_dot(parts, weight, n_mem, keep, beside=()):
     rows = parts[0].shape[0] * n_mem
     depth, width = weight.shape
-    tile = 512 if width % 512 == 0 else 128
+    tile = width
 
     def kernel(*refs):
         part_refs, w_ref = refs[:n_mem], refs[n_mem]
@@ -171,7 +171,7 @@
     q_width, kv_width = w_query.shape[1], w_kv.shape[2]
     rows = req // n_mem
     body = q_width + 2 * kv_width
-    chunks, ahead = 8, 3
+    chunks, ahead = 8, 5
     step = depth // chunks
 
     def kernel(hid_ref, gain_ref, wq_ref, wkv_ref, *refs):
@@ -199,14 +199,6 @@
         acc[:, body:] = jnp.broadcast_to(jnp.sum(wide * wide, 1, keepdims=True), (req, 128))
         normed = to_bf16(wide * gain_buf[...].astype(jnp.float32).reshape(1, depth))
         unfold(normed, spread)
-        kv_copy.wait()
-        both = jnp.dot(
-            spread[...],
-            kv_buf[...].reshape(2 * depth, kv_width),
-            preferred_element_type=jnp.float32,
-        )
-        acc[:, q_width : q_width + kv_width] = both[:req]
-        acc[:, q_width + kv_width : body] = both[req:]
         for i, copy in enumerate(copies):
             copy.wait()
             if i + ahead < chunks:
@@ -217,6 +209,14 @@
                 preferred_element_type=jnp.float32,
             )
             acc[:, :q_width] = term if i == 0 else acc[:, :q_width] + term
+        kv_copy.wait()
+        both = jnp.dot(
+            spread[...],
+            kv_buf[...].reshape(2 * depth, kv_width),
+            preferred_element_type=jnp.float32,
+        )
+        acc[:, q_width : q_width + kv_width] = both[:req]
+        acc[:, q_width + kv_width : body] = both[req:]
         me = lax.axis_index("mem")
         for step_to in range(n_mem):
             at = pl.multiple_of(lax.rem(me + step_to, n_mem) * rows, rows)

time: 102 us -> 100 us (0.980)
  Pallas kernels: 36.8 us -> 35.2 us
    pallas_call x1, Pallas kernels: 7.27 us -> 6.15 us  [query_parts(): pl.pallas_call(kernel, in_specs=[pl.BlockSpec(memory_space=pltpu.HBM)] *...]
  transfers between devices with their start and end apart: 22 -> 22, of which waited for: 13 -> 13; matrix products, arithmetic and copies ran while one was open for 2% -> 2% of each run, Pallas kernels for 16% -> 17%
where the time goes in v4:
time: 100 us
  Pallas kernels  35.2 us (35%)
  starting transfers between devices  30.2 us (30%)
  waiting for transfers between devices  22.1 us (22%)
  matrix products  5.72 us (6%)
  other arithmetic  3.04 us (3%)
  local copies, waits for them, and re-layouts  2.84 us (3%)
  between operations  1.13 us (1%)
    ppermute x18, starting transfers between devices, shifted(): return lax.ppermute(x, axis, [(i, (i + step) % n) for i in range(n)])  27.4 us
    pallas_call x4, Pallas kernels, fetch(): pl.pallas_call(kernel, in_specs=[pl.BlockSpec(memory_space=pl.ANY)] * 2,...  16.7 us
    ppermute x18, waiting for transfers between devices, shifted(): return lax.ppermute(x, axis, [(i, (i + step) % n) for i in range(n)])  14.7 us
    ppermute x4, waiting for transfers between devices, pairwise(): far = lax.ppermute(near, 'comp', [(i, i ^ step) for i in range(n)])  7.42 us
    pallas_call x1, Pallas kernels, gate_up_parts(): pl.pallas_call(kernel, in_specs=whole(4 + n_held) + [pl.BlockSpec(memory_...  7.25 us
    pallas_call x1, Pallas kernels, query_parts(): pl.pallas_call(kernel, in_specs=[pl.BlockSpec(memory_space=pltpu.HBM)] *...  6.15 us
    pallas_call x2, Pallas kernels, gathered_dot(): pl.pallas_call(kernel, in_specs=whole(n_mem + 1) + [pl.BlockSpec(memory_s...  4.69 us
    dot_general x1, matrix products, slot_stats(): jnp.einsum('skgb,sbkd->skgd', weights.astype(jnp.bfloat16), value_rows, p...  3.37 us
  transfers between devices with their start and end apart: 22, of which 13 were waited for; matrix products, arithmetic and copies ran while one was open for 2% of the time, Pallas kernels for 17%

profile of v4, /device:TPU:0, one launch (start us, length us, event | category | flops | bytes accessed | tf_op | source)
XLA Modules:
  0.0 100.2 jit_solution(16371178322261437968)
XLA Ops:
  0.7 6.2 %shard_map.131 = (f32[8,2688]{1,0:T(8,128)}, f32[8,2688]{1,0:T(8,128)}, f32[8,2688]{1,0:T(8,128)}, f32[8,2688]{1,0:T(8,128)}) custom-call(bf16[32,2048]{1,0:T(8,128)(2,1)} %hid_ref.3, bf16[2048]{0:T(1024)(128)(2,1)} %gain_ref.2, bf16[2048,2048]{1,0:T(8,128)(2,1)} %wq_ref.1, bf16[2048,2,256]{2,1,0:T(2,128)(2,1)} %wkv_ref.1), custom_call_target="tpu_custom_call" | custom-call | flops 268435456 | bytes 8388608 | tf_op jit(solution)/shard_map/pallas_call | solution.py:225
  6.8 3.1 %collective-permute-start = (f32[8,2688]{1,0:T(8,128)}, f32[8,2688]{1,0:T(8,128)S(1)}, u32[]{:S(2)}, u32[]{:S(2)}) collective-permute-start(f32[8,2688]{1,0:T(8,128)} %get-tuple-element.14), channel_id=1, source_target_pairs={{0,4},{4,8},{8,12},{12,0},{1,5},{5,9},{9,13},{13,1},{2,6},{6,10},{... | collective-permute-start | bytes 258056 | tf_op jit(solution)/shard_map/ppermute | solution.py:22
  9.9 2.6 %collective-permute-start.1 = (f32[8,2688]{1,0:T(8,128)}, f32[8,2688]{1,0:T(8,128)S(1)}, u32[]{:S(2)}, u32[]{:S(2)}) collective-permute-start(f32[8,2688]{1,0:T(8,128)} %get-tuple-element.15), channel_id=1, source_target_pairs={{0,8},{4,12},{8,0},{12,4},{1,9},{5,13},{9,1},{13,5},{2,10},{6,14},... | collective-permute-start | bytes 258056 | tf_op jit(solution)/shard_map/ppermute | solution.py:22
  12.5 1.4 %collective-permute-start.2 = (f32[8,2688]{1,0:T(8,128)}, f32[8,2688]{1,0:T(8,128)S(1)}, u32[]{:S(2)}, u32[]{:S(2)}) collective-permute-start(f32[8,2688]{1,0:T(8,128)} %get-tuple-element.16), channel_id=1, source_target_pairs={{0,12},{4,0},{8,4},{12,8},{1,13},{5,1},{9,5},{13,9},{2,14},{6,2},{... | collective-permute-start | bytes 258056 | tf_op jit(solution)/shard_map/ppermute | solution.py:22
  14.1 0.6 fusion.20
  14.7 0.3 select_reduce_fusion
  15.2 0.9 copy-done.2
  16.1 3.5 %shard_map.132.refs_6_.refs_4_ = bf16[2048,2048]{1,0:T(8,128)(2,1)S(1)} custom-call(f32[8,2688]{1,0:T(8,128)S(1)} %copy-done.2, bf16[2048,2048]{1,0:T(8,128)(2,1)} %w_ref.4), custom_call_target="tpu_custom_call" | custom-call | flops 2936012800 | tf_op jit(solution)/shard_map/pallas_call | solution.py:103
  19.9 1.1 %collective-permute-start.5 = (bf16[8,2560]{1,0:T(8,128)(2,1)S(1)}, bf16[8,2560]{1,0:T(8,128)(2,1)S(1)}, u32[]{:S(2)}, u32[]{:S(2)}) collective-permute-start(bf16[8,2560]{1,0:T(8,128)(2,1)S(1)} %shard_map.133), channel_id=1, source_target_pairs={{0,4},{4,8},{8,12},{12,0},{1,5},{5,9},{9,13},{13,1},{2,6},{6,10},{... | collective-permute-start | bytes 122888 | tf_op jit(solution)/shard_map/ppermute | solution.py:22
  21.0 1.8 %collective-permute-start.4 = (bf16[8,2560]{1,0:T(8,128)(2,1)S(1)}, bf16[8,2560]{1,0:T(8,128)(2,1)S(1)}, u32[]{:S(2)}, u32[]{:S(2)}) collective-permute-start(bf16[8,2560]{1,0:T(8,128)(2,1)S(1)} %shard_map.133), channel_id=1, source_target_pairs={{0,8},{4,12},{8,0},{12,4},{1,9},{5,13},{9,1},{13,5},{2,10},{6,14},... | collective-permute-start | bytes 122888 | tf_op jit(solution)/shard_map/ppermute | solution.py:22
  22.8 1.0 collective-permute-start.3
  23.9 2.9 %collective-permute-done.3 = bf16[8,2560]{1,0:T(8,128)(2,1)S(1)} collective-permute-done((bf16[8,2560]{1,0:T(8,128)(2,1)S(1)}, bf16[8,2560]{1,0:T(8,128)(2,1)S(1)}, u32[]{:S(2)}, u32[]{:S(2)}) %collective-permute-start.3) | collective-permute-done | bytes 40992 | tf_op jit(solution)/shard_map/ppermute | solution.py:22
  26.9 0.2 fusion.18
  27.2 1.6 %fusion.73 = (f32[40,2,8]{2,1,0:T(2,128)S(1)}, f32[40,2,8,256]{3,2,1,0:T(8,128)S(1)}) fusion(bf16[40,2,8,128]{3,2,1,0:T(8,128)(2,1)S(1)} %bitcast.161, pred[40,256]{1,0:T(8,128)(4,1)S(1)} %iota_compare_fusion.1, bf16[40,256,256]{2,1,0:T(8,128)(2,1)S(1)} %bitcast.160), kind=kOutput, calls=%fused_computation.132 | convolution fusion | flops 42433920 | bytes 6074880 | tf_op jit(solution)/shard_map/skgd,sbkd->skgb/dot_general | solution.py:430
  29.5 0.3 fusion.21
  30.2 3.4 %fusion.15 = f32[2,8,128,40]{2,1,0,3:T(8,128)S(1)} fusion(f32[40,2,8,256]{3,2,1,0:T(8,128)S(1)} %get-tuple-element.60, f32[40,2,8]{2,1,0:T(2,128)S(1)} %get-tuple-element.59, pred[40,256]{1,0:T(8,128)(4,1)S(1)} %iota_compare_fusion.1, f32[2,8,40]{1,0,2:T(2,128)S(1)} %copy.138, bf16[40,256,256]{2,1,0:T(8,128)(2,1)} %param.16), kind=kOutput, calls=%fused_computation.11 | convolution fusion | flops 42516480 | bytes 6241280 | tf_op jit(solution)/shard_map/skgb,sbkd->skgd/dot_general | solution.py:440
  33.6 0.3 convolution_convert_fusion.1
  34.1 1.6 %collective-permute-start.6 = (bf16[8,2176]{1,0:T(8,128)(2,1)S(1)}, bf16[8,2176]{1,0:T(8,128)(2,1)S(1)}, u32[]{:S(2)}, u32[]{:S(2)}) collective-permute-start(bf16[8,2176]{1,0:T(8,128)(2,1)S(1)} %get-tuple-element.31), channel_id=1, source_target_pairs={{0,4},{4,8},{8,12},{12,0},{1,5},{5,9},{9,13},{13,1},{2,6},{6,10},{... | collective-permute-start | bytes 104456 | tf_op jit(solution)/shard_map/ppermute | solution.py:22
  35.7 1.9 %collective-permute-start.7 = (bf16[8,2176]{1,0:T(8,128)(2,1)S(1)}, bf16[8,2176]{1,0:T(8,128)(2,1)S(1)}, u32[]{:S(2)}, u32[]{:S(2)}) collective-permute-start(bf16[8,2176]{1,0:T(8,128)(2,1)S(1)} %get-tuple-element.32), channel_id=1, source_target_pairs={{0,8},{4,12},{8,0},{12,4},{1,9},{5,13},{9,1},{13,5},{2,10},{6,14},... | collective-permute-start | bytes 104456 | tf_op jit(solution)/shard_map/ppermute | solution.py:22
  37.5 0.7 collective-permute-start.8
  38.2 1.6 %collective-permute-done.6 = bf16[8,2176]{1,0:T(8,128)(2,1)S(1)} collective-permute-done((bf16[8,2176]{1,0:T(8,128)(2,1)S(1)}, bf16[8,2176]{1,0:T(8,128)(2,1)S(1)}, u32[]{:S(2)}, u32[]{:S(2)}) %collective-permute-start.6) | collective-permute-done | bytes 34848 | tf_op jit(solution)/shard_map/ppermute | solution.py:22
  40.0 0.6 collective-permute-done.7
  40.7 0.7 collective-permute-done.8
  42.6 2.6 %collective-permute-start.11 = (bf16[8,2048]{1,0:T(8,128)(2,1)S(1)}, bf16[8,2048]{1,0:T(8,128)(2,1)S(1)}, u32[]{:S(2)}, u32[]{:S(2)}) collective-permute-start(bf16[8,2048]{1,0:T(8,128)(2,1)S(1)} %divide_convert_fusion.after_ref.refs_0_), channel_id=1, source_target_pairs={{0,12},{4,0},{8,4},{12,8},{1,13},{5,1},{9,5},{13,9},{2,14},{6,2},{... | collective-permute-start | bytes 98312 | tf_op jit(solution)/shard_map/ppermute | solution.py:22
  45.3 0.5 collective-permute-start.9
  45.8 4.2 %shard_map.134.refs_5_.refs_0_ = bf16[768,2,3584]{2,1,0:T(2,128)(2,1)S(1)} custom-call(bf16[8,2048]{1,0:T(8,128)(2,1)S(1)} %divide_convert_fusion.after_ref.refs_0_, bf16[2048,2,3584]{2,1,0:T(2,128)(2,1)} %refs_2_.1), custom_call_target="tpu_custom_call" | custom-call | flops 3853516800 | tf_op jit(solution)/shard_map/pallas_call | solution.py:103
  50.1 0.9 collective-permute-done.9.refs_1_
  51.0 2.1 %shard_map.135 = (bf16[32,2048]{1,0:T(8,128)(2,1)S(1)}, bf16[32,2048]{1,0:T(8,128)(2,1)}) custom-call(bf16[8,2048]{1,0:T(8,128)(2,1)S(1)} %divide_convert_fusion.after_ref.refs_0_, bf16[8,2048]{1,0:T(8,128)(2,1)S(1)} %collective-permute-done.9.refs_1_, bf16[8,2048]{1,0:T(8,128)(2,1)S(1)} %collective-permute-done.10.refs_2_, ...), custom_call_target="tpu_custom_call" | custom-call | flops 268435456 | bytes 8388608 | tf_op jit(solution)/shard_map/pallas_call | solution.py:144
  53.1 1.3 %collective-permute-done.12.r_ref = bf16[32,2048]{1,0:T(8,128)(2,1)S(1)} collective-permute-done((bf16[32,2048]{1,0:T(8,128)(2,1)S(1)}, bf16[32,2048]{1,0:T(8,128)(2,1)S(1)}, u32[]{:S(2)}, u32[]{:S(2)}) %collective-permute-start.12) | collective-permute-done | bytes 131104 | tf_op jit(solution)/shard_map/ppermute | solution.py:404
  54.5 1.5 %collective-permute-start.13 = (bf16[32,2048]{1,0:T(8,128)(2,1)S(1)}, bf16[32,2048]{1,0:T(8,128)(2,1)S(1)}, u32[]{:S(2)}, u32[]{:S(2)}) collective-permute-start(bf16[32,2048]{1,0:T(8,128)(2,1)S(1)} %shard_map.136.after_ref.near_ref), channel_id=1, source_target_pairs={{0,2},{1,3},{2,0},{3,1},{4,6},{5,7},{6,4},{7,5},{8,10},{9,11},{10,... | collective-permute-start | bytes 393224 | tf_op jit(solution)/shard_map/ppermute | solution.py:404
  56.0 3.7 %shard_map.137.refs_1_ = bf16[640,2,3584]{2,1,0:T(2,128)(2,1)S(1)} custom-call(bf16[32,2048]{1,0:T(8,128)(2,1)S(1)} %shard_map.136.after_ref.near_ref, bf16[2048,2,3584]{2,1,0:T(2,128)(2,1)} %refs_2_.1), custom_call_target="tpu_custom_call" | custom-call | flops 3211264000 | tf_op jit(solution)/shard_map/pallas_call | solution.py:103
  59.7 0.4 collective-permute-done.13.far_ref
  60.1 7.2 %shard_map.138 = (bf16[32,2048]{1,0:T(8,128)(2,1)S(1)}, bf16[16,3712]{1,0:T(8,128)(2,1)S(1)}, bf16[16,3712]{1,0:T(8,128)(2,1)S(1)}, bf16[16,3712]{1,0:T(8,128)(2,1)S(1)}, bf16[16,3712]{1,0:T(8,128)(2,1)S(1)}) custom-call(bf16[32,2048]{1,0:T(8,128)(2,1)S(1)} %copy-done.1, bf16[32,2048]{1,0:T(8,128)(2,1)S(1)} %shard_map.136.after_ref.near_ref, ...), custom_call_target="tpu_custom_call" | custom-call | flops 1879048192 | bytes 29360128 | tf_op jit(solution)/shard_map/pallas_call | solution.py:340
  67.4 2.2 %collective-permute-start.14 = (bf16[16,3712]{1,0:T(8,128)(2,1)S(1)}, bf16[16,3712]{1,0:T(8,128)(2,1)S(1)}, u32[]{:S(2)}, u32[]{:S(2)}) collective-permute-start(bf16[16,3712]{1,0:T(8,128)(2,1)S(1)} %get-tuple-element.21), channel_id=1, source_target_pairs={{0,4},{4,8},{8,12},{12,0},{1,5},{5,9},{9,13},{13,1},{2,6},{6,10},{... | collective-permute-start | bytes 356360 | tf_op jit(solution)/shard_map/ppermute | solution.py:22
  69.6 1.0 %collective-permute-start.15 = (bf16[16,3712]{1,0:T(8,128)(2,1)S(1)}, bf16[16,3712]{1,0:T(8,128)(2,1)S(1)}, u32[]{:S(2)}, u32[]{:S(2)}) collective-permute-start(bf16[16,3712]{1,0:T(8,128)(2,1)S(1)} %get-tuple-element.22), channel_id=1, source_target_pairs={{0,8},{4,12},{8,0},{12,4},{1,9},{5,13},{9,1},{13,5},{2,10},{6,14},... | collective-permute-start | bytes 356360 | tf_op jit(solution)/shard_map/ppermute | solution.py:22
  70.6 1.4 %collective-permute-start.16 = (bf16[16,3712]{1,0:T(8,128)(2,1)S(1)}, bf16[16,3712]{1,0:T(8,128)(2,1)S(1)}, u32[]{:S(2)}, u32[]{:S(2)}) collective-permute-start(bf16[16,3712]{1,0:T(8,128)(2,1)S(1)} %get-tuple-element.23), channel_id=1, source_target_pairs={{0,12},{4,0},{8,4},{12,8},{1,13},{5,1},{9,5},{13,9},{2,14},{6,2},{... | collective-permute-start | bytes 356360 | tf_op jit(solution)/shard_map/ppermute | solution.py:22
  72.0 5.3 %shard_map.139.refs_4_ = bf16[3584,2048]{1,0:T(8,128)(2,1)S(1)} custom-call(bf16[16,3712]{1,0:T(8,128)(2,1)S(1)} %get-tuple-element.20.after_ref.refs_0_, bf16[3584,2048]{1,0:T(8,128)(2,1)} %w_ref.7), custom_call_target="tpu_custom_call" | custom-call | flops 5138022400 | tf_op jit(solution)/shard_map/pallas_call | solution.py:103
  77.3 1.9 %collective-permute-done.15.refs_2_ = bf16[16,3712]{1,0:T(8,128)(2,1)S(1)} collective-permute-done((bf16[16,3712]{1,0:T(8,128)(2,1)S(1)}, bf16[16,3712]{1,0:T(8,128)(2,1)S(1)}, u32[]{:S(2)}, u32[]{:S(2)}) %collective-permute-start.15) | collective-permute-done | bytes 118816 | tf_op jit(solution)/shard_map/ppermute | solution.py:22
  79.4 3.4 %collective-permute-start.19 = (bf16[8,3584]{1,0:T(8,128)(2,1)S(1)}, bf16[8,3584]{1,0:T(8,128)(2,1)S(1)}, u32[]{:S(2)}, u32[]{:S(2)}) collective-permute-start(bf16[8,3584]{1,0:T(8,128)(2,1)S(1)} %shard_map.140.refs_0_), channel_id=1, source_target_pairs={{0,12},{4,0},{8,4},{12,8},{1,13},{5,1},{9,5},{13,9},{2,14},{6,2},{... | collective-permute-start | bytes 172040 | tf_op jit(solution)/shard_map/ppermute | solution.py:22
  82.7 1.2 %collective-permute-start.18 = (bf16[8,3584]{1,0:T(8,128)(2,1)S(1)}, bf16[8,3584]{1,0:T(8,128)(2,1)S(1)}, u32[]{:S(2)}, u32[]{:S(2)}) collective-permute-start(bf16[8,3584]{1,0:T(8,128)(2,1)S(1)} %shard_map.140.refs_0_), channel_id=1, source_target_pairs={{0,8},{4,12},{8,0},{12,4},{1,9},{5,13},{9,1},{13,5},{2,10},{6,14},... | collective-permute-start | bytes 172040 | tf_op jit(solution)/shard_map/ppermute | solution.py:22
  83.9 1.2 %collective-permute-done.19.refs_3_ = bf16[8,3584]{1,0:T(8,128)(2,1)S(1)} collective-permute-done((bf16[8,3584]{1,0:T(8,128)(2,1)S(1)}, bf16[8,3584]{1,0:T(8,128)(2,1)S(1)}, u32[]{:S(2)}, u32[]{:S(2)}) %collective-permute-start.19) | collective-permute-done | bytes 57376 | tf_op jit(solution)/shard_map/ppermute | solution.py:22
  85.1 3.9 %collective-permute-done.18.refs_2_ = bf16[8,3584]{1,0:T(8,128)(2,1)S(1)} collective-permute-done((bf16[8,3584]{1,0:T(8,128)(2,1)S(1)}, bf16[8,3584]{1,0:T(8,128)(2,1)S(1)}, u32[]{:S(2)}, u32[]{:S(2)}) %collective-permute-start.18) | collective-permute-done | bytes 57376 | tf_op jit(solution)/shard_map/ppermute | solution.py:22
  88.9 0.9 collective-permute-done.17.refs_1_
  89.9 2.6 %shard_map.141.l_ref = bf16[32,2048]{1,0:T(8,128)(2,1)S(1)} custom-call(bf16[8,3584]{1,0:T(8,128)(2,1)S(1)} %shard_map.140.refs_0_, bf16[8,3584]{1,0:T(8,128)(2,1)S(1)} %collective-permute-done.17.refs_1_, bf16[8,3584]{1,0:T(8,128)(2,1)S(1)} %collective-permute-done.18.refs_2_, bf16[8,3584]{1,0:T(8,128)(2,1)S(1)} %collective-permute-done.19.refs_3_, ...), custom_call_target="tpu_custom_call" | custom-call | flops 469762048 | bytes 14680064 | tf_op jit(solution)/shard_map/pallas_call | solution.py:144
  92.5 1.4 %collective-permute-done.20.r_ref = bf16[32,2048]{1,0:T(8,128)(2,1)S(1)} collective-permute-done((bf16[32,2048]{1,0:T(8,128)(2,1)S(1)}, bf16[32,2048]{1,0:T(8,128)(2,1)S(1)}, u32[]{:S(2)}, u32[]{:S(2)}) %collective-permute-start.20) | collective-permute-done | bytes 131104 | tf_op jit(solution)/shard_map/ppermute | solution.py:404
  93.9 1.3 %collective-permute-start.21 = (bf16[32,2048]{1,0:T(8,128)(2,1)S(1)}, bf16[32,2048]{1,0:T(8,128)(2,1)S(1)}, u32[]{:S(2)}, u32[]{:S(2)}) collective-permute-start(bf16[32,2048]{1,0:T(8,128)(2,1)S(1)} %shard_map.142), channel_id=1, source_target_pairs={{0,2},{1,3},{2,0},{3,1},{4,6},{5,7},{6,4},{7,5},{8,10},{9,11},{10,... | collective-permute-start | bytes 393224 | tf_op jit(solution)/shard_map/ppermute | solution.py:404
  95.2 4.3 %collective-permute-done.21 = bf16[32,2048]{1,0:T(8,128)(2,1)S(1)} collective-permute-done((bf16[32,2048]{1,0:T(8,128)(2,1)S(1)}, bf16[32,2048]{1,0:T(8,128)(2,1)S(1)}, u32[]{:S(2)}, u32[]{:S(2)}) %collective-permute-start.21) | collective-permute-done | bytes 131104 | tf_op jit(solution)/shard_map/ppermute | solution.py:404
  99.5 0.7 add_convert_fusion
  (101 shorter events, 3.8 us)
Async XLA Ops:
  0.6 13.2 %copy-start.5 = (s32[32]{0:T(128)S(1)}, s32[32]{0:T(128)}, u32[]{:S(2)}) copy-start(s32[32]{0:T(128)} %param.13) | copy-start | bytes 388
  0.6 13.4 %copy-start.4 = (s32[32,128]{1,0:T(8,128)S(1)}, s32[32,128]{1,0:T(8,128)}, u32[]{:S(2)}) copy-start(s32[32,128]{1,0:T(8,128)} %param.14) | copy-start | bytes 49156
  6.8 12.9 %collective-permute-start = (f32[8,2688]{1,0:T(8,128)}, f32[8,2688]{1,0:T(8,128)S(1)}, u32[]{:S(2)}, u32[]{:S(2)}) collective-permute-start(f32[8,2688]{1,0:T(8,128)} %get-tuple-element.14), channel_id=1, source_target_pairs={{0,4},{4,8},{8,12},{12,0},{1,5},{5,9},{9,13},{13,1},{2,6},{6,10},{... | collective-permute-start | bytes 258056 | tf_op jit(solution)/shard_map/ppermute | solution.py:22
  9.9 9.8 %collective-permute-start.1 = (f32[8,2688]{1,0:T(8,128)}, f32[8,2688]{1,0:T(8,128)S(1)}, u32[]{:S(2)}, u32[]{:S(2)}) collective-permute-start(f32[8,2688]{1,0:T(8,128)} %get-tuple-element.15), channel_id=1, source_target_pairs={{0,8},{4,12},{8,0},{12,4},{1,9},{5,13},{9,1},{13,5},{2,10},{6,14},... | collective-permute-start | bytes 258056 | tf_op jit(solution)/shard_map/ppermute | solution.py:22
  12.5 7.2 %collective-permute-start.2 = (f32[8,2688]{1,0:T(8,128)}, f32[8,2688]{1,0:T(8,128)S(1)}, u32[]{:S(2)}, u32[]{:S(2)}) collective-permute-start(f32[8,2688]{1,0:T(8,128)} %get-tuple-element.16), channel_id=1, source_target_pairs={{0,12},{4,0},{8,4},{12,8},{1,13},{5,1},{9,5},{13,9},{2,14},{6,2},{... | collective-permute-start | bytes 258056 | tf_op jit(solution)/shard_map/ppermute | solution.py:22
  15.2 0.9 copy-start.2
  19.6 9.2 %copy-start = (bf16[2048,2048]{1,0:T(8,128)(2,1)}, bf16[2048,2048]{1,0:T(8,128)(2,1)S(1)}, u32[]{:S(2)}) copy-start(bf16[2048,2048]{1,0:T(8,128)(2,1)S(1)} %shard_map.132.refs_6_.refs_4_) | copy-start | bytes 25165828
  19.6 7.6 %slice-start.2 = ((s8[5242880]{0:T(1024)(128)(4,1)}), s8[4194304]{0:T(1024)(128)(4,1)S(1)}, s32[]{:S(2)}) async-start(s8[5242880]{0:T(1024)(128)(4,1)} %bitcast.159), calls=%async_computation.2 | async-start | bytes 8388608
  19.7 7.5 %slice-start.3 = ((s8[5242880]{0:T(1024)(128)(4,1)}), s8[1048576]{0:T(1024)(128)(4,1)S(1)}, s32[]{:S(2)}) async-start(s8[5242880]{0:T(1024)(128)(4,1)} %bitcast.159), calls=%async_computation.3 | async-start | bytes 2097152
  19.9 6.9 %collective-permute-start.5 = (bf16[8,2560]{1,0:T(8,128)(2,1)S(1)}, bf16[8,2560]{1,0:T(8,128)(2,1)S(1)}, u32[]{:S(2)}, u32[]{:S(2)}) collective-permute-start(bf16[8,2560]{1,0:T(8,128)(2,1)S(1)} %shard_map.133), channel_id=1, source_target_pairs={{0,4},{4,8},{8,12},{12,0},{1,5},{5,9},{9,13},{13,1},{2,6},{6,10},{... | collective-permute-start | bytes 122888 | tf_op jit(solution)/shard_map/ppermute | solution.py:22
  21.0 5.8 %collective-permute-start.4 = (bf16[8,2560]{1,0:T(8,128)(2,1)S(1)}, bf16[8,2560]{1,0:T(8,128)(2,1)S(1)}, u32[]{:S(2)}, u32[]{:S(2)}) collective-permute-start(bf16[8,2560]{1,0:T(8,128)(2,1)S(1)} %shard_map.133), channel_id=1, source_target_pairs={{0,8},{4,12},{8,0},{12,4},{1,9},{5,13},{9,1},{13,5},{2,10},{6,14},... | collective-permute-start | bytes 122888 | tf_op jit(solution)/shard_map/ppermute | solution.py:22
  22.8 4.0 %collective-permute-start.3 = (bf16[8,2560]{1,0:T(8,128)(2,1)S(1)}, bf16[8,2560]{1,0:T(8,128)(2,1)S(1)}, u32[]{:S(2)}, u32[]{:S(2)}) collective-permute-start(bf16[8,2560]{1,0:T(8,128)(2,1)S(1)} %shard_map.133), channel_id=1, source_target_pairs={{0,12},{4,0},{8,4},{12,8},{1,13},{5,1},{9,5},{13,9},{2,14},{6,2},{... | collective-permute-start | bytes 122888 | tf_op jit(solution)/shard_map/ppermute | solution.py:22
  34.1 5.8 %collective-permute-start.6 = (bf16[8,2176]{1,0:T(8,128)(2,1)S(1)}, bf16[8,2176]{1,0:T(8,128)(2,1)S(1)}, u32[]{:S(2)}, u32[]{:S(2)}) collective-permute-start(bf16[8,2176]{1,0:T(8,128)(2,1)S(1)} %get-tuple-element.31), channel_id=1, source_target_pairs={{0,4},{4,8},{8,12},{12,0},{1,5},{5,9},{9,13},{13,1},{2,6},{6,10},{... | collective-permute-start | bytes 104456 | tf_op jit(solution)/shard_map/ppermute | solution.py:22
  35.7 4.9 %collective-permute-start.7 = (bf16[8,2176]{1,0:T(8,128)(2,1)S(1)}, bf16[8,2176]{1,0:T(8,128)(2,1)S(1)}, u32[]{:S(2)}, u32[]{:S(2)}) collective-permute-start(bf16[8,2176]{1,0:T(8,128)(2,1)S(1)} %get-tuple-element.32), channel_id=1, source_target_pairs={{0,8},{4,12},{8,0},{12,4},{1,9},{5,13},{9,1},{13,5},{2,10},{6,14},... | collective-permute-start | bytes 104456 | tf_op jit(solution)/shard_map/ppermute | solution.py:22
  37.5 3.9 %collective-permute-start.8 = (bf16[8,2176]{1,0:T(8,128)(2,1)S(1)}, bf16[8,2176]{1,0:T(8,128)(2,1)S(1)}, u32[]{:S(2)}, u32[]{:S(2)}) collective-permute-start(bf16[8,2176]{1,0:T(8,128)(2,1)S(1)} %get-tuple-element.33), channel_id=1, source_target_pairs={{0,12},{4,0},{8,4},{12,8},{1,13},{5,1},{9,5},{13,9},{2,14},{6,2},{... | collective-permute-start | bytes 104456 | tf_op jit(solution)/shard_map/ppermute | solution.py:22
  42.6 8.5 %slice-start = ((s8[8388608]{0:T(1024)(128)(4,1)}), s8[4194304]{0:T(1024)(128)(4,1)S(1)}, s32[]{:S(2)}) async-start(s8[8388608]{0:T(1024)(128)(4,1)} %bitcast.157), calls=%async_computation | async-start | bytes 8388608
  42.6 8.4 %slice-start.1 = ((s8[8388608]{0:T(1024)(128)(4,1)}), s8[4194304]{0:T(1024)(128)(4,1)S(1)}, s32[]{:S(2)}) async-start(s8[8388608]{0:T(1024)(128)(4,1)} %bitcast.157), calls=%async_computation.1 | async-start | bytes 8388608
  42.6 7.5 %collective-permute-start.11 = (bf16[8,2048]{1,0:T(8,128)(2,1)S(1)}, bf16[8,2048]{1,0:T(8,128)(2,1)S(1)}, u32[]{:S(2)}, u32[]{:S(2)}) collective-permute-start(bf16[8,2048]{1,0:T(8,128)(2,1)S(1)} %divide_convert_fusion.after_ref.refs_0_), channel_id=1, source_target_pairs={{0,12},{4,0},{8,4},{12,8},{1,13},{5,1},{9,5},{13,9},{2,14},{6,2},{... | collective-permute-start | bytes 98312 | tf_op jit(solution)/shard_map/ppermute | solution.py:22
  45.2 4.9 %collective-permute-start.10 = (bf16[8,2048]{1,0:T(8,128)(2,1)S(1)}, bf16[8,2048]{1,0:T(8,128)(2,1)S(1)}, u32[]{:S(2)}, u32[]{:S(2)}) collective-permute-start(bf16[8,2048]{1,0:T(8,128)(2,1)S(1)} %divide_convert_fusion.after_ref.refs_0_), channel_id=1, source_target_pairs={{0,8},{4,12},{8,0},{12,4},{1,9},{5,13},{9,1},{13,5},{2,10},{6,14},... | collective-permute-start | bytes 98312 | tf_op jit(solution)/shard_map/ppermute | solution.py:22
  45.3 5.7 %collective-permute-start.9 = (bf16[8,2048]{1,0:T(8,128)(2,1)S(1)}, bf16[8,2048]{1,0:T(8,128)(2,1)S(1)}, u32[]{:S(2)}, u32[]{:S(2)}) collective-permute-start(bf16[8,2048]{1,0:T(8,128)(2,1)S(1)} %divide_convert_fusion.after_ref.refs_0_), channel_id=1, source_target_pairs={{0,4},{4,8},{8,12},{12,0},{1,5},{5,9},{9,13},{13,1},{2,6},{6,10},{... | collective-permute-start | bytes 98312 | tf_op jit(solution)/shard_map/ppermute | solution.py:22
  53.1 1.3 %collective-permute-start.12 = (bf16[32,2048]{1,0:T(8,128)(2,1)S(1)}, bf16[32,2048]{1,0:T(8,128)(2,1)S(1)}, u32[]{:S(2)}, u32[]{:S(2)}) collective-permute-start(bf16[32,2048]{1,0:T(8,128)(2,1)S(1)} %get-tuple-element.18.l_ref), channel_id=1, source_target_pairs={{0,1},{1,0},{2,3},{3,2},{4,5},{5,4},{6,7},{7,6},{8,9},{9,8},{10,11... | collective-permute-start | bytes 393224 | tf_op jit(solution)/shard_map/ppermute | solution.py:404
  54.5 5.6 %copy-start.1 = (bf16[32,2048]{1,0:T(8,128)(2,1)S(1)}, bf16[32,2048]{1,0:T(8,128)(2,1)}, u32[]{:S(2)}) copy-start(bf16[32,2048]{1,0:T(8,128)(2,1)} %hid_ref.3) | copy-start | bytes 393220
  54.5 5.6 %copy-start.3 = (bf16[2048]{0:T(1024)(128)(2,1)S(1)}, bf16[2048]{0:T(1024)(128)(2,1)}, u32[]{:S(2)}) copy-start(bf16[2048]{0:T(1024)(128)(2,1)} %gain_ref.3) | copy-start | bytes 12292
  54.5 5.6 %collective-permute-start.13 = (bf16[32,2048]{1,0:T(8,128)(2,1)S(1)}, bf16[32,2048]{1,0:T(8,128)(2,1)S(1)}, u32[]{:S(2)}, u32[]{:S(2)}) collective-permute-start(bf16[32,2048]{1,0:T(8,128)(2,1)S(1)} %shard_map.136.after_ref.near_ref), channel_id=1, source_target_pairs={{0,2},{1,3},{2,0},{3,1},{4,6},{5,7},{6,4},{7,5},{8,10},{9,11},{10,... | collective-permute-start | bytes 393224 | tf_op jit(solution)/shard_map/ppermute | solution.py:404
  67.4 9.9 %collective-permute-start.14 = (bf16[16,3712]{1,0:T(8,128)(2,1)S(1)}, bf16[16,3712]{1,0:T(8,128)(2,1)S(1)}, u32[]{:S(2)}, u32[]{:S(2)}) collective-permute-start(bf16[16,3712]{1,0:T(8,128)(2,1)S(1)} %get-tuple-element.21), channel_id=1, source_target_pairs={{0,4},{4,8},{8,12},{12,0},{1,5},{5,9},{9,13},{13,1},{2,6},{6,10},{... | collective-permute-start | bytes 356360 | tf_op jit(solution)/shard_map/ppermute | solution.py:22
  69.6 9.7 %collective-permute-start.15 = (bf16[16,3712]{1,0:T(8,128)(2,1)S(1)}, bf16[16,3712]{1,0:T(8,128)(2,1)S(1)}, u32[]{:S(2)}, u32[]{:S(2)}) collective-permute-start(bf16[16,3712]{1,0:T(8,128)(2,1)S(1)} %get-tuple-element.22), channel_id=1, source_target_pairs={{0,8},{4,12},{8,0},{12,4},{1,9},{5,13},{9,1},{13,5},{2,10},{6,14},... | collective-permute-start | bytes 356360 | tf_op jit(solution)/shard_map/ppermute | solution.py:22
  70.6 8.6 %collective-permute-start.16 = (bf16[16,3712]{1,0:T(8,128)(2,1)S(1)}, bf16[16,3712]{1,0:T(8,128)(2,1)S(1)}, u32[]{:S(2)}, u32[]{:S(2)}) collective-permute-start(bf16[16,3712]{1,0:T(8,128)(2,1)S(1)} %get-tuple-element.23), channel_id=1, source_target_pairs={{0,12},{4,0},{8,4},{12,8},{1,13},{5,1},{9,5},{13,9},{2,14},{6,2},{... | collective-permute-start | bytes 356360 | tf_op jit(solution)/shard_map/ppermute | solution.py:22
  79.4 5.7 %collective-permute-start.19 = (bf16[8,3584]{1,0:T(8,128)(2,1)S(1)}, bf16[8,3584]{1,0:T(8,128)(2,1)S(1)}, u32[]{:S(2)}, u32[]{:S(2)}) collective-permute-start(bf16[8,3584]{1,0:T(8,128)(2,1)S(1)} %shard_map.140.refs_0_), channel_id=1, source_target_pairs={{0,12},{4,0},{8,4},{12,8},{1,13},{5,1},{9,5},{13,9},{2,14},{6,2},{... | collective-permute-start | bytes 172040 | tf_op jit(solution)/shard_map/ppermute | solution.py:22
  82.7 6.2 %collective-permute-start.18 = (bf16[8,3584]{1,0:T(8,128)(2,1)S(1)}, bf16[8,3584]{1,0:T(8,128)(2,1)S(1)}, u32[]{:S(2)}, u32[]{:S(2)}) collective-permute-start(bf16[8,3584]{1,0:T(8,128)(2,1)S(1)} %shard_map.140.refs_0_), channel_id=1, source_target_pairs={{0,8},{4,12},{8,0},{12,4},{1,9},{5,13},{9,1},{13,5},{2,10},{6,14},... | collective-permute-start | bytes 172040 | tf_op jit(solution)/shard_map/ppermute | solution.py:22
  83.9 6.0 %collective-permute-start.17 = (bf16[8,3584]{1,0:T(8,128)(2,1)S(1)}, bf16[8,3584]{1,0:T(8,128)(2,1)S(1)}, u32[]{:S(2)}, u32[]{:S(2)}) collective-permute-start(bf16[8,3584]{1,0:T(8,128)(2,1)S(1)} %shard_map.140.refs_0_), channel_id=1, source_target_pairs={{0,4},{4,8},{8,12},{12,0},{1,5},{5,9},{9,13},{13,1},{2,6},{6,10},{... | collective-permute-start | bytes 172040 | tf_op jit(solution)/shard_map/ppermute | solution.py:22
  92.5 1.4 %collective-permute-start.20 = (bf16[32,2048]{1,0:T(8,128)(2,1)S(1)}, bf16[32,2048]{1,0:T(8,128)(2,1)S(1)}, u32[]{:S(2)}, u32[]{:S(2)}) collective-permute-start(bf16[32,2048]{1,0:T(8,128)(2,1)S(1)} %shard_map.141.l_ref), channel_id=1, source_target_pairs={{0,1},{1,0},{2,3},{3,2},{4,5},{5,4},{6,7},{7,6},{8,9},{9,8},{10,11... | collective-permute-start | bytes 393224 | tf_op jit(solution)/shard_map/ppermute | solution.py:404
  93.9 5.6 %collective-permute-start.21 = (bf16[32,2048]{1,0:T(8,128)(2,1)S(1)}, bf16[32,2048]{1,0:T(8,128)(2,1)S(1)}, u32[]{:S(2)}, u32[]{:S(2)}) collective-permute-start(bf16[32,2048]{1,0:T(8,128)(2,1)S(1)} %shard_map.142), channel_id=1, source_target_pairs={{0,2},{1,3},{2,0},{3,1},{4,6},{5,7},{6,4},{7,5},{8,10},{9,11},{10,... | collective-permute-start | bytes 393224 | tf_op jit(solution)/shard_map/ppermute | solution.py:404

commit v5 on v4

--- a/solution.py
+++ b/solution.py
@@ -59,7 +59,7 @@
 GATE_LIMIT = 24 << 20
 QUERY_LIMIT = 56 << 20
 FETCH_LIMIT = 26 << 20
-CUT = (6, 5)
+CUT = (7, 5)
 OUT_LIMIT = 40 << 20
 
 

time: 100 us -> 100 us (level)
  waiting for transfers between devices: 22.1 us -> 21.1 us
    ppermute x18, waiting for transfers between devices: 14.7 us -> 13.7 us  [shifted(): return lax.ppermute(x, axis, [(i, (i + step) % n) for i in range(n)])]
where the time goes in v5:
time: 100 us
  Pallas kernels  35.6 us (36%)
  starting transfers between devices  30.7 us (31%)
  waiting for transfers between devices  21.1 us (21%)
  matrix products  5.72 us (6%)
  other arithmetic  3.04 us (3%)
  local copies, waits for them, and re-layouts  2.84 us (3%)
  between operations  1.13 us (1%)
    ppermute x18, starting transfers between devices, shifted(): return lax.ppermute(x, axis, [(i, (i + step) % n) for i in range(n)])  27.9 us
    pallas_call x4, Pallas kernels, fetch(): pl.pallas_call(kernel, in_specs=[pl.BlockSpec(memory_space=pl.ANY)] * 2,...  17.3 us
    ppermute x18, waiting for transfers between devices, shifted(): return lax.ppermute(x, axis, [(i, (i + step) % n) for i in range(n)])  13.7 us
    ppermute x4, waiting for transfers between devices, pairwise(): far = lax.ppermute(near, 'comp', [(i, i ^ step) for i in range(n)])  7.42 us
    pallas_call x1, Pallas kernels, gate_up_parts(): pl.pallas_call(kernel, in_specs=whole(4 + n_held) + [pl.BlockSpec(memory_...  7.18 us
    pallas_call x1, Pallas kernels, query_parts(): pl.pallas_call(kernel, in_specs=[pl.BlockSpec(memory_space=pltpu.HBM)] *...  6.15 us
    pallas_call x2, Pallas kernels, gathered_dot(): pl.pallas_call(kernel, in_specs=whole(n_mem + 1) + [pl.BlockSpec(memory_s...  4.69 us
    dot_general x1, matrix products, slot_stats(): jnp.einsum('skgb,sbkd->skgd', weights.astype(jnp.bfloat16), value_rows, p...  3.37 us
  transfers between devices with their start and end apart: 22, of which 13 were waited for; matrix products, arithmetic and copies ran while one was open for 2% of the time, Pallas kernels for 17%

profile of v5, /device:TPU:0, one launch (start us, length us, event | category | flops | bytes accessed | tf_op | source)
XLA Modules:
  0.0 100.1 jit_solution(3913128438858617425)
XLA Ops:
  0.7 6.2 %shard_map.131 = (f32[8,2688]{1,0:T(8,128)}, f32[8,2688]{1,0:T(8,128)}, f32[8,2688]{1,0:T(8,128)}, f32[8,2688]{1,0:T(8,128)}) custom-call(bf16[32,2048]{1,0:T(8,128)(2,1)} %hid_ref.3, bf16[2048]{0:T(1024)(128)(2,1)} %gain_ref.2, bf16[2048,2048]{1,0:T(8,128)(2,1)} %wq_ref.1, bf16[2048,2,256]{2,1,0:T(2,128)(2,1)} %wkv_ref.1), custom_call_target="tpu_custom_call" | custom-call | flops 268435456 | bytes 8388608 | tf_op jit(solution)/shard_map/pallas_call | solution.py:225
  6.8 3.1 %collective-permute-start = (f32[8,2688]{1,0:T(8,128)}, f32[8,2688]{1,0:T(8,128)S(1)}, u32[]{:S(2)}, u32[]{:S(2)}) collective-permute-start(f32[8,2688]{1,0:T(8,128)} %get-tuple-element.14), channel_id=1, source_target_pairs={{0,4},{4,8},{8,12},{12,0},{1,5},{5,9},{9,13},{13,1},{2,6},{6,10},{... | collective-permute-start | bytes 258056 | tf_op jit(solution)/shard_map/ppermute | solution.py:22
  9.9 2.6 %collective-permute-start.1 = (f32[8,2688]{1,0:T(8,128)}, f32[8,2688]{1,0:T(8,128)S(1)}, u32[]{:S(2)}, u32[]{:S(2)}) collective-permute-start(f32[8,2688]{1,0:T(8,128)} %get-tuple-element.15), channel_id=1, source_target_pairs={{0,8},{4,12},{8,0},{12,4},{1,9},{5,13},{9,1},{13,5},{2,10},{6,14},... | collective-permute-start | bytes 258056 | tf_op jit(solution)/shard_map/ppermute | solution.py:22
  12.5 1.4 %collective-permute-start.2 = (f32[8,2688]{1,0:T(8,128)}, f32[8,2688]{1,0:T(8,128)S(1)}, u32[]{:S(2)}, u32[]{:S(2)}) collective-permute-start(f32[8,2688]{1,0:T(8,128)} %get-tuple-element.16), channel_id=1, source_target_pairs={{0,12},{4,0},{8,4},{12,8},{1,13},{5,1},{9,5},{13,9},{2,14},{6,2},{... | collective-permute-start | bytes 258056 | tf_op jit(solution)/shard_map/ppermute | solution.py:22
  14.1 0.6 fusion.20
  14.7 0.3 select_reduce_fusion
  15.2 0.9 copy-done.2
  16.1 3.5 %shard_map.132.refs_6_.refs_4_ = bf16[2048,2048]{1,0:T(8,128)(2,1)S(1)} custom-call(f32[8,2688]{1,0:T(8,128)S(1)} %copy-done.2, bf16[2048,2048]{1,0:T(8,128)(2,1)} %w_ref.4), custom_call_target="tpu_custom_call" | custom-call | flops 2936012800 | tf_op jit(solution)/shard_map/pallas_call | solution.py:103
  19.9 1.1 %collective-permute-start.5 = (bf16[8,2560]{1,0:T(8,128)(2,1)S(1)}, bf16[8,2560]{1,0:T(8,128)(2,1)S(1)}, u32[]{:S(2)}, u32[]{:S(2)}) collective-permute-start(bf16[8,2560]{1,0:T(8,128)(2,1)S(1)} %shard_map.133), channel_id=1, source_target_pairs={{0,4},{4,8},{8,12},{12,0},{1,5},{5,9},{9,13},{13,1},{2,6},{6,10},{... | collective-permute-start | bytes 122888 | tf_op jit(solution)/shard_map/ppermute | solution.py:22
  21.0 1.8 %collective-permute-start.4 = (bf16[8,2560]{1,0:T(8,128)(2,1)S(1)}, bf16[8,2560]{1,0:T(8,128)(2,1)S(1)}, u32[]{:S(2)}, u32[]{:S(2)}) collective-permute-start(bf16[8,2560]{1,0:T(8,128)(2,1)S(1)} %shard_map.133), channel_id=1, source_target_pairs={{0,8},{4,12},{8,0},{12,4},{1,9},{5,13},{9,1},{13,5},{2,10},{6,14},... | collective-permute-start | bytes 122888 | tf_op jit(solution)/shard_map/ppermute | solution.py:22
  22.8 1.0 collective-permute-start.3
  23.9 2.9 %collective-permute-done.3 = bf16[8,2560]{1,0:T(8,128)(2,1)S(1)} collective-permute-done((bf16[8,2560]{1,0:T(8,128)(2,1)S(1)}, bf16[8,2560]{1,0:T(8,128)(2,1)S(1)}, u32[]{:S(2)}, u32[]{:S(2)}) %collective-permute-start.3) | collective-permute-done | bytes 40992 | tf_op jit(solution)/shard_map/ppermute | solution.py:22
  26.9 0.2 fusion.18
  27.2 1.6 %fusion.73 = (f32[40,2,8]{2,1,0:T(2,128)S(1)}, f32[40,2,8,256]{3,2,1,0:T(8,128)S(1)}) fusion(bf16[40,2,8,128]{3,2,1,0:T(8,128)(2,1)S(1)} %bitcast.161, pred[40,256]{1,0:T(8,128)(4,1)S(1)} %iota_compare_fusion.1, bf16[40,256,256]{2,1,0:T(8,128)(2,1)S(1)} %bitcast.160), kind=kOutput, calls=%fused_computation.132 | convolution fusion | flops 42433920 | bytes 6074880 | tf_op jit(solution)/shard_map/skgd,sbkd->skgb/dot_general | solution.py:430
  29.5 0.3 fusion.21
  30.2 3.4 %fusion.15 = f32[2,8,128,40]{2,1,0,3:T(8,128)S(1)} fusion(f32[40,2,8,256]{3,2,1,0:T(8,128)S(1)} %get-tuple-element.60, f32[40,2,8]{2,1,0:T(2,128)S(1)} %get-tuple-element.59, pred[40,256]{1,0:T(8,128)(4,1)S(1)} %iota_compare_fusion.1, f32[2,8,40]{1,0,2:T(2,128)S(1)} %copy.138, bf16[40,256,256]{2,1,0:T(8,128)(2,1)} %param.16), kind=kOutput, calls=%fused_computation.11 | convolution fusion | flops 42516480 | bytes 6241280 | tf_op jit(solution)/shard_map/skgb,sbkd->skgd/dot_general | solution.py:440
  33.6 0.3 convolution_convert_fusion.1
  34.1 1.6 %collective-permute-start.6 = (bf16[8,2176]{1,0:T(8,128)(2,1)S(1)}, bf16[8,2176]{1,0:T(8,128)(2,1)S(1)}, u32[]{:S(2)}, u32[]{:S(2)}) collective-permute-start(bf16[8,2176]{1,0:T(8,128)(2,1)S(1)} %get-tuple-element.31), channel_id=1, source_target_pairs={{0,4},{4,8},{8,12},{12,0},{1,5},{5,9},{9,13},{13,1},{2,6},{6,10},{... | collective-permute-start | bytes 104456 | tf_op jit(solution)/shard_map/ppermute | solution.py:22
  35.7 1.9 %collective-permute-start.7 = (bf16[8,2176]{1,0:T(8,128)(2,1)S(1)}, bf16[8,2176]{1,0:T(8,128)(2,1)S(1)}, u32[]{:S(2)}, u32[]{:S(2)}) collective-permute-start(bf16[8,2176]{1,0:T(8,128)(2,1)S(1)} %get-tuple-element.32), channel_id=1, source_target_pairs={{0,8},{4,12},{8,0},{12,4},{1,9},{5,13},{9,1},{13,5},{2,10},{6,14},... | collective-permute-start | bytes 104456 | tf_op jit(solution)/shard_map/ppermute | solution.py:22
  37.5 0.7 collective-permute-start.8
  38.2 1.6 %collective-permute-done.6 = bf16[8,2176]{1,0:T(8,128)(2,1)S(1)} collective-permute-done((bf16[8,2176]{1,0:T(8,128)(2,1)S(1)}, bf16[8,2176]{1,0:T(8,128)(2,1)S(1)}, u32[]{:S(2)}, u32[]{:S(2)}) %collective-permute-start.6) | collective-permute-done | bytes 34848 | tf_op jit(solution)/shard_map/ppermute | solution.py:22
  40.0 0.6 collective-permute-done.7
  40.7 0.7 collective-permute-done.8
  42.6 2.6 %collective-permute-start.11 = (bf16[8,2048]{1,0:T(8,128)(2,1)S(1)}, bf16[8,2048]{1,0:T(8,128)(2,1)S(1)}, u32[]{:S(2)}, u32[]{:S(2)}) collective-permute-start(bf16[8,2048]{1,0:T(8,128)(2,1)S(1)} %divide_convert_fusion.after_ref.refs_0_), channel_id=1, source_target_pairs={{0,12},{4,0},{8,4},{12,8},{1,13},{5,1},{9,5},{13,9},{2,14},{6,2},{... | collective-permute-start | bytes 98312 | tf_op jit(solution)/shard_map/ppermute | solution.py:22
  45.3 0.5 collective-permute-start.9
  45.8 4.8 %shard_map.134.refs_5_.refs_0_ = bf16[896,2,3584]{2,1,0:T(2,128)(2,1)S(1)} custom-call(bf16[8,2048]{1,0:T(8,128)(2,1)S(1)} %divide_convert_fusion.after_ref.refs_0_, bf16[2048,2,3584]{2,1,0:T(2,128)(2,1)} %refs_2_.1), custom_call_target="tpu_custom_call" | custom-call | flops 4495769600 | tf_op jit(solution)/shard_map/pallas_call | solution.py:103
  50.6 0.4 collective-permute-done.9.refs_1_
  51.0 2.1 %shard_map.135 = (bf16[32,2048]{1,0:T(8,128)(2,1)S(1)}, bf16[32,2048]{1,0:T(8,128)(2,1)}) custom-call(bf16[8,2048]{1,0:T(8,128)(2,1)S(1)} %divide_convert_fusion.after_ref.refs_0_, bf16[8,2048]{1,0:T(8,128)(2,1)S(1)} %collective-permute-done.9.refs_1_, bf16[8,2048]{1,0:T(8,128)(2,1)S(1)} %collective-permute-done.10.refs_2_, ...), custom_call_target="tpu_custom_call" | custom-call | flops 268435456 | bytes 8388608 | tf_op jit(solution)/shard_map/pallas_call | solution.py:144
  53.1 1.3 %collective-permute-done.12.r_ref = bf16[32,2048]{1,0:T(8,128)(2,1)S(1)} collective-permute-done((bf16[32,2048]{1,0:T(8,128)(2,1)S(1)}, bf16[32,2048]{1,0:T(8,128)(2,1)S(1)}, u32[]{:S(2)}, u32[]{:S(2)}) %collective-permute-start.12) | collective-permute-done | bytes 131104 | tf_op jit(solution)/shard_map/ppermute | solution.py:404
  54.5 1.5 %collective-permute-start.13 = (bf16[32,2048]{1,0:T(8,128)(2,1)S(1)}, bf16[32,2048]{1,0:T(8,128)(2,1)S(1)}, u32[]{:S(2)}, u32[]{:S(2)}) collective-permute-start(bf16[32,2048]{1,0:T(8,128)(2,1)S(1)} %shard_map.136.after_ref.near_ref), channel_id=1, source_target_pairs={{0,2},{1,3},{2,0},{3,1},{4,6},{5,7},{6,4},{7,5},{8,10},{9,11},{10,... | collective-permute-start | bytes 393224 | tf_op jit(solution)/shard_map/ppermute | solution.py:404
  56.0 3.7 %shard_map.137.refs_1_ = bf16[640,2,3584]{2,1,0:T(2,128)(2,1)S(1)} custom-call(bf16[32,2048]{1,0:T(8,128)(2,1)S(1)} %shard_map.136.after_ref.near_ref, bf16[2048,2,3584]{2,1,0:T(2,128)(2,1)} %refs_2_.1), custom_call_target="tpu_custom_call" | custom-call | flops 3211264000 | tf_op jit(solution)/shard_map/pallas_call | solution.py:103
  59.7 0.4 collective-permute-done.13.far_ref
  60.1 7.2 %shard_map.138 = (bf16[32,2048]{1,0:T(8,128)(2,1)S(1)}, bf16[16,3712]{1,0:T(8,128)(2,1)S(1)}, bf16[16,3712]{1,0:T(8,128)(2,1)S(1)}, bf16[16,3712]{1,0:T(8,128)(2,1)S(1)}, bf16[16,3712]{1,0:T(8,128)(2,1)S(1)}) custom-call(bf16[32,2048]{1,0:T(8,128)(2,1)S(1)} %copy-done.1, bf16[32,2048]{1,0:T(8,128)(2,1)S(1)} %shard_map.136.after_ref.near_ref, ...), custom_call_target="tpu_custom_call" | custom-call | flops 1879048192 | bytes 29360128 | tf_op jit(solution)/shard_map/pallas_call | solution.py:340
  67.3 2.7 %collective-permute-start.14 = (bf16[16,3712]{1,0:T(8,128)(2,1)S(1)}, bf16[16,3712]{1,0:T(8,128)(2,1)S(1)}, u32[]{:S(2)}, u32[]{:S(2)}) collective-permute-start(bf16[16,3712]{1,0:T(8,128)(2,1)S(1)} %get-tuple-element.21), channel_id=1, source_target_pairs={{0,4},{4,8},{8,12},{12,0},{1,5},{5,9},{9,13},{13,1},{2,6},{6,10},{... | collective-permute-start | bytes 356360 | tf_op jit(solution)/shard_map/ppermute | solution.py:22
  70.0 1.0 %collective-permute-start.15 = (bf16[16,3712]{1,0:T(8,128)(2,1)S(1)}, bf16[16,3712]{1,0:T(8,128)(2,1)S(1)}, u32[]{:S(2)}, u32[]{:S(2)}) collective-permute-start(bf16[16,3712]{1,0:T(8,128)(2,1)S(1)} %get-tuple-element.22), channel_id=1, source_target_pairs={{0,8},{4,12},{8,0},{12,4},{1,9},{5,13},{9,1},{13,5},{2,10},{6,14},... | collective-permute-start | bytes 356360 | tf_op jit(solution)/shard_map/ppermute | solution.py:22
  71.1 1.4 %collective-permute-start.16 = (bf16[16,3712]{1,0:T(8,128)(2,1)S(1)}, bf16[16,3712]{1,0:T(8,128)(2,1)S(1)}, u32[]{:S(2)}, u32[]{:S(2)}) collective-permute-start(bf16[16,3712]{1,0:T(8,128)(2,1)S(1)} %get-tuple-element.23), channel_id=1, source_target_pairs={{0,12},{4,0},{8,4},{12,8},{1,13},{5,1},{9,5},{13,9},{2,14},{6,2},{... | collective-permute-start | bytes 356360 | tf_op jit(solution)/shard_map/ppermute | solution.py:22
  72.5 5.3 %shard_map.139.refs_4_ = bf16[3584,2048]{1,0:T(8,128)(2,1)S(1)} custom-call(bf16[16,3712]{1,0:T(8,128)(2,1)S(1)} %get-tuple-element.20.after_ref.refs_0_, bf16[3584,2048]{1,0:T(8,128)(2,1)} %w_ref.7), custom_call_target="tpu_custom_call" | custom-call | flops 5138022400 | tf_op jit(solution)/shard_map/pallas_call | solution.py:103
  77.8 1.4 %collective-permute-done.15.refs_2_ = bf16[16,3712]{1,0:T(8,128)(2,1)S(1)} collective-permute-done((bf16[16,3712]{1,0:T(8,128)(2,1)S(1)}, bf16[16,3712]{1,0:T(8,128)(2,1)S(1)}, u32[]{:S(2)}, u32[]{:S(2)}) %collective-permute-start.15) | collective-permute-done | bytes 118816 | tf_op jit(solution)/shard_map/ppermute | solution.py:22
  79.3 3.9 %collective-permute-start.19 = (bf16[8,3584]{1,0:T(8,128)(2,1)S(1)}, bf16[8,3584]{1,0:T(8,128)(2,1)S(1)}, u32[]{:S(2)}, u32[]{:S(2)}) collective-permute-start(bf16[8,3584]{1,0:T(8,128)(2,1)S(1)} %shard_map.140.refs_0_), channel_id=1, source_target_pairs={{0,12},{4,0},{8,4},{12,8},{1,13},{5,1},{9,5},{13,9},{2,14},{6,2},{... | collective-permute-start | bytes 172040 | tf_op jit(solution)/shard_map/ppermute | solution.py:22
  83.2 0.7 collective-permute-start.18
  83.8 1.6 %collective-permute-done.19.refs_3_ = bf16[8,3584]{1,0:T(8,128)(2,1)S(1)} collective-permute-done((bf16[8,3584]{1,0:T(8,128)(2,1)S(1)}, bf16[8,3584]{1,0:T(8,128)(2,1)S(1)}, u32[]{:S(2)}, u32[]{:S(2)}) %collective-permute-start.19) | collective-permute-done | bytes 57376 | tf_op jit(solution)/shard_map/ppermute | solution.py:22
  85.4 3.6 %collective-permute-done.18.refs_2_ = bf16[8,3584]{1,0:T(8,128)(2,1)S(1)} collective-permute-done((bf16[8,3584]{1,0:T(8,128)(2,1)S(1)}, bf16[8,3584]{1,0:T(8,128)(2,1)S(1)}, u32[]{:S(2)}, u32[]{:S(2)}) %collective-permute-start.18) | collective-permute-done | bytes 57376 | tf_op jit(solution)/shard_map/ppermute | solution.py:22
  89.0 0.8 collective-permute-done.17.refs_1_
  89.8 2.6 %shard_map.141.l_ref = bf16[32,2048]{1,0:T(8,128)(2,1)S(1)} custom-call(bf16[8,3584]{1,0:T(8,128)(2,1)S(1)} %shard_map.140.refs_0_, bf16[8,3584]{1,0:T(8,128)(2,1)S(1)} %collective-permute-done.17.refs_1_, bf16[8,3584]{1,0:T(8,128)(2,1)S(1)} %collective-permute-done.18.refs_2_, bf16[8,3584]{1,0:T(8,128)(2,1)S(1)} %collective-permute-done.19.refs_3_, ...), custom_call_target="tpu_custom_call" | custom-call | flops 469762048 | bytes 14680064 | tf_op jit(solution)/shard_map/pallas_call | solution.py:144
  92.4 1.4 %collective-permute-done.20.r_ref = bf16[32,2048]{1,0:T(8,128)(2,1)S(1)} collective-permute-done((bf16[32,2048]{1,0:T(8,128)(2,1)S(1)}, bf16[32,2048]{1,0:T(8,128)(2,1)S(1)}, u32[]{:S(2)}, u32[]{:S(2)}) %collective-permute-start.20) | collective-permute-done | bytes 131104 | tf_op jit(solution)/shard_map/ppermute | solution.py:404
  93.8 1.3 %collective-permute-start.21 = (bf16[32,2048]{1,0:T(8,128)(2,1)S(1)}, bf16[32,2048]{1,0:T(8,128)(2,1)S(1)}, u32[]{:S(2)}, u32[]{:S(2)}) collective-permute-start(bf16[32,2048]{1,0:T(8,128)(2,1)S(1)} %shard_map.142), channel_id=1, source_target_pairs={{0,2},{1,3},{2,0},{3,1},{4,6},{5,7},{6,4},{7,5},{8,10},{9,11},{10,... | collective-permute-start | bytes 393224 | tf_op jit(solution)/shard_map/ppermute | solution.py:404
  95.1 4.3 %collective-permute-done.21 = bf16[32,2048]{1,0:T(8,128)(2,1)S(1)} collective-permute-done((bf16[32,2048]{1,0:T(8,128)(2,1)S(1)}, bf16[32,2048]{1,0:T(8,128)(2,1)S(1)}, u32[]{:S(2)}, u32[]{:S(2)}) %collective-permute-start.21) | collective-permute-done | bytes 131104 | tf_op jit(solution)/shard_map/ppermute | solution.py:404
  99.4 0.7 add_convert_fusion
  (101 shorter events, 3.8 us)
Async XLA Ops:
  0.6 13.2 %copy-start.5 = (s32[32]{0:T(128)S(1)}, s32[32]{0:T(128)}, u32[]{:S(2)}) copy-start(s32[32]{0:T(128)} %param.13) | copy-start | bytes 388
  0.6 13.4 %copy-start.4 = (s32[32,128]{1,0:T(8,128)S(1)}, s32[32,128]{1,0:T(8,128)}, u32[]{:S(2)}) copy-start(s32[32,128]{1,0:T(8,128)} %param.14) | copy-start | bytes 49156
  6.8 12.9 %collective-permute-start = (f32[8,2688]{1,0:T(8,128)}, f32[8,2688]{1,0:T(8,128)S(1)}, u32[]{:S(2)}, u32[]{:S(2)}) collective-permute-start(f32[8,2688]{1,0:T(8,128)} %get-tuple-element.14), channel_id=1, source_target_pairs={{0,4},{4,8},{8,12},{12,0},{1,5},{5,9},{9,13},{13,1},{2,6},{6,10},{... | collective-permute-start | bytes 258056 | tf_op jit(solution)/shard_map/ppermute | solution.py:22
  9.9 9.8 %collective-permute-start.1 = (f32[8,2688]{1,0:T(8,128)}, f32[8,2688]{1,0:T(8,128)S(1)}, u32[]{:S(2)}, u32[]{:S(2)}) collective-permute-start(f32[8,2688]{1,0:T(8,128)} %get-tuple-element.15), channel_id=1, source_target_pairs={{0,8},{4,12},{8,0},{12,4},{1,9},{5,13},{9,1},{13,5},{2,10},{6,14},... | collective-permute-start | bytes 258056 | tf_op jit(solution)/shard_map/ppermute | solution.py:22
  12.5 7.2 %collective-permute-start.2 = (f32[8,2688]{1,0:T(8,128)}, f32[8,2688]{1,0:T(8,128)S(1)}, u32[]{:S(2)}, u32[]{:S(2)}) collective-permute-start(f32[8,2688]{1,0:T(8,128)} %get-tuple-element.16), channel_id=1, source_target_pairs={{0,12},{4,0},{8,4},{12,8},{1,13},{5,1},{9,5},{13,9},{2,14},{6,2},{... | collective-permute-start | bytes 258056 | tf_op jit(solution)/shard_map/ppermute | solution.py:22
  15.2 0.9 copy-start.2
  19.6 9.2 %copy-start = (bf16[2048,2048]{1,0:T(8,128)(2,1)}, bf16[2048,2048]{1,0:T(8,128)(2,1)S(1)}, u32[]{:S(2)}) copy-start(bf16[2048,2048]{1,0:T(8,128)(2,1)S(1)} %shard_map.132.refs_6_.refs_4_) | copy-start | bytes 25165828
  19.6 7.6 %slice-start.2 = ((s8[5242880]{0:T(1024)(128)(4,1)}), s8[4194304]{0:T(1024)(128)(4,1)S(1)}, s32[]{:S(2)}) async-start(s8[5242880]{0:T(1024)(128)(4,1)} %bitcast.159), calls=%async_computation.2 | async-start | bytes 8388608
  19.7 7.5 %slice-start.3 = ((s8[5242880]{0:T(1024)(128)(4,1)}), s8[1048576]{0:T(1024)(128)(4,1)S(1)}, s32[]{:S(2)}) async-start(s8[5242880]{0:T(1024)(128)(4,1)} %bitcast.159), calls=%async_computation.3 | async-start | bytes 2097152
  19.9 6.9 %collective-permute-start.5 = (bf16[8,2560]{1,0:T(8,128)(2,1)S(1)}, bf16[8,2560]{1,0:T(8,128)(2,1)S(1)}, u32[]{:S(2)}, u32[]{:S(2)}) collective-permute-start(bf16[8,2560]{1,0:T(8,128)(2,1)S(1)} %shard_map.133), channel_id=1, source_target_pairs={{0,4},{4,8},{8,12},{12,0},{1,5},{5,9},{9,13},{13,1},{2,6},{6,10},{... | collective-permute-start | bytes 122888 | tf_op jit(solution)/shard_map/ppermute | solution.py:22
  21.0 5.8 %collective-permute-start.4 = (bf16[8,2560]{1,0:T(8,128)(2,1)S(1)}, bf16[8,2560]{1,0:T(8,128)(2,1)S(1)}, u32[]{:S(2)}, u32[]{:S(2)}) collective-permute-start(bf16[8,2560]{1,0:T(8,128)(2,1)S(1)} %shard_map.133), channel_id=1, source_target_pairs={{0,8},{4,12},{8,0},{12,4},{1,9},{5,13},{9,1},{13,5},{2,10},{6,14},... | collective-permute-start | bytes 122888 | tf_op jit(solution)/shard_map/ppermute | solution.py:22
  22.8 4.0 %collective-permute-start.3 = (bf16[8,2560]{1,0:T(8,128)(2,1)S(1)}, bf16[8,2560]{1,0:T(8,128)(2,1)S(1)}, u32[]{:S(2)}, u32[]{:S(2)}) collective-permute-start(bf16[8,2560]{1,0:T(8,128)(2,1)S(1)} %shard_map.133), channel_id=1, source_target_pairs={{0,12},{4,0},{8,4},{12,8},{1,13},{5,1},{9,5},{13,9},{2,14},{6,2},{... | collective-permute-start | bytes 122888 | tf_op jit(solution)/shard_map/ppermute | solution.py:22
  34.1 5.8 %collective-permute-start.6 = (bf16[8,2176]{1,0:T(8,128)(2,1)S(1)}, bf16[8,2176]{1,0:T(8,128)(2,1)S(1)}, u32[]{:S(2)}, u32[]{:S(2)}) collective-permute-start(bf16[8,2176]{1,0:T(8,128)(2,1)S(1)} %get-tuple-element.31), channel_id=1, source_target_pairs={{0,4},{4,8},{8,12},{12,0},{1,5},{5,9},{9,13},{13,1},{2,6},{6,10},{... | collective-permute-start | bytes 104456 | tf_op jit(solution)/shard_map/ppermute | solution.py:22
  35.7 4.9 %collective-permute-start.7 = (bf16[8,2176]{1,0:T(8,128)(2,1)S(1)}, bf16[8,2176]{1,0:T(8,128)(2,1)S(1)}, u32[]{:S(2)}, u32[]{:S(2)}) collective-permute-start(bf16[8,2176]{1,0:T(8,128)(2,1)S(1)} %get-tuple-element.32), channel_id=1, source_target_pairs={{0,8},{4,12},{8,0},{12,4},{1,9},{5,13},{9,1},{13,5},{2,10},{6,14},... | collective-permute-start | bytes 104456 | tf_op jit(solution)/shard_map/ppermute | solution.py:22
  37.5 3.9 %collective-permute-start.8 = (bf16[8,2176]{1,0:T(8,128)(2,1)S(1)}, bf16[8,2176]{1,0:T(8,128)(2,1)S(1)}, u32[]{:S(2)}, u32[]{:S(2)}) collective-permute-start(bf16[8,2176]{1,0:T(8,128)(2,1)S(1)} %get-tuple-element.33), channel_id=1, source_target_pairs={{0,12},{4,0},{8,4},{12,8},{1,13},{5,1},{9,5},{13,9},{2,14},{6,2},{... | collective-permute-start | bytes 104456 | tf_op jit(solution)/shard_map/ppermute | solution.py:22
  42.6 8.5 %slice-start = ((s8[8388608]{0:T(1024)(128)(4,1)}), s8[4194304]{0:T(1024)(128)(4,1)S(1)}, s32[]{:S(2)}) async-start(s8[8388608]{0:T(1024)(128)(4,1)} %bitcast.157), calls=%async_computation | async-start | bytes 8388608
  42.6 8.4 %slice-start.1 = ((s8[8388608]{0:T(1024)(128)(4,1)}), s8[4194304]{0:T(1024)(128)(4,1)S(1)}, s32[]{:S(2)}) async-start(s8[8388608]{0:T(1024)(128)(4,1)} %bitcast.157), calls=%async_computation.1 | async-start | bytes 8388608
  42.6 8.0 %collective-permute-start.11 = (bf16[8,2048]{1,0:T(8,128)(2,1)S(1)}, bf16[8,2048]{1,0:T(8,128)(2,1)S(1)}, u32[]{:S(2)}, u32[]{:S(2)}) collective-permute-start(bf16[8,2048]{1,0:T(8,128)(2,1)S(1)} %divide_convert_fusion.after_ref.refs_0_), channel_id=1, source_target_pairs={{0,12},{4,0},{8,4},{12,8},{1,13},{5,1},{9,5},{13,9},{2,14},{6,2},{... | collective-permute-start | bytes 98312 | tf_op jit(solution)/shard_map/ppermute | solution.py:22
  45.2 5.4 %collective-permute-start.10 = (bf16[8,2048]{1,0:T(8,128)(2,1)S(1)}, bf16[8,2048]{1,0:T(8,128)(2,1)S(1)}, u32[]{:S(2)}, u32[]{:S(2)}) collective-permute-start(bf16[8,2048]{1,0:T(8,128)(2,1)S(1)} %divide_convert_fusion.after_ref.refs_0_), channel_id=1, source_target_pairs={{0,8},{4,12},{8,0},{12,4},{1,9},{5,13},{9,1},{13,5},{2,10},{6,14},... | collective-permute-start | bytes 98312 | tf_op jit(solution)/shard_map/ppermute | solution.py:22
  45.3 5.7 %collective-permute-start.9 = (bf16[8,2048]{1,0:T(8,128)(2,1)S(1)}, bf16[8,2048]{1,0:T(8,128)(2,1)S(1)}, u32[]{:S(2)}, u32[]{:S(2)}) collective-permute-start(bf16[8,2048]{1,0:T(8,128)(2,1)S(1)} %divide_convert_fusion.after_ref.refs_0_), channel_id=1, source_target_pairs={{0,4},{4,8},{8,12},{12,0},{1,5},{5,9},{9,13},{13,1},{2,6},{6,10},{... | collective-permute-start | bytes 98312 | tf_op jit(solution)/shard_map/ppermute | solution.py:22
  53.1 1.3 %collective-permute-start.12 = (bf16[32,2048]{1,0:T(8,128)(2,1)S(1)}, bf16[32,2048]{1,0:T(8,128)(2,1)S(1)}, u32[]{:S(2)}, u32[]{:S(2)}) collective-permute-start(bf16[32,2048]{1,0:T(8,128)(2,1)S(1)} %get-tuple-element.18.l_ref), channel_id=1, source_target_pairs={{0,1},{1,0},{2,3},{3,2},{4,5},{5,4},{6,7},{7,6},{8,9},{9,8},{10,11... | collective-permute-start | bytes 393224 | tf_op jit(solution)/shard_map/ppermute | solution.py:404
  54.5 5.6 %copy-start.1 = (bf16[32,2048]{1,0:T(8,128)(2,1)S(1)}, bf16[32,2048]{1,0:T(8,128)(2,1)}, u32[]{:S(2)}) copy-start(bf16[32,2048]{1,0:T(8,128)(2,1)} %hid_ref.3) | copy-start | bytes 393220
  54.5 5.6 %copy-start.3 = (bf16[2048]{0:T(1024)(128)(2,1)S(1)}, bf16[2048]{0:T(1024)(128)(2,1)}, u32[]{:S(2)}) copy-start(bf16[2048]{0:T(1024)(128)(2,1)} %gain_ref.3) | copy-start | bytes 12292
  54.5 5.6 %collective-permute-start.13 = (bf16[32,2048]{1,0:T(8,128)(2,1)S(1)}, bf16[32,2048]{1,0:T(8,128)(2,1)S(1)}, u32[]{:S(2)}, u32[]{:S(2)}) collective-permute-start(bf16[32,2048]{1,0:T(8,128)(2,1)S(1)} %shard_map.136.after_ref.near_ref), channel_id=1, source_target_pairs={{0,2},{1,3},{2,0},{3,1},{4,6},{5,7},{6,4},{7,5},{8,10},{9,11},{10,... | collective-permute-start | bytes 393224 | tf_op jit(solution)/shard_map/ppermute | solution.py:404
  67.3 10.4 %collective-permute-start.14 = (bf16[16,3712]{1,0:T(8,128)(2,1)S(1)}, bf16[16,3712]{1,0:T(8,128)(2,1)S(1)}, u32[]{:S(2)}, u32[]{:S(2)}) collective-permute-start(bf16[16,3712]{1,0:T(8,128)(2,1)S(1)} %get-tuple-element.21), channel_id=1, source_target_pairs={{0,4},{4,8},{8,12},{12,0},{1,5},{5,9},{9,13},{13,1},{2,6},{6,10},{... | collective-permute-start | bytes 356360 | tf_op jit(solution)/shard_map/ppermute | solution.py:22
  70.0 9.1 %collective-permute-start.15 = (bf16[16,3712]{1,0:T(8,128)(2,1)S(1)}, bf16[16,3712]{1,0:T(8,128)(2,1)S(1)}, u32[]{:S(2)}, u32[]{:S(2)}) collective-permute-start(bf16[16,3712]{1,0:T(8,128)(2,1)S(1)} %get-tuple-element.22), channel_id=1, source_target_pairs={{0,8},{4,12},{8,0},{12,4},{1,9},{5,13},{9,1},{13,5},{2,10},{6,14},... | collective-permute-start | bytes 356360 | tf_op jit(solution)/shard_map/ppermute | solution.py:22
  71.1 8.1 %collective-permute-start.16 = (bf16[16,3712]{1,0:T(8,128)(2,1)S(1)}, bf16[16,3712]{1,0:T(8,128)(2,1)S(1)}, u32[]{:S(2)}, u32[]{:S(2)}) collective-permute-start(bf16[16,3712]{1,0:T(8,128)(2,1)S(1)} %get-tuple-element.23), channel_id=1, source_target_pairs={{0,12},{4,0},{8,4},{12,8},{1,13},{5,1},{9,5},{13,9},{2,14},{6,2},{... | collective-permute-start | bytes 356360 | tf_op jit(solution)/shard_map/ppermute | solution.py:22
  79.3 6.1 %collective-permute-start.19 = (bf16[8,3584]{1,0:T(8,128)(2,1)S(1)}, bf16[8,3584]{1,0:T(8,128)(2,1)S(1)}, u32[]{:S(2)}, u32[]{:S(2)}) collective-permute-start(bf16[8,3584]{1,0:T(8,128)(2,1)S(1)} %shard_map.140.refs_0_), channel_id=1, source_target_pairs={{0,12},{4,0},{8,4},{12,8},{1,13},{5,1},{9,5},{13,9},{2,14},{6,2},{... | collective-permute-start | bytes 172040 | tf_op jit(solution)/shard_map/ppermute | solution.py:22
  83.2 5.9 %collective-permute-start.18 = (bf16[8,3584]{1,0:T(8,128)(2,1)S(1)}, bf16[8,3584]{1,0:T(8,128)(2,1)S(1)}, u32[]{:S(2)}, u32[]{:S(2)}) collective-permute-start(bf16[8,3584]{1,0:T(8,128)(2,1)S(1)} %shard_map.140.refs_0_), channel_id=1, source_target_pairs={{0,8},{4,12},{8,0},{12,4},{1,9},{5,13},{9,1},{13,5},{2,10},{6,14},... | collective-permute-start | bytes 172040 | tf_op jit(solution)/shard_map/ppermute | solution.py:22
  83.8 6.0 %collective-permute-start.17 = (bf16[8,3584]{1,0:T(8,128)(2,1)S(1)}, bf16[8,3584]{1,0:T(8,128)(2,1)S(1)}, u32[]{:S(2)}, u32[]{:S(2)}) collective-permute-start(bf16[8,3584]{1,0:T(8,128)(2,1)S(1)} %shard_map.140.refs_0_), channel_id=1, source_target_pairs={{0,4},{4,8},{8,12},{12,0},{1,5},{5,9},{9,13},{13,1},{2,6},{6,10},{... | collective-permute-start | bytes 172040 | tf_op jit(solution)/shard_map/ppermute | solution.py:22
  92.4 1.4 %collective-permute-start.20 = (bf16[32,2048]{1,0:T(8,128)(2,1)S(1)}, bf16[32,2048]{1,0:T(8,128)(2,1)S(1)}, u32[]{:S(2)}, u32[]{:S(2)}) collective-permute-start(bf16[32,2048]{1,0:T(8,128)(2,1)S(1)} %shard_map.141.l_ref), channel_id=1, source_target_pairs={{0,1},{1,0},{2,3},{3,2},{4,5},{5,4},{6,7},{7,6},{8,9},{9,8},{10,11... | collective-permute-start | bytes 393224 | tf_op jit(solution)/shard_map/ppermute | solution.py:404
  93.8 5.6 %collective-permute-start.21 = (bf16[32,2048]{1,0:T(8,128)(2,1)S(1)}, bf16[32,2048]{1,0:T(8,128)(2,1)S(1)}, u32[]{:S(2)}, u32[]{:S(2)}) collective-permute-start(bf16[32,2048]{1,0:T(8,128)(2,1)S(1)} %shard_map.142), channel_id=1, source_target_pairs={{0,2},{1,3},{2,0},{3,1},{4,6},{5,7},{6,4},{7,5},{8,10},{9,11},{10,... | collective-permute-start | bytes 393224 | tf_op jit(solution)/shard_map/ppermute | solution.py:404
